TPU v7x, 32 devices: a whole 2x2x4 slice. The times are simulated.
32 devices in a mesh: req: 4 (over x, core), exp: 8 (over z, y).
Axes of the slice: x: 2, y: 2, z: 4, core: 2. Of those that a mesh axis runs over, the one named last changes fastest.
Arguments:
- residual: bfloat16 [1024, 2048], P('exp'), may hold values from -6 to 6
- queries: bfloat16 [1024, 2048], P('exp', 'req'), may hold values from -128 to 128, as said below
- prefix_kv: bfloat16 [4, 2048, 256], P('req', 'exp'), may hold values from -4.5 to 4.5
- suffix_kv: bfloat16 [1024, 4, 256], P('exp', 'req'), may hold values from -6 to 6
- suffix_lengths: int32 [8, 4], P('exp'), may hold values from 1 to 96, 128 in all within a row
- out_proj: bfloat16 [2048, 2048], P('req'), may hold values from -0.5 to 0.5
- norm_gain: bfloat16 [2048], replicated, may hold values from 0.099609375 to 1.8984375
- routes: int32 [1024, 6], P('exp'), may hold values from 0 to 7, all different within a row; in each aligned block of 128 rows (0 to 127, 128 to 255, ...) at most 128 rows name the same one
- route_weights: float32 [1024, 6], P('exp'), may hold values from 0.1 to 0.5
- expert_gate: bfloat16 [8, 2048, 1408], P('exp', None, 'req'), may hold values from -0.125 to 0.125
- expert_up: bfloat16 [8, 2048, 1408], P('exp', None, 'req'), may hold values from -0.125 to 0.125
- expert_down: bfloat16 [8, 1408, 2048], P('exp', 'req'), may hold values from -0.15625 to 0.15625
- shared_gate: bfloat16 [2048, 1408], P(None, 'req'), may hold values from -0.125 to 0.125
- shared_up: bfloat16 [2048, 1408], P(None, 'req'), may hold values from -0.125 to 0.125
- shared_down: bfloat16 [1408, 2048], P('req'), may hold values from -0.15625 to 0.15625
Outputs:
- layer_out: bfloat16 [1024, 2048], P('exp')
Inputs may be any that keep to these rules, and one draw needn't show every extreme that they name: In the hidden draw some queries are strong multiples of prefix keys. `suffix_lengths`: each row (the requests of one index of exp) sums to 128, and in every row one request has exactly 96 tokens. `routes`: the 6 experts of a token are different. Among the 128 tokens of one index of exp no expert is picked more than 128 times, and in every draw some expert is picked exactly 128 times by the tokens of some index of exp.
All inputs are finite; a program needn't handle non-finite values.
Results may differ from a plain program's by a relative error of at most 0.015.
Values may be sent and summed in bfloat16 or wider, within the bound.
No kernel may reach another device: no remote copies, remote signals or barrier semaphores. Data moves between devices by JAX's collectives and lax.ppermute only.
A program may use at most 128 MiB of HBM per device.

v0:
```python
import math

import jax
import jax.numpy as jnp
from jax import lax
from jax.sharding import PartitionSpec as P

HD = 128
TOP = 6


neg_big = -1e30
norm_eps = 1e-06


def on_device(
    residual,
    queries,
    prefix_kv,
    suffix_kv,
    suffix_lengths,
    out_proj,
    norm_gain,
    routes,
    route_weights,
    expert_gate,
    expert_up,
    expert_down,
    shared_gate,
    shared_up,
    shared_down,
):
    tokens_here = residual.shape[0]
    feat_width = residual.shape[1]
    head_count = queries.shape[1] // HD
    scaling = 1.0 / math.sqrt(HD)
    query_heads = jnp.transpose(queries.reshape(tokens_here, head_count, HD), (1, 0, 2))
    start_state = (
        jnp.full((head_count, tokens_here), neg_big, jnp.float32),
        jnp.zeros((head_count, tokens_here), jnp.float32),
        jnp.zeros((head_count, tokens_here, HD), jnp.float32),
    )

    def absorb(carried, key_rows, value_rows, allowed):
        running_max, running_sum, running_acc = carried
        scores = (
            jnp.einsum("htd,kd->htk", query_heads, key_rows, preferred_element_type=jnp.float32)
            * scaling
        )
        if allowed is not None:
            scores = jnp.where(allowed[None], scores, neg_big)
        new_max = jnp.maximum(running_max, jnp.max(scores, axis=-1))
        factor = jnp.exp(running_max - new_max)
        exp_scores = jnp.exp(scores - new_max[..., None])
        new_sum = running_sum * factor + jnp.sum(exp_scores, axis=-1)
        new_acc = running_acc * factor[..., None] + jnp.einsum(
            "htk,kd->htd",
            exp_scores.astype(jnp.bfloat16),
            value_rows,
            preferred_element_type=jnp.float32,
        )
        return (new_max, new_sum, new_acc)

    portion = lax.all_gather(prefix_kv, "exp", axis=1, tiled=True)
    key_count = portion.shape[1]
    window_len = math.gcd(key_count, 2048)

    def inner(position, inner_state):
        window = lax.dynamic_slice_in_dim(portion[0], position * window_len, window_len, 0)
        return absorb(inner_state, window[:, :HD], window[:, HD:], None)

    carried = lax.fori_loop(0, key_count // window_len, inner, start_state)
    request_ends = jnp.cumsum(suffix_lengths[0])
    positions = jnp.arange(tokens_here, dtype=jnp.int32)
    request_ids = jnp.sum((positions[:, None] >= request_ends[None, :]).astype(jnp.int32), axis=1)
    allowed = (request_ids[:, None] == request_ids[None, :]) & (
        positions[None, :] <= positions[:, None]
    )
    carried = absorb(carried, suffix_kv[:, 0, :HD], suffix_kv[:, 0, HD:], allowed)
    running_max, running_sum, running_acc = carried
    attention = (
        jnp.transpose(running_acc / running_sum[..., None], (1, 0, 2))
        .reshape(tokens_here, head_count * HD)
        .astype(jnp.bfloat16)
    )
    attn_terms = jnp.dot(attention, out_proj, preferred_element_type=jnp.float32)
    attn_out = lax.psum(attn_terms.astype(jnp.bfloat16), "req").astype(jnp.float32)
    hidden_state = (residual.astype(jnp.float32) + attn_out).astype(jnp.bfloat16)
    hidden_float = hidden_state.astype(jnp.float32)
    mean_square = jnp.mean(hidden_float * hidden_float, axis=-1, keepdims=True)
    normed = (
        hidden_float * lax.rsqrt(mean_square + norm_eps) * norm_gain.astype(jnp.float32)
    ).astype(jnp.bfloat16)
    shared_gate_act = jnp.dot(normed, shared_gate, preferred_element_type=jnp.float32)
    shared_up_act = jnp.dot(normed, shared_up, preferred_element_type=jnp.float32)
    shared_hidden = (jax.nn.silu(shared_gate_act) * shared_up_act).astype(jnp.bfloat16)
    shared_part = jnp.dot(shared_hidden, shared_down, preferred_element_type=jnp.float32)
    exp_count = lax.axis_size("exp")
    experts = exp_count * expert_gate.shape[0]
    capacity = min(tokens_here, 4 * ((tokens_here * TOP + 2 * experts - 1) // (2 * experts)))
    pick_ids = routes.reshape(-1)
    one_hot = (pick_ids[:, None] == jnp.arange(experts, dtype=jnp.int32)[None, :]).astype(jnp.int32)
    pick_ranks = jnp.sum((jnp.cumsum(one_hot, axis=0) - one_hot) * one_hot, axis=1)
    pick_slots = (pick_ids * capacity + pick_ranks).reshape(tokens_here, TOP)
    slot_ids = jnp.arange(experts * capacity, dtype=jnp.int32)
    placement = jnp.any(pick_slots[None, :, :] == slot_ids[:, None, None], axis=2).astype(
        jnp.bfloat16
    )
    buffer = (
        jnp.dot(placement, normed, preferred_element_type=jnp.float32)
        .astype(jnp.bfloat16)
        .reshape(experts, capacity, feat_width)
    )
    source_rows = lax.all_to_all(buffer, "exp", split_axis=0, concat_axis=0, tiled=True)
    sources, slot_count, row_width = source_rows.shape
    flat_rows = source_rows.reshape(sources * slot_count, row_width)
    gate_act = jnp.dot(flat_rows, expert_gate[0], preferred_element_type=jnp.float32)
    up_act = jnp.dot(flat_rows, expert_up[0], preferred_element_type=jnp.float32)
    expert_hidden = (jax.nn.silu(gate_act) * up_act).astype(jnp.bfloat16)
    partial_out = jnp.dot(expert_hidden, expert_down[0], preferred_element_type=jnp.float32).astype(
        jnp.bfloat16
    )
    finish_partial_out = partial_out.reshape(sources, slot_count, row_width)
    returned = lax.all_to_all(finish_partial_out, "exp", split_axis=0, concat_axis=0, tiled=True)
    flat_back = returned.reshape(experts * capacity, feat_width)
    picked_rows = (
        flat_back[pick_slots.reshape(-1)].astype(jnp.float32).reshape(tokens_here, TOP, feat_width)
    )
    routed = jnp.sum(picked_rows * route_weights[:, :, None], axis=1)
    summed = lax.psum((shared_part + routed).astype(jnp.bfloat16), "req").astype(jnp.float32)
    return (hidden_float + summed).astype(jnp.bfloat16)


def solution(mesh):
    placed = (
        P("exp", None),
        P("exp", "req"),
        P("req", "exp", None),
        P("exp", "req", None),
        P("exp", None),
        P("req", None),
        P(),
        P("exp", None),
        P("exp", None),
        P("exp", None, "req"),
        P("exp", None, "req"),
        P("exp", "req", None),
        P(None, "req"),
        P(None, "req"),
        P("req", None),
    )
    return jax.shard_map(
        on_device, mesh=mesh, in_specs=placed, out_specs=P("exp", None), check_vma=False
    )
```

profile of v0, /device:TPU:0, one launch (start us, length us, event | category | flops | bytes accessed | tf_op | source)
XLA Modules:
  0.0 371.6 jit_solution(7959437539989059676)
XLA Ops:
  8.4 0.8 reduce-window.18
  9.2 1.7 reduce-window.19
  11.8 1.1 fusion.68
  12.9 39.6 %all-gather.2.cloned.1.call-done = bf16[1,2048,256]{2,1,0:T(8,128)(2,1)} async-done(((bf16[1,256,256]{2,1,0:T(8,128)(2,1)}), bf16[1,2048,256]{2,1,0:T(8,128)(2,1)}) %all-gather.2.cloned.1.call-update) | async-done | bytes 1048592 | tf_op jit(solution)/shard_map/all_gather | solution.py:64
  52.5 1.9 multiply_reduce_fusion.1
  55.6 1.0 fusion.24
  56.9 1.3 convolution_convert_fusion.2
  58.8 31.4 %all-reduce.3.cloned.1.call-done = bf16[128,2048]{1,0:T(8,128)(2,1)} async-done(((bf16[128,2048]{1,0:T(8,128)(2,1)}), bf16[128,2048]{1,0:T(8,128)(2,1)}) %all-reduce.3.cloned.1.call-update) | async-done | bytes 524304 | tf_op jit(solution)/shard_map/psum | solution.py:87
  90.2 1.3 fusion.29
  91.5 1.3 fusion.31
  92.8 1.2 convolution_convert_fusion.1
  94.1 97.9 %all_to_all.10 = bf16[8,128,2048]{2,1,0:T(8,128)(2,1)S(1)} all-to-all(bf16[8,128,2048]{2,1,0:T(8,128)(2,1)S(1)} %bitcast.119), channel_id=1, replica_groups=mesh['req'=4,'exp'=8] {'exp'}, dimensions={0} | all-to-all | bytes 8388608 | tf_op jit(solution)/shard_map/all_to_all | solution.py:114
  192.0 2.0 copy-done.2
  194.0 2.9 fusion.10
  196.9 9.4 %convolution_convert_fusion = bf16[1024,2048]{1,0:T(8,128)(2,1)} fusion(bf16[1,352,2048]{2,1,0:T(8,128)(2,1)} %param.26, bf16[1024,2048]{1,0:T(8,128)(2,1)} %bitcast.122, bf16[1,2048,352]{1,2,0:T(8,128)(2,1)} %param.25, f32[1024,352]{0,1:T(8,128)} %fusion.10), kind=kOutput, calls=%fused_computation.4 | convolution fusion | flops 2957049856 | bytes 12713984 | tf_op jit(solution)/shard_map/dot_general | solution.py:120
  206.2 4.9 %all-to-all-start.1 = ((bf16[8,128,2048]{2,1,0:T(8,128)(2,1)}), bf16[8,128,2048]{2,1,0:T(8,128)(2,1)}, u32[]{:S(2)}, u32[]{:S(2)}) async-start(bf16[8,128,2048]{2,1,0:T(8,128)(2,1)} %bitcast.120), calls=%async_computation.1 | async-start | bytes 8388608 | tf_op jit(solution)/shard_map/all_to_all | solution.py:124
  211.4 1.9 fusion.69
  213.4 89.7 %all-to-all-done.1 = bf16[8,128,2048]{2,1,0:T(8,128)(2,1)} async-done(((bf16[8,128,2048]{2,1,0:T(8,128)(2,1)}), bf16[8,128,2048]{2,1,0:T(8,128)(2,1)}, u32[]{:S(2)}, u32[]{:S(2)}) %all-to-all-start.1) | async-done | bytes 4194336 | tf_op jit(solution)/shard_map/all_to_all | solution.py:124
  303.0 9.8 %gather_fusion = bf16[768,2048]{1,0:T(8,128)(2,1)} fusion(bf16[1024,2048]{1,0:T(8,128)(2,1)} %bitcast.26, s32[1024]{0:T(1024)S(1)} %pad_clamp_fusion), kind=kCustom, calls=%fused_computation | custom fusion | bytes 6294528 | tf_op jit(solution)/shard_map/gather | solution.py:127
  312.8 6.6 %reshape.185 = f32[128,6,2048]{2,1,0:T(8,128)} reshape(bf16[768,2048]{1,0:T(8,128)(2,1)} %gather_fusion) | data formatting | bytes 9437184 | tf_op jit(solution)/shard_map/convert_element_type | solution.py:127
  319.4 7.6 %multiply_reduce_fusion = f32[128,2048]{1,0:T(8,128)} fusion(f32[128,6,2048]{2,1,0:T(8,128)} %reshape.185, f32[128,6]{1,0:T(8,128)S(1)} %copy.44), kind=kLoop, calls=%fused_computation.1 | loop fusion | flops 2883584 | bytes 7343104 | tf_op jit(solution)/shard_map/reduce_sum | solution.py:129
  327.0 4.4 %fusion.3 = bf16[128,2048]{1,0:T(8,128)(2,1)} fusion(f32[128,2048]{1,0:T(8,128)} %multiply_reduce_fusion, bf16[352,2048]{1,0:T(8,128)(2,1)} %param.29, bf16[128,2048]{1,0:T(8,128)(2,1)S(1)} %fusion.31, bf16[2048,352]{0,1:T(8,128)(2,1)} %param.28, f32[128,352]{0,1:T(8,128)S(1)} %fusion.69), kind=kOutput, calls=%fused_computation.11 | convolution fusion | flops 369893376 | bytes 5160960 | tf_op jit(solution)/shard_map/dot_general | solution.py:97
  331.4 31.5 %all-reduce.5.cloned.1.call-done = bf16[128,2048]{1,0:T(8,128)(2,1)} async-done(((bf16[128,2048]{1,0:T(8,128)(2,1)}), bf16[128,2048]{1,0:T(8,128)(2,1)}) %all-reduce.5.cloned.1.call-update) | async-done | bytes 524304 | tf_op jit(solution)/shard_map/psum | solution.py:130
  362.9 2.2 fusion.32
  (47 shorter events, 5.1 us)
Async XLA Ops:
  6.5 50.3 %copy-start = (bf16[512,2048]{1,0:T(8,128)(2,1)S(1)}, bf16[512,2048]{1,0:T(8,128)(2,1)}, u32[]{:S(2)}) copy-start(bf16[512,2048]{1,0:T(8,128)(2,1)} %param.20) | copy-start | bytes 6291460
  6.5 45.9 %all-gather.2.cloned.1.call-start = ((), (), s32[]{:S(2)}) async-start(), calls=%async_computation.2 | async-start | bytes 1179648 | tf_op jit(solution)/shard_map/all_gather | solution.py:64
  7.3 83.0 %all-reduce.3.cloned.1.call-start = ((), (), s32[]{:S(2)}) async-start(), calls=%async_computation.3 | async-start | bytes 1048576 | tf_op jit(solution)/shard_map/psum | solution.py:87
  54.4 1.2 copy-start.3
  55.6 1.0 copy-start.7
  56.6 1.6 copy-start.4
  56.9 33.4 %copy-start.1 = (bf16[128,2048]{1,0:T(8,128)(2,1)S(1)}, bf16[128,2048]{1,0:T(8,128)(2,1)}, u32[]{:S(2)}) copy-start(bf16[128,2048]{1,0:T(8,128)(2,1)} %param.15) | copy-start | bytes 1572868
  94.1 99.9 %copy-start.6 = (bf16[1,2048,352]{1,2,0:T(8,128)(2,1)S(1)}, bf16[1,2048,352]{1,2,0:T(8,128)(2,1)}, u32[]{:S(2)}) copy-start(bf16[1,2048,352]{1,2,0:T(8,128)(2,1)} %param.24) | copy-start | bytes 4325380
  192.0 2.0 copy-start.2
  206.2 5.1 %copy-start.5 = (f32[128,6]{0,1:T(8,128)S(1)}, f32[128,6]{0,1:T(8,128)}, u32[]{:S(2)}) copy-start(f32[128,6]{0,1:T(8,128)} %param.23) | copy-start | bytes 9220
  206.2 96.8 %all-to-all-start.1 = ((bf16[8,128,2048]{2,1,0:T(8,128)(2,1)}), bf16[8,128,2048]{2,1,0:T(8,128)(2,1)}, u32[]{:S(2)}, u32[]{:S(2)}) async-start(bf16[8,128,2048]{2,1,0:T(8,128)(2,1)} %bitcast.120), calls=%async_computation.1 | async-start | bytes 8388608 | tf_op jit(solution)/shard_map/all_to_all | solution.py:124
  211.1 151.8 %all-reduce.5.cloned.1.call-start = ((), (), s32[]{:S(2)}) async-start(), calls=%async_computation.4 | async-start | bytes 1048576 | tf_op jit(solution)/shard_map/psum | solution.py:130
Sparse Core Ops, SparseCore 0:
  9.5 42.9 all-gather.1
  58.3 31.8 all-reduce.2
  331.5 31.2 all-reduce.4
where the time goes:
time: 372 us
  waiting for transfers between devices  193 us (52%)
  blocking collectives  97.9 us (26%)
  matrix products  25.3 us (7%)
  local copies, waits for them, and re-layouts  20.5 us (6%)
  other arithmetic  16.8 us (5%)
  between operations  13.3 us (4%)
  starting transfers between devices  4.94 us (1%)
    all_to_all x1, blocking collectives, on_device(): lax.all_to_all(buffer, 'exp', split_axis=0, concat_axis=0, tiled=True)  97.9 us
    all_to_all x1, waiting for transfers between devices, on_device(): lax.all_to_all(finish_partial_out, 'exp', split_axis=0, concat_axis=0, ti...  89.7 us
    all_gather x1, waiting for transfers between devices, on_device(): portion = lax.all_gather(prefix_kv, 'exp', axis=1, tiled=True)  39.6 us
    psum x1, waiting for transfers between devices, on_device(): lax.psum((shared_part + routed).astype(jnp.bfloat16), 'req')  31.5 us
    psum x1, waiting for transfers between devices, on_device(): lax.psum(attn_terms.astype(jnp.bfloat16), 'req').astype(jnp.float32)  31.4 us
    gather x1, local copies, waits for them, and re-layouts, on_device(): flat_back[pick_slots.reshape(-1)].astype(jnp.float32)  9.82 us
    dot_general x1, matrix products, on_device(): jnp.dot(expert_hidden, expert_down[0], preferred_element_type=jnp.float32)  9.36 us
    reduce_sum x1, other arithmetic, on_device(): routed = jnp.sum(picked_rows * route_weights[:, :, None], axis=1)  7.62 us
  transfers between devices with their start and end apart: 4, of which 4 were waited for; matrix products, arithmetic and copies ran while one was open for 2% of the time, Pallas kernels for 0%

commit v1 on v0

--- a/solution.py
+++ b/solution.py
@@ -1,16 +1,287 @@
+import functools
 import math
 
 import jax
 import jax.numpy as jnp
 from jax import lax
+from jax.experimental import pallas as pl
+from jax.experimental.pallas import tpu as pltpu
 from jax.sharding import PartitionSpec as P
 
 HD = 128
 TOP = 6
 
-
 neg_big = -1e30
 norm_eps = 1e-06
+f32 = jnp.float32
+bf16 = jnp.bfloat16
+
+
+def dot(a, b):
+    return jnp.dot(a, b, preferred_element_type=f32)
+
+
+def expert_capacity(tokens_here, experts):
+    return min(tokens_here, 4 * ((tokens_here * TOP + 2 * experts - 1) // (2 * experts)))
+
+
+def attend_kernel(heads, tokens, page_len, page_count, first, last, *refs):
+    refs = list(refs)
+    q_ref = refs.pop(0)
+    if first:
+        lengths_ref, suffix_ref = refs.pop(0), refs.pop(0)
+    else:
+        max_in, sum_in, acc_in = refs.pop(0), refs.pop(0), refs.pop(0)
+    if last:
+        core_ref = refs.pop(0)
+    page_refs = [refs.pop(0) for _ in range(page_count)]
+    scaling = 1.0 / math.sqrt(HD)
+    q = jnp.concatenate([q_ref[:, h * HD : (h + 1) * HD] for h in range(heads)], axis=0)
+    blocks = [(ref[:page_len, :HD], ref[:page_len, HD:]) for ref in page_refs]
+    scores = [
+        lax.dot_general(q, k, (((1,), (1,)), ((), ())), preferred_element_type=f32) * scaling
+        for k, _ in blocks
+    ]
+    if first:
+        ends, total = [], 0
+        for i in range(lengths_ref.shape[1]):
+            total = total + lengths_ref[0, i]
+            ends.append(total)
+        rows = lax.broadcasted_iota(jnp.int32, (tokens, tokens), 0)
+        cols = lax.broadcasted_iota(jnp.int32, (tokens, tokens), 1)
+        row_ids = sum((rows >= e).astype(jnp.int32) for e in ends)
+        col_ids = sum((cols >= e).astype(jnp.int32) for e in ends)
+        bias = jnp.where((row_ids == col_ids) & (cols <= rows), 0.0, neg_big).astype(f32)
+        k, v = suffix_ref[:, :HD], suffix_ref[:, HD:]
+        own = lax.dot_general(q, k, (((1,), (1,)), ((), ())), preferred_element_type=f32) * scaling
+        own = jnp.where(jnp.concatenate([bias] * heads, axis=0) < 0.0, neg_big, own)
+        scores.append(own)
+        blocks.append((k, v))
+    new_max = functools.reduce(
+        jnp.maximum, [jnp.max(s, axis=-1, keepdims=True) for s in scores]
+    )
+    if not first:
+        old_max = max_in[:, :1]
+        new_max = jnp.maximum(new_max, old_max)
+        factor = jnp.exp(old_max - new_max)
+        total = sum_in[:, :1] * factor
+        acc = acc_in[...] * factor
+    else:
+        total, acc = 0.0, 0.0
+    for s, (_, v) in zip(scores, blocks):
+        e = jnp.exp(s - new_max)
+        total = total + jnp.sum(e, axis=-1, keepdims=True)
+        acc = acc + jnp.dot(e.astype(bf16), v, preferred_element_type=f32)
+    if last:
+        keep_ref, send_ref = refs
+        half = tokens // 2
+        out = (acc / total).astype(bf16)
+        second = core_ref[0] == 1
+        for h in range(heads):
+            low = out[h * tokens : h * tokens + half]
+            high = out[h * tokens + half : (h + 1) * tokens]
+            keep_ref[:, h * HD : (h + 1) * HD] = jnp.where(second, high, low)
+            send_ref[:, h * HD : (h + 1) * HD] = jnp.where(second, low, high)
+    else:
+        max_out, sum_out, acc_out = refs
+        max_out[...] = jnp.broadcast_to(new_max, max_out.shape)
+        sum_out[...] = jnp.broadcast_to(total, sum_out.shape)
+        acc_out[...] = acc
+
+
+def attend(queries, pages, page_len, state=None, suffix=None, core=None):
+    tokens, width = queries.shape
+    heads = width // HD
+    first, last = state is None, core is not None
+    vmem, smem = pl.BlockSpec(memory_space=pltpu.VMEM), pl.BlockSpec(memory_space=pltpu.SMEM)
+    args, specs = [queries], [vmem]
+    if first:
+        args += list(suffix)
+        specs += [smem, vmem]
+    else:
+        args += list(state)
+        specs += [vmem] * 3
+    if last:
+        args.append(core)
+        specs.append(smem)
+    args += pages
+    specs += [vmem] * len(pages)
+    if last:
+        outs = [jax.ShapeDtypeStruct((tokens // 2, width), bf16)] * 2
+    else:
+        outs = [jax.ShapeDtypeStruct((heads * tokens, HD), f32)] * 3
+    keys = sum(page_len for _ in pages) + (tokens if first else 0)
+    return pl.pallas_call(
+        functools.partial(attend_kernel, heads, tokens, page_len, len(pages), first, last),
+        out_shape=outs,
+        in_specs=specs,
+        out_specs=[vmem] * len(outs),
+        compiler_params=pltpu.CompilerParams(vmem_limit_bytes=32 << 20),
+        cost_estimate=pl.CostEstimate(
+            flops=4 * heads * tokens * keys * HD,
+            bytes_accessed=4 * keys * HD + 2 * tokens * width,
+            transcendentals=heads * tokens * keys,
+        ),
+    )(*args)
+
+
+def on_device_ring(
+    residual,
+    queries,
+    prefix_kv,
+    suffix_kv,
+    suffix_lengths,
+    out_proj,
+    norm_gain,
+    routes,
+    route_weights,
+    expert_gate,
+    expert_up,
+    expert_down,
+    shared_gate,
+    shared_up,
+    shared_down,
+):
+    tokens, width = residual.shape
+    half = tokens // 2
+    n = lax.axis_size("exp")
+    steps = n // 2
+    order = list(range(0, n, 2)) + list(range(n - 1, 0, -2))
+    right = [(order[k], order[(k + 1) % n]) for k in range(n)]
+    left = [(b, a) for a, b in right]
+    req = lax.axis_size("req")
+    sibling = [(i, i ^ 1) for i in range(req)]
+    across = [(i, i ^ 2) for i in range(req)]
+    core = lax.rem(lax.axis_index("req"), 2)
+    me = lax.axis_index("exp")
+
+    def half_of(x):
+        return lax.dynamic_slice_in_dim(x, core * half, half, 0)
+
+    slots = jnp.arange(n, dtype=jnp.int32)
+    dense = jnp.sum(
+        jnp.where(routes.T[None] == slots[:, None, None], route_weights.T[None], 0.0), axis=1
+    )
+    head = lax.reduce_precision(dense, 8, 7)
+    rest = lax.reduce_precision(dense - head, 8, 7)
+    gates = jnp.concatenate([head, rest], axis=1).astype(bf16)
+    page_len = prefix_kv.shape[1]
+    pad = -n % 16
+    page = jnp.concatenate([prefix_kv[0], gates, jnp.zeros((pad, gates.shape[1]), bf16)], axis=0)
+
+    out_proj_sib = lax.ppermute(out_proj, "req", sibling)
+    shared_gate_sib = lax.ppermute(shared_gate, "req", sibling)
+    shared_up_sib = lax.ppermute(shared_up, "req", sibling)
+    shared_down_sib = lax.ppermute(shared_down, "req", sibling)
+    gate_sib = lax.ppermute(expert_gate[0], "req", sibling)
+    up_sib = lax.ppermute(expert_up[0], "req", sibling)
+    down_sib = lax.ppermute(expert_down[0], "req", sibling)
+
+    suffix = (suffix_lengths, suffix_kv[:, 0])
+    core_arr = jnp.reshape(core, (1,)).astype(jnp.int32)
+    gate_rows = {0: gates}
+    from_left, from_right = page, page
+    state = None
+    arrived = [page]
+    cut = (page_len // 2)
+    for s in range(1, steps + 1):
+        if s < steps:
+            from_left = lax.ppermute(from_left, "exp", right)
+            from_right = lax.ppermute(from_right, "exp", left)
+            now = [from_left, from_right]
+            gate_rows[s] = from_left[page_len : page_len + n]
+            gate_rows[-s] = from_right[page_len : page_len + n]
+        else:
+            low = lax.ppermute(from_left[:cut], "exp", right)
+            high = lax.ppermute(from_right[cut:], "exp", left)
+            gate_rows[s] = high[page_len - cut : page_len - cut + n]
+            now = [low, high[: page_len - cut]]
+        if s == 1:
+            arrived += now
+            state = attend(queries, arrived, page_len, suffix=suffix)
+        elif s < steps:
+            state = attend(queries, now, page_len, state=state)
+        else:
+            keep, send = attend(queries, now, cut, state=state, core=core_arr)
+
+    other = lax.ppermute(send, "req", sibling)
+    terms = (dot(keep, out_proj) + dot(other, out_proj_sib)).astype(bf16)
+    terms_across = lax.ppermute(terms, "req", across)
+    hidden_state = (
+        half_of(residual).astype(f32) + (terms.astype(f32) + terms_across.astype(f32))
+    ).astype(bf16)
+    hidden_float = hidden_state.astype(f32)
+    mean_square = jnp.mean(hidden_float * hidden_float, axis=-1, keepdims=True)
+    normed = (
+        hidden_float * lax.rsqrt(mean_square + norm_eps) * norm_gain.astype(f32)
+    ).astype(bf16)
+
+    def glu(rows, weights, scale):
+        total = 0.0
+        for gate, up, down in weights:
+            hidden = (jax.nn.silu(dot(rows, gate)) * dot(rows, up)).astype(bf16)
+            total = total + dot(hidden, down)
+        return total if scale is None else total * scale
+
+    shared_weights = [
+        (shared_gate, shared_up, shared_down),
+        (shared_gate_sib, shared_up_sib, shared_down_sib),
+    ]
+    expert_weights = [
+        (expert_gate[0], expert_up[0], expert_down[0]),
+        (gate_sib, up_sib, down_sib),
+    ]
+    shared_part = glu(normed, shared_weights, None)
+
+    def scale_of(distance):
+        row = lax.dynamic_slice_in_dim(gate_rows[distance], me, 1, 0)[0].astype(f32)
+        return half_of(row[:tokens] + row[tokens:])
+
+    def experts(blocks):
+        rows = jnp.concatenate([b for _, b in blocks], axis=0)
+        scale = jnp.concatenate([scale_of(d) for d, _ in blocks])[:, None]
+        out = glu(rows, expert_weights, scale).astype(bf16)
+        return {d: out[i * half : (i + 1) * half] for i, (d, _) in enumerate(blocks)}
+
+    parts = {}
+    from_left, from_right = normed, normed
+    quarter = half // 2
+    for s in range(1, steps + 1):
+        if s < steps:
+            from_left = lax.ppermute(from_left, "exp", right)
+            from_right = lax.ppermute(from_right, "exp", left)
+            now = [(s, from_left), (-s, from_right)]
+            if s == 1:
+                now = [(0, normed)] + now
+        else:
+            low = lax.ppermute(from_left[:quarter], "exp", right)
+            high = lax.ppermute(from_right[quarter:], "exp", left)
+            now = [(s, jnp.concatenate([low, high], axis=0))]
+        parts.update(experts(now))
+
+    def add(a, b):
+        return (a.astype(f32) + b.astype(f32)).astype(bf16)
+
+    to_right = lax.ppermute(parts[steps][:quarter], "exp", right)
+    to_left = lax.ppermute(parts[steps][quarter:], "exp", left)
+    for k in range(steps - 1, 0, -1):
+        a, b = parts[-k], parts[k]
+        if k == steps - 1:
+            a = jnp.concatenate([add(a[:quarter], to_right), a[quarter:]], axis=0)
+            b = jnp.concatenate([b[:quarter], add(b[quarter:], to_left)], axis=0)
+        else:
+            a, b = add(a, to_right), add(b, to_left)
+        to_right = lax.ppermute(a, "exp", right)
+        to_left = lax.ppermute(b, "exp", left)
+    routed = parts[0].astype(f32) + (to_right.astype(f32) + to_left.astype(f32))
+    summed = (shared_part + routed).astype(bf16)
+    summed_across = lax.ppermute(summed, "req", across)
+    mine = (hidden_float + (summed.astype(f32) + summed_across.astype(f32))).astype(bf16)
+    theirs = lax.ppermute(mine, "req", sibling)
+    first = core == 0
+    return jnp.concatenate(
+        [jnp.where(first, mine, theirs), jnp.where(first, theirs, mine)], axis=0
+    )
 
 
 def on_device(
@@ -97,7 +368,7 @@
     shared_part = jnp.dot(shared_hidden, shared_down, preferred_element_type=jnp.float32)
     exp_count = lax.axis_size("exp")
     experts = exp_count * expert_gate.shape[0]
-    capacity = min(tokens_here, 4 * ((tokens_here * TOP + 2 * experts - 1) // (2 * experts)))
+    capacity = expert_capacity(tokens_here, experts)
     pick_ids = routes.reshape(-1)
     one_hot = (pick_ids[:, None] == jnp.arange(experts, dtype=jnp.int32)[None, :]).astype(jnp.int32)
     pick_ranks = jnp.sum((jnp.cumsum(one_hot, axis=0) - one_hot) * one_hot, axis=1)
@@ -149,6 +420,19 @@
         P(None, "req"),
         P("req", None),
     )
-    return jax.shard_map(
-        on_device, mesh=mesh, in_specs=placed, out_specs=P("exp", None), check_vma=False
-    )
+
+    def program(residual, *rest):
+        n_exp, n_req = mesh.shape["exp"], mesh.shape["req"]
+        tokens_here = residual.shape[0] // n_exp
+        experts = rest[8].shape[0]
+        every_row = expert_capacity(tokens_here, experts) == tokens_here
+        ring = every_row and experts == n_exp and n_req == 4 and n_exp % 2 == 0 and n_exp >= 4
+        return jax.shard_map(
+            on_device_ring if ring else on_device,
+            mesh=mesh,
+            in_specs=placed,
+            out_specs=P("exp", None),
+            check_vma=False,
+        )(residual, *rest)
+
+    return program

time: 372 us -> 155 us (0.42)
  waiting for transfers between devices: 193 us -> 45.4 us
  blocking collectives: 97.9 us -> 0 us
  matrix products: 25.3 us -> 53.2 us
  starting transfers between devices: 4.94 us -> 29.5 us
  between operations: 13.3 us -> 0.43 us
  other arithmetic: 16.8 us -> 7.58 us
  local copies, waits for them, and re-layouts: 20.5 us -> 11.6 us
  Pallas kernels: 0 us -> 6.23 us
    all_to_all x1 -> x0, blocking collectives: 97.9 us -> none  [on_device(): lax.all_to_all(buffer, 'exp', split_axis=0, concat_axis=0, tiled=True)]
    all_to_all x1 -> x0, waiting for transfers between devices: 89.7 us -> none  [on_device(): lax.all_to_all(finish_partial_out, 'exp', split_axis=0, concat_axis=0, ti...]
    psum x2 -> x0, waiting for transfers between devices: 62.9 us -> none  [the longest x1 31.5 us: on_device(): lax.psum((shared_part + routed).astype(jnp.bfloat16), 'req')]
    ppermute x0 -> x35, waiting for transfers between devices: none -> 45.4 us  [the longest x6 12 us: on_device_ring(): from_right = lax.ppermute(from_right, 'exp', left)]
    all_gather x1 -> x0, waiting for transfers between devices: 39.6 us -> none  [on_device(): portion = lax.all_gather(prefix_kv, 'exp', axis=1, tiled=True)]
    ppermute x0 -> x35, starting transfers between devices: none -> 29.5 us  [the longest x6 10.9 us: on_device_ring(): from_left = lax.ppermute(from_left, 'exp', right)]
    dot_general x10 -> x22, matrix products: 25.3 us -> 53.2 us  [dot(): return jnp.dot(a, b, preferred_element_type=f32)]
    gather x1 -> x0, local copies, waits for them, and re-layouts: 9.82 us -> none  [on_device(): flat_back[pick_slots.reshape(-1)].astype(jnp.float32)]
  transfers between devices with their start and end apart: 4 -> 35, of which waited for: 4 -> 22; matrix products, arithmetic and copies ran while one was open for 2% -> 40% of each run, Pallas kernels for 0% -> 4%
where the time goes in v1:
time: 155 us; the launch traced here: 154 us
  matrix products  53.2 us (34%)
  waiting for transfers between devices  45.4 us (29%)
  starting transfers between devices  29.5 us (19%)
  local copies, waits for them, and re-layouts  11.6 us (7%)
  other arithmetic  7.58 us (5%)
  Pallas kernels  6.23 us (4%)
    dot_general x22, matrix products, dot(): return jnp.dot(a, b, preferred_element_type=f32)  53.2 us
    ppermute x6, waiting for transfers between devices, on_device_ring(): from_right = lax.ppermute(from_right, 'exp', left)  12 us
    ppermute x6, starting transfers between devices, on_device_ring(): from_left = lax.ppermute(from_left, 'exp', right)  10.9 us
    ppermute x3, waiting for transfers between devices, on_device_ring(): to_right = lax.ppermute(a, 'exp', right)  7.82 us
    unnamed x43, local copies, waits for them, and re-layouts  7.45 us
    ppermute x1, waiting for transfers between devices, on_device_ring(): terms_across = lax.ppermute(terms, 'req', across)  6.78 us
    pallas_call x4, Pallas kernels, attend(): pl.pallas_call(functools.partial(attend_kernel, heads, tokens, page_len,...  6.23 us
    ppermute x1, waiting for transfers between devices, on_device_ring(): summed_across = lax.ppermute(summed, 'req', across)  4.89 us
  transfers between devices with their start and end apart: 35, of which 22 were waited for; matrix products, arithmetic and copies ran while one was open for 40% of the time, Pallas kernels for 4%

profile of v1, /device:TPU:0, one launch (start us, length us, event | category | flops | bytes accessed | tf_op | source)
XLA Modules:
  0.0 154.0 jit_solution(7563338840326055100)
XLA Ops:
  1.8 3.1 %collective-permute-start = (bf16[272,256]{1,0:T(8,128)(2,1)S(1)}, bf16[272,256]{1,0:T(8,128)(2,1)S(1)}, u32[]{:S(2)}, u32[]{:S(2)}) collective-permute-start(bf16[272,256]{1,0:T(8,128)(2,1)S(1)} %maximum_maximum_fusion.refs_3_), channel_id=1, source_target_pairs={{0,2},{2,4},{4,6},{6,7},{7,5},{5,3},{3,1},{1,0},{8,10},{10,12},{12... | collective-permute-start | bytes 417800 | tf_op jit(solution)/shard_map/ppermute | solution.py:189
  6.1 2.4 %collective-permute-done.refs_4_ = bf16[272,256]{1,0:T(8,128)(2,1)S(1)} collective-permute-done((bf16[272,256]{1,0:T(8,128)(2,1)S(1)}, bf16[272,256]{1,0:T(8,128)(2,1)S(1)}, u32[]{:S(2)}, u32[]{:S(2)}) %collective-permute-start) | collective-permute-done | bytes 139296 | tf_op jit(solution)/shard_map/ppermute | solution.py:189
  28.4 1.9 %collective-permute-done.8 = bf16[64,512]{1,0:T(8,128)(2,1)S(1)} collective-permute-done((bf16[64,512]{1,0:T(8,128)(2,1)S(1)}, bf16[64,512]{1,0:T(8,128)(2,1)S(1)}, u32[]{:S(2)}, u32[]{:S(2)}) %collective-permute-start.8) | collective-permute-done | bytes 65568 | tf_op jit(solution)/shard_map/ppermute | solution.py:207
  32.9 6.8 %collective-permute-done.10 = bf16[64,2048]{1,0:T(8,128)(2,1)S(1)} collective-permute-done((bf16[64,2048]{1,0:T(8,128)(2,1)S(1)}, bf16[64,2048]{1,0:T(8,128)(2,1)S(1)}, u32[]{:S(2)}, u32[]{:S(2)}) %collective-permute-start.10) | collective-permute-done | bytes 262176 | tf_op jit(solution)/shard_map/ppermute | solution.py:209
  42.8 3.9 %fusion.12 = f32[64,2048]{1,0:T(8,128)} fusion(bf16[352,2048]{1,0:T(8,128)(2,1)} %param.29, bf16[64,2048]{1,0:T(8,128)(2,1)S(1)} %fusion.15, bf16[2048,352]{0,1:T(8,128)(2,1)} %param.28, f32[64,352]{1,0:T(8,128)S(1)} %fusion.114), kind=kOutput, calls=%fused_computation.19 | convolution fusion | flops 184684544 | bytes 3760128 | tf_op jit(solution)/shard_map/dot_general | solution.py:21
  50.6 2.4 %fusion.89 = f32[192,352]{1,0:T(8,128)} fusion(bf16[1,2048,352]{1,2,0:T(8,128)(2,1)S(1)} %copy-done.3, bf16[64,2048]{1,0:T(8,128)(2,1)} %collective-permute-done.15, bf16[64,2048]{1,0:T(8,128)(2,1)} %copy-done.19, bf16[64,2048]{1,0:T(8,128)(2,1)S(1)} %fusion.15), kind=kOutput, calls=%fused_computation.145 | convolution fusion | flops 279183360 | bytes 2498560 | tf_op jit(solution)/shard_map/dot_general | solution.py:21
  53.0 4.6 %fusion.17 = f32[192,2048]{1,0:T(8,128)} fusion(f32[192,352]{1,0:T(8,128)} %fusion.89, bf16[1,352,2048]{2,1,0:T(8,128)(2,1)} %param.26, bf16[1,2048,352]{1,2,0:T(8,128)(2,1)} %param.25, bf16[64,2048]{1,0:T(8,128)(2,1)} %collective-permute-done.15, bf16[64,2048]{1,0:T(8,128)(2,1)} %copy-done.19, bf16[64,2048]{1,0:T(8,128)(2,1)S(1)} %fusion.15), kind=kOutput, calls=%fused_computation.46 | convolution fusion | flops 556412928 | bytes 5513216 | tf_op jit(solution)/shard_map/dot_general | solution.py:21
  58.1 2.9 %fusion.101 = f32[192,352]{1,0:T(8,128)} fusion(bf16[2048,352]{0,1:T(8,128)(2,1)} %collective-permute-done.17, bf16[64,2048]{1,0:T(8,128)(2,1)} %collective-permute-done.15, bf16[64,2048]{1,0:T(8,128)(2,1)} %copy-done.19, bf16[64,2048]{1,0:T(8,128)(2,1)S(1)} %fusion.15), kind=kOutput, calls=%fused_computation.157 | convolution fusion | flops 279183360 | bytes 2498560 | tf_op jit(solution)/shard_map/dot_general | solution.py:21
  62.7 2.9 %collective-permute-done.20 = bf16[64,2048]{1,0:T(8,128)(2,1)S(1)} collective-permute-done((bf16[64,2048]{1,0:T(8,128)(2,1)}, bf16[64,2048]{1,0:T(8,128)(2,1)S(1)}, u32[]{:S(2)}, u32[]{:S(2)}) %collective-permute-start.20) | collective-permute-done | bytes 262176 | tf_op jit(solution)/shard_map/ppermute | solution.py:252
  68.4 4.4 %fusion.25 = f32[128,2048]{1,0:T(8,128)} fusion(f32[128,352]{0,1:T(8,128)} %fusion.87, bf16[1,352,2048]{2,1,0:T(8,128)(2,1)} %param.26, bf16[128,2048]{1,0:T(8,128)(2,1)S(1)} %constant_dynamic-update-slice_fusion, bf16[1,2048,352]{1,2,0:T(8,128)(2,1)} %param.25), kind=kOutput, calls=%fused_computation.58 | convolution fusion | flops 369369088 | bytes 4636672 | tf_op jit(solution)/shard_map/dot_general | solution.py:21
  75.4 4.9 %collective-permute-done.22 = bf16[64,2048]{1,0:T(8,128)(2,1)S(1)} collective-permute-done((bf16[64,2048]{1,0:T(8,128)(2,1)}, bf16[64,2048]{1,0:T(8,128)(2,1)S(1)}, u32[]{:S(2)}, u32[]{:S(2)}) %collective-permute-start.22) | collective-permute-done | bytes 262176 | tf_op jit(solution)/shard_map/ppermute | solution.py:252
  85.3 4.5 %fusion.26 = f32[128,2048]{1,0:T(8,128)} fusion(f32[128,352]{0,1:T(8,128)} %fusion.85, bf16[1,352,2048]{2,1,0:T(8,128)(2,1)} %param.26, bf16[128,2048]{1,0:T(8,128)(2,1)} %copy-done.4, bf16[1,2048,352]{1,2,0:T(8,128)(2,1)} %param.25), kind=kOutput, calls=%fused_computation.59 | convolution fusion | flops 369369088 | bytes 4636672 | tf_op jit(solution)/shard_map/dot_general | solution.py:21
  90.8 4.6 %fusion.5 = bf16[128,2048]{1,0:T(8,128)(2,1)} fusion(f32[128,2048]{1,0:T(8,128)} %fusion.26, bf16[352,2048]{1,0:T(8,128)(2,1)} %collective-permute-done.18, f32[128]{0:T(128)S(1)} %pad_maximum_fusion.6, f32[128,352]{0,1:T(8,128)} %fusion.117, bf16[128,2048]{1,0:T(8,128)(2,1)} %copy-done.4, bf16[2048,352]{0,1:T(8,128)(2,1)} %collective-permute-done.17), kind=kOutput, calls=%fused_computation.8 | convolution fusion | flops 370155520 | bytes 5161472 | tf_op jit(solution)/shard_map/dot_general | solution.py:21
  98.5 3.1 %fusion.31 = f32[64,2048]{1,0:T(8,128)S(1)} fusion(f32[64,352]{1,0:T(8,128)S(1)} %fusion.83, bf16[1,352,2048]{2,1,0:T(8,128)(2,1)} %param.26, bf16[64,2048]{1,0:T(8,128)(2,1)} %copy-done.7, bf16[1,2048,352]{1,2,0:T(8,128)(2,1)} %param.25), kind=kOutput, calls=%fused_computation.64 | convolution fusion | flops 184684544 | bytes 3760128 | tf_op jit(solution)/shard_map/dot_general | solution.py:21
  102.2 3.8 %fusion.8 = bf16[64,2048]{1,0:T(8,128)(2,1)} fusion(f32[64,2048]{1,0:T(8,128)S(1)} %fusion.31, bf16[352,2048]{1,0:T(8,128)(2,1)} %collective-permute-done.18, f32[64]{0:T(128)S(1)} %fusion.54, f32[64,352]{1,0:T(8,128)S(1)} %fusion.118, bf16[64,2048]{1,0:T(8,128)(2,1)S(1)} %copy-done.8, bf16[2048,352]{0,1:T(8,128)(2,1)} %collective-permute-done.17), kind=kOutput, calls=%fused_computation.14 | convolution fusion | flops 185077760 | bytes 4022528 | tf_op jit(solution)/shard_map/dot_general | solution.py:21
  109.1 2.9 %collective-permute-done.25 = bf16[32,2048]{1,0:T(8,128)(2,1)S(1)} collective-permute-done((bf16[32,2048]{1,0:T(8,128)(2,1)S(1)}, bf16[32,2048]{1,0:T(8,128)(2,1)S(1)}, u32[]{:S(2)}, u32[]{:S(2)}) %collective-permute-start.25) | collective-permute-done | bytes 131104 | tf_op jit(solution)/shard_map/ppermute | solution.py:265
  116.7 3.4 %fusion.4 = bf16[128,2048]{1,0:T(8,128)(2,1)S(1)} fusion(f32[128,2048]{1,0:T(8,128)S(1)} %copy-done.9, bf16[352,2048]{1,0:T(8,128)(2,1)} %collective-permute-done.18, f32[128]{0:T(128)S(1)} %pad_maximum_fusion.5, f32[128,352]{0,1:T(8,128)} %fusion.116, bf16[128,2048]{1,0:T(8,128)(2,1)S(1)} %constant_dynamic-update-slice_fusion, ...), kind=kOutput, calls=%fused_computation.7 | convolution fusion | flops 370155520 | bytes 5161472 | tf_op jit(solution)/shard_map/dot_general | solution.py:21
  120.6 2.5 %collective-permute-done.26 = bf16[64,2048]{1,0:T(8,128)(2,1)} collective-permute-done((bf16[64,2048]{1,0:T(8,128)(2,1)}, bf16[64,2048]{1,0:T(8,128)(2,1)}, u32[]{:S(2)}, u32[]{:S(2)}) %collective-permute-start.26) | collective-permute-done | bytes 262176 | tf_op jit(solution)/shard_map/ppermute | solution.py:274
  127.1 3.4 %fusion.1 = bf16[192,2048]{1,0:T(8,128)(2,1)S(1)} fusion(f32[192,2048]{1,0:T(8,128)} %fusion.17, bf16[352,2048]{1,0:T(8,128)(2,1)} %collective-permute-done.18, f32[192]{0:T(256)S(1)} %pad_maximum_fusion.4, f32[192,352]{1,0:T(8,128)} %fusion.101, bf16[2048,352]{0,1:T(8,128)(2,1)S(1)} %collective-permute-done.16, ...), kind=kOutput, calls=%fused_computation.2 | convolution fusion | flops 557592576 | bytes 6300416 | tf_op jit(solution)/shard_map/dot_general | solution.py:21
  130.5 2.9 %collective-permute-done.27 = bf16[64,2048]{1,0:T(8,128)(2,1)S(1)} collective-permute-done((bf16[64,2048]{1,0:T(8,128)(2,1)}, bf16[64,2048]{1,0:T(8,128)(2,1)S(1)}, u32[]{:S(2)}, u32[]{:S(2)}) %collective-permute-start.27) | collective-permute-done | bytes 262176 | tf_op jit(solution)/shard_map/ppermute | solution.py:274
  136.3 1.9 %fusion.115 = f32[64,352]{1,0:T(8,128)S(1)} fusion(bf16[64,2048]{1,0:T(8,128)(2,1)S(1)} %copy-done.6, bf16[2048,352]{0,1:T(8,128)(2,1)} %collective-permute-done.11), kind=kOutput, calls=%fused_computation.167 | convolution fusion | flops 92274688 | bytes 1794048 | tf_op jit(solution)/shard_map/dot_general | solution.py:21
  138.2 2.4 %collective-permute-done.28 = bf16[64,2048]{1,0:T(8,128)(2,1)S(1)} collective-permute-done((bf16[64,2048]{1,0:T(8,128)(2,1)S(1)}, bf16[64,2048]{1,0:T(8,128)(2,1)S(1)}, u32[]{:S(2)}, u32[]{:S(2)}) %collective-permute-start.28) | collective-permute-done | bytes 262176 | tf_op jit(solution)/shard_map/ppermute | solution.py:274
  142.0 3.0 %fusion.9 = bf16[64,2048]{1,0:T(8,128)(2,1)S(1)} fusion(f32[64,2048]{1,0:T(8,128)S(1)} %copy-done.12, bf16[352,2048]{1,0:T(8,128)(2,1)} %collective-permute-done.13, bf16[64,2048]{1,0:T(8,128)(2,1)S(1)} %collective-permute-done.32, bf16[64,2048]{1,0:T(8,128)(2,1)S(1)} %collective-permute-done.28, bf16[192,2048]{1,0:T(8,128)(2,1)S(1)} %fusion.1, ...), kind=kOutput, calls=%fused_computation.15 | convolution fusion | flops 185733120 | bytes 4808704 | tf_op jit(solution)/shard_map/dot_general | solution.py:21
  146.5 4.9 %collective-permute-done.33 = bf16[64,2048]{1,0:T(8,128)(2,1)S(1)} collective-permute-done((bf16[64,2048]{1,0:T(8,128)(2,1)S(1)}, bf16[64,2048]{1,0:T(8,128)(2,1)S(1)}, u32[]{:S(2)}, u32[]{:S(2)}) %collective-permute-start.33) | collective-permute-done | bytes 262176 | tf_op jit(solution)/shard_map/ppermute | solution.py:278
  (173 shorter events, 70.3 us)
Async XLA Ops:
  1.8 6.7 %collective-permute-start = (bf16[272,256]{1,0:T(8,128)(2,1)S(1)}, bf16[272,256]{1,0:T(8,128)(2,1)S(1)}, u32[]{:S(2)}, u32[]{:S(2)}) collective-permute-start(bf16[272,256]{1,0:T(8,128)(2,1)S(1)} %maximum_maximum_fusion.refs_3_), channel_id=1, source_target_pairs={{0,2},{2,4},{4,6},{6,7},{7,5},{5,3},{3,1},{1,0},{8,10},{10,12},{12... | collective-permute-start | bytes 417800 | tf_op jit(solution)/shard_map/ppermute | solution.py:189
  4.9 25.4 %collective-permute-start.9 = (bf16[512,2048]{1,0:T(8,128)(2,1)}, bf16[512,2048]{1,0:T(8,128)(2,1)S(1)}, u32[]{:S(2)}, u32[]{:S(2)}) collective-permute-start(bf16[512,2048]{1,0:T(8,128)(2,1)} %param.20), channel_id=1, source_target_pairs={{0,8},{8,0},{16,24},{24,16},{1,9},{9,1},{17,25},{25,17},{2,10},{10... | collective-permute-start | bytes 6291464 | tf_op jit(solution)/shard_map/ppermute | solution.py:172
  4.9 52.7 %collective-permute-start.17 = (bf16[2048,352]{0,1:T(8,128)(2,1)}, bf16[2048,352]{0,1:T(8,128)(2,1)}, u32[]{:S(2)}, u32[]{:S(2)}) collective-permute-start(bf16[2048,352]{0,1:T(8,128)(2,1)} %bitcast.104), channel_id=1, source_target_pairs={{0,8},{8,0},{16,24},{24,16},{1,9},{9,1},{17,25},{25,17},{2,10},{10... | collective-permute-start | bytes 4325384 | tf_op jit(solution)/shard_map/ppermute | solution.py:177
  5.4 130.8 %collective-permute-start.11 = (bf16[2048,352]{0,1:T(8,128)(2,1)}, bf16[2048,352]{0,1:T(8,128)(2,1)}, u32[]{:S(2)}, u32[]{:S(2)}) collective-permute-start(bf16[2048,352]{0,1:T(8,128)(2,1)} %param.27), channel_id=1, source_target_pairs={{0,8},{8,0},{16,24},{24,16},{1,9},{9,1},{17,25},{25,17},{2,10},{10... | collective-permute-start | bytes 4325384 | tf_op jit(solution)/shard_map/ppermute | solution.py:173
  10.1 7.1 %collective-permute-start.2 = (bf16[272,256]{1,0:T(8,128)(2,1)S(1)}, bf16[272,256]{1,0:T(8,128)(2,1)S(1)}, u32[]{:S(2)}, u32[]{:S(2)}) collective-permute-start(bf16[272,256]{1,0:T(8,128)(2,1)S(1)} %collective-permute-done.refs_4_), channel_id=1, source_target_pairs={{0,2},{2,4},{4,6},{6,7},{7,5},{5,3},{3,1},{1,0},{8,10},{10,12},{12... | collective-permute-start | bytes 417800 | tf_op jit(solution)/shard_map/ppermute | solution.py:189
  27.0 111.2 %collective-permute-start.12 = (bf16[2048,352]{0,1:T(8,128)(2,1)}, bf16[2048,352]{0,1:T(8,128)(2,1)}, u32[]{:S(2)}, u32[]{:S(2)}) collective-permute-start(bf16[2048,352]{0,1:T(8,128)(2,1)} %param.28), channel_id=1, source_target_pairs={{0,8},{8,0},{16,24},{24,16},{1,9},{9,1},{17,25},{25,17},{2,10},{10... | collective-permute-start | bytes 4325384 | tf_op jit(solution)/shard_map/ppermute | solution.py:174
  31.3 8.4 %collective-permute-start.10 = (bf16[64,2048]{1,0:T(8,128)(2,1)S(1)}, bf16[64,2048]{1,0:T(8,128)(2,1)S(1)}, u32[]{:S(2)}, u32[]{:S(2)}) collective-permute-start(bf16[64,2048]{1,0:T(8,128)(2,1)S(1)} %fusion.10), channel_id=1, source_target_pairs={{0,16},{8,24},{16,0},{24,8},{1,17},{9,25},{17,1},{25,9},{2,18},{10... | collective-permute-start | bytes 786440 | tf_op jit(solution)/shard_map/ppermute | solution.py:209
  40.1 7.6 %collective-permute-start.14 = (bf16[64,2048]{1,0:T(8,128)(2,1)S(1)}, bf16[64,2048]{1,0:T(8,128)(2,1)S(1)}, u32[]{:S(2)}, u32[]{:S(2)}) collective-permute-start(bf16[64,2048]{1,0:T(8,128)(2,1)S(1)} %fusion.15), channel_id=1, source_target_pairs={{0,2},{2,4},{4,6},{6,7},{7,5},{5,3},{3,1},{1,0},{8,10},{10,12},{12... | collective-permute-start | bytes 786440 | tf_op jit(solution)/shard_map/ppermute | solution.py:251
  41.7 7.3 %collective-permute-start.15 = (bf16[64,2048]{1,0:T(8,128)(2,1)S(1)}, bf16[64,2048]{1,0:T(8,128)(2,1)}, u32[]{:S(2)}, u32[]{:S(2)}) collective-permute-start(bf16[64,2048]{1,0:T(8,128)(2,1)S(1)} %fusion.15), channel_id=1, source_target_pairs={{2,0},{4,2},{6,4},{7,6},{5,7},{3,5},{1,3},{0,1},{10,8},{12,10},{14... | collective-permute-start | bytes 786440 | tf_op jit(solution)/shard_map/ppermute | solution.py:252
  48.4 24.4 %collective-permute-start.16 = (bf16[2048,352]{0,1:T(8,128)(2,1)S(1)}, bf16[2048,352]{0,1:T(8,128)(2,1)S(1)}, u32[]{:S(2)}, u32[]{:S(2)}) collective-permute-start(bf16[2048,352]{0,1:T(8,128)(2,1)S(1)} %bitcast.103), channel_id=1, source_target_pairs={{0,8},{8,0},{16,24},{24,16},{1,9},{9,1},{17,25},{25,17},{2,10},{10... | collective-permute-start | bytes 4325384 | tf_op jit(solution)/shard_map/ppermute | solution.py:176
  49.1 11.9 %collective-permute-start.19 = (bf16[64,2048]{1,0:T(8,128)(2,1)}, bf16[64,2048]{1,0:T(8,128)(2,1)S(1)}, u32[]{:S(2)}, u32[]{:S(2)}) collective-permute-start(bf16[64,2048]{1,0:T(8,128)(2,1)} %copy-done.19), channel_id=1, source_target_pairs={{0,2},{2,4},{4,6},{6,7},{7,5},{5,3},{3,1},{1,0},{8,10},{10,12},{12... | collective-permute-start | bytes 786440 | tf_op jit(solution)/shard_map/ppermute | solution.py:251
  57.6 8.0 %collective-permute-start.20 = (bf16[64,2048]{1,0:T(8,128)(2,1)}, bf16[64,2048]{1,0:T(8,128)(2,1)S(1)}, u32[]{:S(2)}, u32[]{:S(2)}) collective-permute-start(bf16[64,2048]{1,0:T(8,128)(2,1)} %collective-permute-done.15), channel_id=1, source_target_pairs={{2,0},{4,2},{6,4},{7,6},{5,7},{3,5},{1,3},{0,1},{10,8},{12,10},{14... | collective-permute-start | bytes 786440 | tf_op jit(solution)/shard_map/ppermute | solution.py:252
  61.7 28.0 %collective-permute-start.18 = (bf16[352,2048]{1,0:T(8,128)(2,1)}, bf16[352,2048]{1,0:T(8,128)(2,1)}, u32[]{:S(2)}, u32[]{:S(2)}) collective-permute-start(bf16[352,2048]{1,0:T(8,128)(2,1)} %bitcast.7), channel_id=1, source_target_pairs={{0,8},{8,0},{16,24},{24,16},{1,9},{9,1},{17,25},{25,17},{2,10},{10... | collective-permute-start | bytes 4325384 | tf_op jit(solution)/shard_map/ppermute | solution.py:178
  65.6 8.8 %collective-permute-start.21 = (bf16[64,2048]{1,0:T(8,128)(2,1)}, bf16[64,2048]{1,0:T(8,128)(2,1)}, u32[]{:S(2)}, u32[]{:S(2)}) collective-permute-start(bf16[64,2048]{1,0:T(8,128)(2,1)} %copy-done.16), channel_id=1, source_target_pairs={{0,2},{2,4},{4,6},{6,7},{7,5},{5,3},{3,1},{1,0},{8,10},{10,12},{12... | collective-permute-start | bytes 786440 | tf_op jit(solution)/shard_map/ppermute | solution.py:251
  72.7 7.5 %collective-permute-start.22 = (bf16[64,2048]{1,0:T(8,128)(2,1)}, bf16[64,2048]{1,0:T(8,128)(2,1)S(1)}, u32[]{:S(2)}, u32[]{:S(2)}) collective-permute-start(bf16[64,2048]{1,0:T(8,128)(2,1)} %copy-done.17), channel_id=1, source_target_pairs={{2,0},{4,2},{6,4},{7,6},{5,7},{3,5},{1,3},{0,1},{10,8},{12,10},{14... | collective-permute-start | bytes 786440 | tf_op jit(solution)/shard_map/ppermute | solution.py:252
  74.4 63.8 %collective-permute-start.13 = (bf16[352,2048]{1,0:T(8,128)(2,1)}, bf16[352,2048]{1,0:T(8,128)(2,1)}, u32[]{:S(2)}, u32[]{:S(2)}) collective-permute-start(bf16[352,2048]{1,0:T(8,128)(2,1)} %param.29), channel_id=1, source_target_pairs={{0,8},{8,0},{16,24},{24,16},{1,9},{9,1},{17,25},{25,17},{2,10},{10... | collective-permute-start | bytes 4325384 | tf_op jit(solution)/shard_map/ppermute | solution.py:175
  80.2 15.2 %collective-permute-start.23 = (bf16[32,2048]{1,0:T(8,128)(2,1)S(1)}, bf16[32,2048]{1,0:T(8,128)(2,1)}, u32[]{:S(2)}, u32[]{:S(2)}) collective-permute-start(bf16[32,2048]{1,0:T(8,128)(2,1)S(1)} %slice.205), channel_id=1, source_target_pairs={{0,2},{2,4},{4,6},{6,7},{7,5},{5,3},{3,1},{1,0},{8,10},{10,12},{12... | collective-permute-start | bytes 393224 | tf_op jit(solution)/shard_map/ppermute | solution.py:257
  89.7 6.6 %collective-permute-start.24 = (bf16[32,2048]{1,0:T(8,128)(2,1)}, bf16[32,2048]{1,0:T(8,128)(2,1)}, u32[]{:S(2)}, u32[]{:S(2)}) collective-permute-start(bf16[32,2048]{1,0:T(8,128)(2,1)} %slice.206), channel_id=1, source_target_pairs={{2,0},{4,2},{6,4},{7,6},{5,7},{3,5},{1,3},{0,1},{10,8},{12,10},{14... | collective-permute-start | bytes 393224 | tf_op jit(solution)/shard_map/ppermute | solution.py:258
  114.0 6.7 %collective-permute-start.30 = (bf16[64,2048]{1,0:T(8,128)(2,1)}, bf16[64,2048]{1,0:T(8,128)(2,1)}, u32[]{:S(2)}, u32[]{:S(2)}) collective-permute-start(bf16[64,2048]{1,0:T(8,128)(2,1)} %pad_maximum_fusion.3), channel_id=1, source_target_pairs={{2,0},{4,2},{6,4},{7,6},{5,7},{3,5},{1,3},{0,1},{10,8},{12,10},{14... | collective-permute-start | bytes 786440 | tf_op jit(solution)/shard_map/ppermute | solution.py:275
  115.8 7.4 %collective-permute-start.26 = (bf16[64,2048]{1,0:T(8,128)(2,1)}, bf16[64,2048]{1,0:T(8,128)(2,1)}, u32[]{:S(2)}, u32[]{:S(2)}) collective-permute-start(bf16[64,2048]{1,0:T(8,128)(2,1)} %pad_maximum_fusion.2), channel_id=1, source_target_pairs={{0,2},{2,4},{4,6},{6,7},{7,5},{5,3},{3,1},{1,0},{8,10},{10,12},{12... | collective-permute-start | bytes 786440 | tf_op jit(solution)/shard_map/ppermute | solution.py:274
  125.0 8.4 %collective-permute-start.27 = (bf16[64,2048]{1,0:T(8,128)(2,1)}, bf16[64,2048]{1,0:T(8,128)(2,1)S(1)}, u32[]{:S(2)}, u32[]{:S(2)}) collective-permute-start(bf16[64,2048]{1,0:T(8,128)(2,1)} %get-tuple-element.33), channel_id=1, source_target_pairs={{0,2},{2,4},{4,6},{6,7},{7,5},{5,3},{3,1},{1,0},{8,10},{10,12},{12... | collective-permute-start | bytes 786440 | tf_op jit(solution)/shard_map/ppermute | solution.py:274
  125.8 8.3 %collective-permute-start.31 = (bf16[64,2048]{1,0:T(8,128)(2,1)S(1)}, bf16[64,2048]{1,0:T(8,128)(2,1)S(1)}, u32[]{:S(2)}, u32[]{:S(2)}) collective-permute-start(bf16[64,2048]{1,0:T(8,128)(2,1)S(1)} %get-tuple-element.34), channel_id=1, source_target_pairs={{2,0},{4,2},{6,4},{7,6},{5,7},{3,5},{1,3},{0,1},{10,8},{12,10},{14... | collective-permute-start | bytes 786440 | tf_op jit(solution)/shard_map/ppermute | solution.py:275
  134.2 6.4 %collective-permute-start.28 = (bf16[64,2048]{1,0:T(8,128)(2,1)S(1)}, bf16[64,2048]{1,0:T(8,128)(2,1)S(1)}, u32[]{:S(2)}, u32[]{:S(2)}) collective-permute-start(bf16[64,2048]{1,0:T(8,128)(2,1)S(1)} %get-tuple-element.29), channel_id=1, source_target_pairs={{0,2},{2,4},{4,6},{6,7},{7,5},{5,3},{3,1},{1,0},{8,10},{10,12},{12... | collective-permute-start | bytes 786440 | tf_op jit(solution)/shard_map/ppermute | solution.py:274
  144.9 6.4 %collective-permute-start.33 = (bf16[64,2048]{1,0:T(8,128)(2,1)S(1)}, bf16[64,2048]{1,0:T(8,128)(2,1)S(1)}, u32[]{:S(2)}, u32[]{:S(2)}) collective-permute-start(bf16[64,2048]{1,0:T(8,128)(2,1)S(1)} %fusion.9), channel_id=1, source_target_pairs={{0,16},{8,24},{16,0},{24,8},{1,17},{9,25},{17,1},{25,9},{2,18},{10... | collective-permute-start | bytes 786440 | tf_op jit(solution)/shard_map/ppermute | solution.py:278
  (31 other events, 158.9 us)

commit v2 on v1

--- a/solution.py
+++ b/solution.py
@@ -15,6 +15,10 @@
 norm_eps = 1e-06
 f32 = jnp.float32
 bf16 = jnp.bfloat16
+STAGE_VMEM = 1 << 20
+SHARED_VMEM = 8 << 20
+EXPERT_VMEM = 5 << 20
+COLUMNS = 512
 
 
 def dot(a, b):
@@ -33,8 +37,12 @@
     else:
         max_in, sum_in, acc_in = refs.pop(0), refs.pop(0), refs.pop(0)
     if last:
-        core_ref = refs.pop(0)
+        core_ref, proj_ref = refs.pop(0), refs.pop(0)
     page_refs = [refs.pop(0) for _ in range(page_count)]
+    if last:
+        keep_ref, send_ref, proj_buf, proj_sem = refs
+        fetch = pltpu.make_async_copy(proj_ref, proj_buf, proj_sem)
+        fetch.start()
     scaling = 1.0 / math.sqrt(HD)
     q = jnp.concatenate([q_ref[:, h * HD : (h + 1) * HD] for h in range(heads)], axis=0)
     blocks = [(ref[:page_len, :HD], ref[:page_len, HD:]) for ref in page_refs]
@@ -73,15 +81,17 @@
         total = total + jnp.sum(e, axis=-1, keepdims=True)
         acc = acc + jnp.dot(e.astype(bf16), v, preferred_element_type=f32)
     if last:
-        keep_ref, send_ref = refs
+        out = (acc / total).astype(bf16)
+        rows = jnp.concatenate([out[h * tokens : (h + 1) * tokens] for h in range(heads)], axis=1)
         half = tokens // 2
-        out = (acc / total).astype(bf16)
         second = core_ref[0] == 1
-        for h in range(heads):
-            low = out[h * tokens : h * tokens + half]
-            high = out[h * tokens + half : (h + 1) * tokens]
-            keep_ref[:, h * HD : (h + 1) * HD] = jnp.where(second, high, low)
-            send_ref[:, h * HD : (h + 1) * HD] = jnp.where(second, low, high)
+        fetch.wait()
+        for c in range(0, proj_buf.shape[1], COLUMNS):
+            cols = slice(c, c + COLUMNS)
+            terms = jnp.dot(rows, proj_buf[:, cols], preferred_element_type=f32).astype(bf16)
+            low, high = terms[:half], terms[half:]
+            keep_ref[:, cols] = jnp.where(second, high, low)
+            send_ref[:, cols] = jnp.where(second, low, high)
     else:
         max_out, sum_out, acc_out = refs
         max_out[...] = jnp.broadcast_to(new_max, max_out.shape)
@@ -89,7 +99,7 @@
         acc_out[...] = acc
 
 
-def attend(queries, pages, page_len, state=None, suffix=None, core=None):
+def attend(queries, pages, page_len, state=None, suffix=None, core=None, out_proj=None):
     tokens, width = queries.shape
     heads = width // HD
     first, last = state is None, core is not None
@@ -102,27 +112,180 @@
         args += list(state)
         specs += [vmem] * 3
     if last:
-        args.append(core)
-        specs.append(smem)
+        args += [core, pltpu.with_memory_space_constraint(out_proj, pltpu.HBM)]
+        specs += [smem, pl.BlockSpec(memory_space=pl.ANY)]
     args += pages
     specs += [vmem] * len(pages)
     if last:
-        outs = [jax.ShapeDtypeStruct((tokens // 2, width), bf16)] * 2
+        outs = [jax.ShapeDtypeStruct((tokens // 2, out_proj.shape[1]), bf16)] * 2
+        scratch = [pltpu.VMEM(out_proj.shape, bf16), pltpu.SemaphoreType.DMA(())]
     else:
         outs = [jax.ShapeDtypeStruct((heads * tokens, HD), f32)] * 3
+        scratch = []
     keys = sum(page_len for _ in pages) + (tokens if first else 0)
     return pl.pallas_call(
         functools.partial(attend_kernel, heads, tokens, page_len, len(pages), first, last),
         out_shape=outs,
         in_specs=specs,
         out_specs=[vmem] * len(outs),
-        compiler_params=pltpu.CompilerParams(vmem_limit_bytes=32 << 20),
+        scratch_shapes=scratch,
+        compiler_params=pltpu.CompilerParams(vmem_limit_bytes=12 << 20),
         cost_estimate=pl.CostEstimate(
             flops=4 * heads * tokens * keys * HD,
             bytes_accessed=4 * keys * HD + 2 * tokens * width,
             transcendentals=heads * tokens * keys,
         ),
     )(*args)
+
+
+def stage_kernel(*refs):
+    sources, outs, sems = refs[:6], refs[6:9], refs[9]
+    block = sources[0].shape[0]
+    copies = [
+        pltpu.make_async_copy(
+            sources[i], outs[i // 2].at[pl.ds(i % 2 * block, block)], sems.at[i]
+        )
+        for i in range(6)
+    ]
+    for copy in copies:
+        copy.start()
+    for copy in copies:
+        copy.wait()
+
+
+def stage(weights):
+    block, width = weights[0].shape
+    return pl.pallas_call(
+        stage_kernel,
+        out_shape=[pltpu.VMEM((2 * block, width), bf16)] * 3,
+        in_specs=[pl.BlockSpec(memory_space=pl.ANY)] * 6,
+        out_specs=[pl.BlockSpec(memory_space=pltpu.VMEM)] * 3,
+        scratch_shapes=[pltpu.SemaphoreType.DMA((6,))],
+        compiler_params=pltpu.CompilerParams(vmem_limit_bytes=STAGE_VMEM),
+        cost_estimate=pl.CostEstimate(
+            flops=0, bytes_accessed=12 * block * width, transcendentals=0
+        ),
+    )(*[pltpu.with_memory_space_constraint(w, pltpu.HBM) for w in weights])
+
+
+def fetches(sources, bufs, sems):
+    block = sources[0].shape[0]
+    return [
+        pltpu.make_async_copy(
+            sources[i], bufs[i // 2 % 2].at[pl.ds(i % 2 * block, block)], sems.at[i]
+        )
+        for i in range(6)
+    ]
+
+
+def hidden_units(x, copies, bufs):
+    contract = (((1,), (1,)), ((), ()))
+    for copy in copies[:4]:
+        copy.start()
+    for copy in copies[:2]:
+        copy.wait()
+    gate = lax.dot_general(x, bufs[0][...], contract, preferred_element_type=f32)
+    for copy in copies[4:]:
+        copy.start()
+    for copy in copies[2:4]:
+        copy.wait()
+    up = lax.dot_general(x, bufs[1][...], contract, preferred_element_type=f32)
+    hidden = (gate / (1.0 + jnp.exp(-gate)) * up).astype(bf16)
+    for copy in copies[4:]:
+        copy.wait()
+    return hidden
+
+
+def glu_call(kernel, args, specs, weights, outs, rows):
+    block, width = weights[0].shape
+    vmem = pl.BlockSpec(memory_space=pltpu.VMEM)
+    return pl.pallas_call(
+        kernel,
+        out_shape=outs,
+        in_specs=specs + [pl.BlockSpec(memory_space=pl.ANY)] * 6,
+        out_specs=[vmem] * len(outs),
+        scratch_shapes=[pltpu.VMEM((2 * block, width), bf16)] * 2
+        + [pltpu.SemaphoreType.DMA((6,))],
+        compiler_params=pltpu.CompilerParams(vmem_limit_bytes=SHARED_VMEM),
+        cost_estimate=pl.CostEstimate(
+            flops=12 * rows * width * block,
+            bytes_accessed=12 * block * width,
+            transcendentals=2 * rows * block,
+        ),
+    )(*args, *[pltpu.with_memory_space_constraint(w, pltpu.HBM) for w in weights])
+
+
+def shared_kernel(x_ref, *refs):
+    sources, out_ref, bufs, sems = refs[:6], refs[6], refs[7:9], refs[9]
+    width = out_ref.shape[1]
+    hidden = hidden_units(x_ref[:, :width], fetches(sources, bufs, sems), bufs)
+    for c in range(0, width, COLUMNS):
+        cols = slice(c, c + COLUMNS)
+        out_ref[:, cols] = jnp.dot(hidden, bufs[0][:, cols], preferred_element_type=f32)
+
+
+def shared_expert(rows, weights):
+    width = weights[0].shape[1]
+    outs = [jax.ShapeDtypeStruct((rows.shape[0], width), f32)]
+    specs = [pl.BlockSpec(memory_space=pltpu.VMEM)]
+    return glu_call(shared_kernel, [rows], specs, weights, outs, rows.shape[0])[0]
+
+
+def expert_kernel(n_experts, counts, plus, *refs):
+    refs = list(refs)
+    place_ref = refs.pop(0)
+    sources = [refs.pop(0) for _ in range(sum(counts))]
+    shared_ref = refs.pop(0) if plus else None
+    gate_ref, up_ref, down_ref = refs[:3]
+    keeps, send_ref = refs[3:-1], refs[-1]
+    width = send_ref.shape[1]
+    x = jnp.concatenate([ref[:, :width] for ref in sources], axis=0)
+    contract = (((1,), (1,)), ((), ()))
+    gate = lax.dot_general(x, gate_ref[...], contract, preferred_element_type=f32)
+    up = lax.dot_general(x, up_ref[...], contract, preferred_element_type=f32)
+    hidden = (gate / (1.0 + jnp.exp(-gate)) * up).astype(bf16)
+    lanes = jnp.concatenate([ref[:, width:] for ref in sources], axis=0).astype(f32)
+    lane = lax.broadcasted_iota(jnp.int32, lanes.shape, 1)
+    e, second = place_ref[0], place_ref[1] == 1
+    scale = jnp.sum(
+        jnp.where((lane == e) | (lane == e + n_experts), lanes, 0.0), axis=1, keepdims=True
+    )
+    part = keeps[0].shape[0]
+    for c in range(0, width, COLUMNS):
+        cols = slice(c, c + COLUMNS)
+        out = jnp.dot(hidden, down_ref[:, cols], preferred_element_type=f32) * scale
+        for i, keep_ref in enumerate(keeps):
+            low = out[2 * part * i : 2 * part * i + part]
+            high = out[2 * part * i + part : 2 * part * (i + 1)]
+            if plus and i == 0:
+                low = low + shared_ref[:part, cols]
+                high = high + shared_ref[part:, cols]
+            low, high = low.astype(bf16), high.astype(bf16)
+            keep_ref[:, cols] = jnp.where(second, high, low)
+            send_ref[part * i : part * (i + 1), cols] = jnp.where(second, low, high)
+
+
+def expert(blocks, weights, n_experts, place, shared=None):
+    counts = [len(b) for b in blocks]
+    rows = sum(a.shape[0] for b in blocks for a in b)
+    part = rows // len(blocks) // 2
+    hidden, width = weights[0].shape
+    vmem, smem = pl.BlockSpec(memory_space=pltpu.VMEM), pl.BlockSpec(memory_space=pltpu.SMEM)
+    args = [place] + [a for b in blocks for a in b] + ([] if shared is None else [shared])
+    outs = pl.pallas_call(
+        functools.partial(expert_kernel, n_experts, counts, shared is not None),
+        out_shape=[jax.ShapeDtypeStruct((part, width), bf16)] * len(blocks)
+        + [jax.ShapeDtypeStruct((part * len(blocks), width), bf16)],
+        in_specs=[smem] + [vmem] * (len(args) - 1 + 3),
+        out_specs=[vmem] * (len(blocks) + 1),
+        compiler_params=pltpu.CompilerParams(vmem_limit_bytes=EXPERT_VMEM),
+        cost_estimate=pl.CostEstimate(
+            flops=6 * rows * width * hidden,
+            bytes_accessed=4 * rows * width,
+            transcendentals=rows * hidden,
+        ),
+    )(*args, *[pltpu.with_memory_space_constraint(w, pltpu.VMEM) for w in weights])
+    return outs[:-1], outs[-1]
 
 
 def on_device_ring(
@@ -153,6 +316,7 @@
     sibling = [(i, i ^ 1) for i in range(req)]
     across = [(i, i ^ 2) for i in range(req)]
     core = lax.rem(lax.axis_index("req"), 2)
+    plane = lax.div(lax.axis_index("req"), 2)
     me = lax.axis_index("exp")
 
     def half_of(x):
@@ -160,53 +324,47 @@
 
     slots = jnp.arange(n, dtype=jnp.int32)
     dense = jnp.sum(
-        jnp.where(routes.T[None] == slots[:, None, None], route_weights.T[None], 0.0), axis=1
+        jnp.where(half_of(routes)[:, :, None] == slots, half_of(route_weights)[:, :, None], 0.0),
+        axis=1,
     )
     head = lax.reduce_precision(dense, 8, 7)
     rest = lax.reduce_precision(dense - head, 8, 7)
-    gates = jnp.concatenate([head, rest], axis=1).astype(bf16)
-    page_len = prefix_kv.shape[1]
-    pad = -n % 16
-    page = jnp.concatenate([prefix_kv[0], gates, jnp.zeros((pad, gates.shape[1]), bf16)], axis=0)
-
-    out_proj_sib = lax.ppermute(out_proj, "req", sibling)
-    shared_gate_sib = lax.ppermute(shared_gate, "req", sibling)
-    shared_up_sib = lax.ppermute(shared_up, "req", sibling)
-    shared_down_sib = lax.ppermute(shared_down, "req", sibling)
-    gate_sib = lax.ppermute(expert_gate[0], "req", sibling)
-    up_sib = lax.ppermute(expert_up[0], "req", sibling)
-    down_sib = lax.ppermute(expert_down[0], "req", sibling)
+    gates = jnp.concatenate(
+        [head, rest, jnp.zeros((half, -2 * n % HD), f32)], axis=1
+    ).astype(bf16)
+    page = prefix_kv[0]
+    page_len = page.shape[0]
+
+    shared_weights = (shared_gate.T, shared_up.T, shared_down)
+    expert_weights = (expert_gate[0].T, expert_up[0].T, expert_down[0])
+
+    def with_sibling(weights):
+        return [w for own in weights for w in (own, lax.ppermute(own, "req", sibling))]
+
+    shared_weights = with_sibling(shared_weights)
+    expert_weights = with_sibling(expert_weights)
 
     suffix = (suffix_lengths, suffix_kv[:, 0])
     core_arr = jnp.reshape(core, (1,)).astype(jnp.int32)
-    gate_rows = {0: gates}
     from_left, from_right = page, page
-    state = None
-    arrived = [page]
-    cut = (page_len // 2)
-    for s in range(1, steps + 1):
-        if s < steps:
-            from_left = lax.ppermute(from_left, "exp", right)
-            from_right = lax.ppermute(from_right, "exp", left)
-            now = [from_left, from_right]
-            gate_rows[s] = from_left[page_len : page_len + n]
-            gate_rows[-s] = from_right[page_len : page_len + n]
-        else:
-            low = lax.ppermute(from_left[:cut], "exp", right)
-            high = lax.ppermute(from_right[cut:], "exp", left)
-            gate_rows[s] = high[page_len - cut : page_len - cut + n]
-            now = [low, high[: page_len - cut]]
-        if s == 1:
-            arrived += now
-            state = attend(queries, arrived, page_len, suffix=suffix)
-        elif s < steps:
-            state = attend(queries, now, page_len, state=state)
-        else:
-            keep, send = attend(queries, now, cut, state=state, core=core_arr)
+    cut = page_len // 2
+    state = attend(queries, [page], page_len, suffix=suffix)
+    for s in range(1, steps):
+        from_left = lax.ppermute(from_left, "exp", right)
+        from_right = lax.ppermute(from_right, "exp", left)
+        from_left, state = lax.optimization_barrier((from_left, state))
+        state = attend(queries, [from_left, from_right], page_len, state=state)
+    low = lax.ppermute(from_left[:cut], "exp", right)
+    high = lax.ppermute(from_right[cut:], "exp", left)
+    low, state = lax.optimization_barrier((low, state))
+    keep, send = attend(
+        queries, [low, high], cut, state=state, core=core_arr, out_proj=out_proj
+    )
 
     other = lax.ppermute(send, "req", sibling)
-    terms = (dot(keep, out_proj) + dot(other, out_proj_sib)).astype(bf16)
+    terms = (keep.astype(f32) + other.astype(f32)).astype(bf16)
     terms_across = lax.ppermute(terms, "req", across)
+    terms_across, staged = lax.optimization_barrier((terms_across, stage(expert_weights)))
     hidden_state = (
         half_of(residual).astype(f32) + (terms.astype(f32) + terms_across.astype(f32))
     ).astype(bf16)
@@ -216,72 +374,67 @@
         hidden_float * lax.rsqrt(mean_square + norm_eps) * norm_gain.astype(f32)
     ).astype(bf16)
 
-    def glu(rows, weights, scale):
-        total = 0.0
-        for gate, up, down in weights:
-            hidden = (jax.nn.silu(dot(rows, gate)) * dot(rows, up)).astype(bf16)
-            total = total + dot(hidden, down)
-        return total if scale is None else total * scale
-
-    shared_weights = [
-        (shared_gate, shared_up, shared_down),
-        (shared_gate_sib, shared_up_sib, shared_down_sib),
-    ]
-    expert_weights = [
-        (expert_gate[0], expert_up[0], expert_down[0]),
-        (gate_sib, up_sib, down_sib),
-    ]
-    shared_part = glu(normed, shared_weights, None)
-
-    def scale_of(distance):
-        row = lax.dynamic_slice_in_dim(gate_rows[distance], me, 1, 0)[0].astype(f32)
-        return half_of(row[:tokens] + row[tokens:])
-
-    def experts(blocks):
-        rows = jnp.concatenate([b for _, b in blocks], axis=0)
-        scale = jnp.concatenate([scale_of(d) for d, _ in blocks])[:, None]
-        out = glu(rows, expert_weights, scale).astype(bf16)
-        return {d: out[i * half : (i + 1) * half] for i, (d, _) in enumerate(blocks)}
-
-    parts = {}
+    normed = jnp.concatenate([normed, gates], axis=1)
+    place = jnp.stack([me, plane]).astype(jnp.int32)
+
+    own, summand = {}, {}
+    quarter = half // 2
+
+    def work(blocks, shared=None):
+        keeps, send = expert([b for _, b in blocks], staged, n, place, shared)
+        for (d, _), keep in zip(blocks, keeps):
+            own[d] = keep
+        got = lax.ppermute(send, "req", across)
+        for i, (d, _) in enumerate(blocks):
+            summand[d] = got[i * quarter : (i + 1) * quarter]
+        return keeps, got
+
     from_left, from_right = normed, normed
-    quarter = half // 2
-    for s in range(1, steps + 1):
-        if s < steps:
-            from_left = lax.ppermute(from_left, "exp", right)
-            from_right = lax.ppermute(from_right, "exp", left)
-            now = [(s, from_left), (-s, from_right)]
-            if s == 1:
-                now = [(0, normed)] + now
+    before = shared_part = shared_expert(normed, shared_weights)
+    on_way, next_on_way = (), ()
+    for s in range(1, steps):
+        from_left = lax.ppermute(from_left, "exp", right)
+        from_right = lax.ppermute(from_right, "exp", left)
+        from_left, before, on_way = lax.optimization_barrier((from_left, before, on_way))
+        blocks = [(s, [from_left]), (-s, [from_right])]
+        on_way = next_on_way
+        if s == 1:
+            before, next_on_way = work([(0, [normed])] + blocks, shared_part)
         else:
-            low = lax.ppermute(from_left[:quarter], "exp", right)
-            high = lax.ppermute(from_right[quarter:], "exp", left)
-            now = [(s, jnp.concatenate([low, high], axis=0))]
-        parts.update(experts(now))
-
-    def add(a, b):
-        return (a.astype(f32) + b.astype(f32)).astype(bf16)
-
-    to_right = lax.ppermute(parts[steps][:quarter], "exp", right)
-    to_left = lax.ppermute(parts[steps][quarter:], "exp", left)
+            before, next_on_way = work(blocks)
+    low = lax.ppermute(from_left[:quarter], "exp", right)
+    high = lax.ppermute(from_right[quarter:], "exp", left)
+    low, before, on_way = lax.optimization_barrier((low, before, on_way))
+    work([(steps, [low, high])])
+
+    def part(d):
+        return own[d].astype(f32) + summand[d].astype(f32)
+
+    eighth = quarter // 2
+    far = part(steps).astype(bf16)
+    to_right = lax.ppermute(far[:eighth], "exp", right)
+    to_left = lax.ppermute(far[eighth:], "exp", left)
     for k in range(steps - 1, 0, -1):
-        a, b = parts[-k], parts[k]
+        a, b = part(-k), part(k)
         if k == steps - 1:
-            a = jnp.concatenate([add(a[:quarter], to_right), a[quarter:]], axis=0)
-            b = jnp.concatenate([b[:quarter], add(b[quarter:], to_left)], axis=0)
+            a = jnp.concatenate([a[:eighth] + to_right.astype(f32), a[eighth:]], axis=0)
+            b = jnp.concatenate([b[:eighth], b[eighth:] + to_left.astype(f32)], axis=0)
         else:
-            a, b = add(a, to_right), add(b, to_left)
-        to_right = lax.ppermute(a, "exp", right)
-        to_left = lax.ppermute(b, "exp", left)
-    routed = parts[0].astype(f32) + (to_right.astype(f32) + to_left.astype(f32))
-    summed = (shared_part + routed).astype(bf16)
-    summed_across = lax.ppermute(summed, "req", across)
-    mine = (hidden_float + (summed.astype(f32) + summed_across.astype(f32))).astype(bf16)
-    theirs = lax.ppermute(mine, "req", sibling)
-    first = core == 0
-    return jnp.concatenate(
-        [jnp.where(first, mine, theirs), jnp.where(first, theirs, mine)], axis=0
-    )
+            a, b = a + to_right.astype(f32), b + to_left.astype(f32)
+        to_right = lax.ppermute(a.astype(bf16), "exp", right)
+        to_left = lax.ppermute(b.astype(bf16), "exp", left)
+    total = part(0) + (to_right.astype(f32) + to_left.astype(f32))
+    hidden_here = lax.dynamic_slice_in_dim(hidden_state, plane * quarter, quarter, 0)
+    mine = (hidden_here.astype(f32) + total).astype(bf16)
+
+    def joined(index, here, there):
+        first = index == 0
+        return jnp.concatenate(
+            [jnp.where(first, here, there), jnp.where(first, there, here)], axis=0
+        )
+
+    mine = joined(plane, mine, lax.ppermute(mine, "req", across))
+    return joined(core, mine, lax.ppermute(mine, "req", sibling))
 
 
 def on_device(

time: 155 us -> 116 us (0.75)
  matrix products: 53.2 us -> 0 us
  Pallas kernels: 6.23 us -> 30.8 us
  waiting for transfers between devices: 45.4 us -> 39.9 us
  other arithmetic: 7.58 us -> 2.85 us
  starting transfers between devices: 29.5 us -> 33.5 us
  local copies, waits for them, and re-layouts: 11.6 us -> 8.27 us
    dot_general x22 -> x0, matrix products: 53.2 us -> none  [dot(): return jnp.dot(a, b, preferred_element_type=f32)]
    pallas_call x0 -> x6, Pallas kernels: none -> 21.8 us  [the longest x4 12.4 us: expert(): pl.pallas_call(functools.partial(expert_kernel, n_experts, counts, shared...]
    ppermute x6, waiting for transfers between devices: 12 us -> 0.02 us  [on_device_ring(): from_right = lax.ppermute(from_right, 'exp', left)]
    ppermute x17 -> x20, waiting for transfers between devices: 20.8 us -> 31.2 us  [the longest x3 10.3 us: on_device_ring(): to_right = lax.ppermute(a.astype(bf16), 'exp', right)]
    ppermute x1, waiting for transfers between devices: 6.78 us -> 0.01 us  [on_device_ring(): terms_across = lax.ppermute(terms, 'req', across)]
    ppermute x17 -> x20, starting transfers between devices: 10.3 us -> 14.5 us  [the longest x3 4.32 us: on_device_ring(): to_right = lax.ppermute(a.astype(bf16), 'exp', right)]
    pallas_call x4 -> x5, Pallas kernels: 6.23 us -> 8.91 us  [attend(): pl.pallas_call(functools.partial(attend_kernel, heads, tokens, page_len,...]
    concatenate x7 -> x4, other arithmetic: 3.52 us -> 0.88 us  [the longest x2 0.86 us: joined(): jnp.concatenate([jnp.where(first, here, there), jnp.where(first, there, h...]
  transfers between devices with their start and end apart: 35 -> 38, of which waited for: 22 -> 20; matrix products, arithmetic and copies ran while one was open for 40% -> 1% of each run, Pallas kernels for 4% -> 24%
where the time goes in v2:
time: 116 us
  waiting for transfers between devices  39.9 us (34%)
  starting transfers between devices  33.5 us (29%)
  Pallas kernels  30.8 us (27%)
  local copies, waits for them, and re-layouts  8.27 us (7%)
  other arithmetic  2.85 us (2%)
    pallas_call x4, Pallas kernels, expert(): pl.pallas_call(functools.partial(expert_kernel, n_experts, counts, shared...  12.4 us
    ppermute x6, starting transfers between devices, on_device_ring(): from_left = lax.ppermute(from_left, 'exp', right)  11.7 us
    ppermute x3, waiting for transfers between devices, on_device_ring(): to_right = lax.ppermute(a.astype(bf16), 'exp', right)  10.3 us
    ppermute x4, waiting for transfers between devices, work(): got = lax.ppermute(send, 'req', across)  10.1 us
    pallas_call x5, Pallas kernels, attend(): pl.pallas_call(functools.partial(attend_kernel, heads, tokens, page_len,...  8.91 us
    unnamed x38, local copies, waits for them, and re-layouts  7.68 us
    pallas_call x1, Pallas kernels, glu_call(): pl.pallas_call(kernel, out_shape=outs, in_specs=specs + [pl.BlockSpec(mem...  5.88 us
    ppermute x3, starting transfers between devices, on_device_ring(): to_right = lax.ppermute(a.astype(bf16), 'exp', right)  4.32 us
  transfers between devices with their start and end apart: 38, of which 20 were waited for; matrix products, arithmetic and copies ran while one was open for 1% of the time, Pallas kernels for 24%

profile of v2, /device:TPU:0, one launch (start us, length us, event | category | flops | bytes accessed | tf_op | source)
XLA Modules:
  0.0 115.7 jit_solution(12766328558182266952)
XLA Ops:
  0.5 3.0 %collective-permute-start = (bf16[256,256]{1,0:T(8,128)(2,1)}, bf16[256,256]{1,0:T(8,128)(2,1)S(1)}, u32[]{:S(2)}, u32[]{:S(2)}) collective-permute-start(bf16[256,256]{1,0:T(8,128)(2,1)} %bitcast.14), channel_id=1, source_target_pairs={{0,2},{2,4},{4,6},{6,7},{7,5},{5,3},{3,1},{1,0},{8,10},{10,12},{12... | collective-permute-start | bytes 393224 | tf_op jit(solution)/shard_map/ppermute | solution.py:353
  8.0 2.1 %collective-permute-start.1 = (bf16[256,256]{1,0:T(8,128)(2,1)S(1)}, bf16[256,256]{1,0:T(8,128)(2,1)S(1)}, u32[]{:S(2)}, u32[]{:S(2)}) collective-permute-start(bf16[256,256]{1,0:T(8,128)(2,1)S(1)} %collective-permute-done.refs_4_), channel_id=1, source_target_pairs={{0,2},{2,4},{4,6},{6,7},{7,5},{5,3},{3,1},{1,0},{8,10},{10,12},{12... | collective-permute-start | bytes 393224 | tf_op jit(solution)/shard_map/ppermute | solution.py:353
  10.1 1.9 %shard_map.146 = (f32[512,128]{1,0:T(8,128)S(1)}, f32[512,128]{1,0:T(8,128)S(1)}, f32[512,128]{1,0:T(8,128)S(1)}) custom-call(bf16[128,512]{1,0:T(8,128)(2,1)S(1)} %copy-done.5, f32[512,128]{1,0:T(8,128)S(1)} %get-tuple-element.62.refs_1_, f32[512,128]{1,0:T(8,128)S(1)} %get-tuple-element.63.refs_2_, f32[512,128]{1,0:T(8,128)S(1)} %get-tuple-element.64.refs_3_, ...), custom_call_target="tpu_custom_call" | custom-call | flops 134217728 | bytes 393216 | tf_op jit(solution)/shard_map/pallas_call | solution.py:126
  13.3 1.8 %collective-permute-start.3 = (bf16[256,256]{1,0:T(8,128)(2,1)S(1)}, bf16[256,256]{1,0:T(8,128)(2,1)S(1)}, u32[]{:S(2)}, u32[]{:S(2)}) collective-permute-start(bf16[256,256]{1,0:T(8,128)(2,1)S(1)} %collective-permute-done.1.refs_4_), channel_id=1, source_target_pairs={{0,2},{2,4},{4,6},{6,7},{7,5},{5,3},{3,1},{1,0},{8,10},{10,12},{12... | collective-permute-start | bytes 393224 | tf_op jit(solution)/shard_map/ppermute | solution.py:353
  15.3 1.9 %shard_map.147 = (f32[512,128]{1,0:T(8,128)S(1)}, f32[512,128]{1,0:T(8,128)S(1)}, f32[512,128]{1,0:T(8,128)S(1)}) custom-call(bf16[128,512]{1,0:T(8,128)(2,1)S(1)} %copy-done.5, f32[512,128]{1,0:T(8,128)S(1)} %get-tuple-element.69.refs_1_, f32[512,128]{1,0:T(8,128)S(1)} %get-tuple-element.70.refs_2_, f32[512,128]{1,0:T(8,128)S(1)} %get-tuple-element.71.refs_3_, ...), custom_call_target="tpu_custom_call" | custom-call | flops 134217728 | bytes 393216 | tf_op jit(solution)/shard_map/pallas_call | solution.py:126
  18.2 1.8 %collective-permute-start.5 = (bf16[128,256]{1,0:T(8,128)(2,1)S(1)}, bf16[128,256]{1,0:T(8,128)(2,1)S(1)}, u32[]{:S(2)}, u32[]{:S(2)}) collective-permute-start(bf16[128,256]{1,0:T(8,128)(2,1)S(1)} %slice.53), channel_id=1, source_target_pairs={{0,2},{2,4},{4,6},{6,7},{7,5},{5,3},{3,1},{1,0},{8,10},{10,12},{12... | collective-permute-start | bytes 196616 | tf_op jit(solution)/shard_map/ppermute | solution.py:357
  20.3 1.9 %shard_map.148 = (f32[512,128]{1,0:T(8,128)S(1)}, f32[512,128]{1,0:T(8,128)S(1)}, f32[512,128]{1,0:T(8,128)S(1)}) custom-call(bf16[128,512]{1,0:T(8,128)(2,1)S(1)} %copy-done.6, f32[512,128]{1,0:T(8,128)S(1)} %get-tuple-element.76.refs_1_, f32[512,128]{1,0:T(8,128)S(1)} %get-tuple-element.77.refs_2_, f32[512,128]{1,0:T(8,128)S(1)} %get-tuple-element.78.refs_3_, ...), custom_call_target="tpu_custom_call" | custom-call | flops 134217728 | bytes 393216 | tf_op jit(solution)/shard_map/pallas_call | solution.py:126
  22.5 1.9 %collective-permute-done.7.refs_7_ = bf16[128,256]{1,0:T(8,128)(2,1)S(1)} collective-permute-done((bf16[128,256]{1,0:T(8,128)(2,1)S(1)}, bf16[128,256]{1,0:T(8,128)(2,1)S(1)}, u32[]{:S(2)}, u32[]{:S(2)}) %collective-permute-start.7) | collective-permute-done | bytes 65568 | tf_op jit(solution)/shard_map/ppermute | solution.py:358
  24.4 2.1 %shard_map.149 = (bf16[64,2048]{1,0:T(8,128)(2,1)S(1)}, bf16[64,2048]{1,0:T(8,128)(2,1)S(1)}) custom-call(bf16[128,512]{1,0:T(8,128)(2,1)S(1)} %copy-done.6, f32[512,128]{1,0:T(8,128)S(1)} %get-tuple-element.82.refs_1_, f32[512,128]{1,0:T(8,128)S(1)} %get-tuple-element.83.refs_2_, f32[512,128]{1,0:T(8,128)S(1)} %get-tuple-element.84.refs_3_, ...), custom_call_target="tpu_custom_call" | custom-call | flops 67108864 | bytes 262144 | tf_op jit(solution)/shard_map/pallas_call | solution.py:126
  30.6 3.6 %shard_map.150 = (bf16[704,2048]{1,0:T(8,128)(2,1)S(1)}, bf16[704,2048]{1,0:T(8,128)(2,1)S(1)}, bf16[704,2048]{1,0:T(8,128)(2,1)S(1)}) custom-call(bf16[352,2048]{1,0:T(8,128)(2,1)} %bitcast.19, bf16[352,2048]{1,0:T(8,128)(2,1)} %copy-done.14, bf16[352,2048]{1,0:T(8,128)(2,1)} %bitcast.21, bf16[352,2048]{1,0:T(8,128)(2,1)} %collective-permute-done.11.refs_3_, ...), custom_call_target="tpu_custom_call" | custom-call | bytes 8650752 | tf_op jit(solution)/shard_map/pallas_call | solution.py:158
  40.5 5.9 %shard_map.151.refs_4_ = f32[64,2048]{1,0:T(8,128)S(1)} custom-call(bf16[64,2176]{1,0:T(8,128)(2,1)S(1)} %concatenate.20.x_ref.refs_1_, bf16[352,2048]{1,0:T(8,128)(2,1)} %bitcast.12.refs_0_, bf16[352,2048]{1,0:T(8,128)(2,1)} %collective-permute-done.14.refs_1_, bf16[352,2048]{1,0:T(8,128)(2,1)} %bitcast.13.refs_2_, ...), custom_call_target="tpu_custom_call" | custom-call | flops 553648128 | bytes 8650752 | tf_op jit(solution)/shard_map/pallas_call | solution.py:202
  49.1 3.5 %shard_map.152 = (bf16[32,2048]{1,0:T(8,128)(2,1)S(1)}, bf16[32,2048]{1,0:T(8,128)(2,1)S(1)}, bf16[32,2048]{1,0:T(8,128)(2,1)S(1)}, bf16[96,2048]{1,0:T(8,128)(2,1)S(1)}) custom-call(s32[2]{0:T(128)S(1)} %pad_add_fusion.refs_0_, bf16[64,2176]{1,0:T(8,128)(2,1)S(1)} %concatenate.20.x_ref.refs_1_, bf16[64,2176]{1,0:T(8,128)(2,1)} %collective-permute-done.13.refs_2_, ...), custom_call_target="tpu_custom_call" | custom-call | flops 1660944384 | bytes 1572864 | tf_op jit(solution)/shard_map/pallas_call | solution.py:275
  56.8 3.0 %shard_map.153 = (bf16[32,2048]{1,0:T(8,128)(2,1)S(1)}, bf16[32,2048]{1,0:T(8,128)(2,1)S(1)}, bf16[64,2048]{1,0:T(8,128)(2,1)S(1)}) custom-call(s32[2]{0:T(128)S(1)} %pad_add_fusion.refs_0_, bf16[64,2176]{1,0:T(8,128)(2,1)S(1)} %collective-permute-done.19.refs_1_, bf16[64,2176]{1,0:T(8,128)(2,1)S(1)} %collective-permute-done.20.refs_2_, ...), custom_call_target="tpu_custom_call" | custom-call | flops 1107296256 | bytes 1048576 | tf_op jit(solution)/shard_map/pallas_call | solution.py:275
  60.5 4.9 %collective-permute-done.18 = bf16[96,2048]{1,0:T(8,128)(2,1)S(1)} collective-permute-done((bf16[96,2048]{1,0:T(8,128)(2,1)S(1)}, bf16[96,2048]{1,0:T(8,128)(2,1)S(1)}, u32[]{:S(2)}, u32[]{:S(2)}) %collective-permute-start.18) | collective-permute-done | bytes 393248 | tf_op jit(solution)/shard_map/ppermute | solution.py:387
  67.5 3.0 %shard_map.154 = (bf16[32,2048]{1,0:T(8,128)(2,1)S(1)}, bf16[32,2048]{1,0:T(8,128)(2,1)S(1)}, bf16[64,2048]{1,0:T(8,128)(2,1)S(1)}) custom-call(s32[2]{0:T(128)S(1)} %pad_add_fusion.refs_0_, bf16[64,2176]{1,0:T(8,128)(2,1)S(1)} %collective-permute-done.22.refs_1_, bf16[64,2176]{1,0:T(8,128)(2,1)S(1)} %collective-permute-done.23.refs_2_, ...), custom_call_target="tpu_custom_call" | custom-call | flops 1107296256 | bytes 1048576 | tf_op jit(solution)/shard_map/pallas_call | solution.py:275
  72.1 2.9 %shard_map.155 = (bf16[32,2048]{1,0:T(8,128)(2,1)S(1)}, bf16[32,2048]{1,0:T(8,128)(2,1)S(1)}) custom-call(s32[2]{0:T(128)S(1)} %pad_add_fusion.refs_0_, bf16[32,2176]{1,0:T(8,128)(2,1)S(1)} %collective-permute-done.25.refs_1_, bf16[32,2176]{1,0:T(8,128)(2,1)S(1)} %collective-permute-done.26.refs_2_, bf16[704,2048]{1,0:T(8,128)(2,1)S(1)} %get-tuple-element.93.refs_5_.refs_3_, ...), custom_call_target="tpu_custom_call" | custom-call | flops 553648128 | bytes 524288 | tf_op jit(solution)/shard_map/pallas_call | solution.py:275
  77.1 2.9 %collective-permute-done.27 = bf16[32,2048]{1,0:T(8,128)(2,1)S(1)} collective-permute-done((bf16[32,2048]{1,0:T(8,128)(2,1)S(1)}, bf16[32,2048]{1,0:T(8,128)(2,1)S(1)}, u32[]{:S(2)}, u32[]{:S(2)}) %collective-permute-start.27) | collective-permute-done | bytes 131104 | tf_op jit(solution)/shard_map/ppermute | solution.py:387
  80.6 2.3 %collective-permute-done.24 = bf16[64,2048]{1,0:T(8,128)(2,1)S(1)} collective-permute-done((bf16[64,2048]{1,0:T(8,128)(2,1)S(1)}, bf16[64,2048]{1,0:T(8,128)(2,1)S(1)}, u32[]{:S(2)}, u32[]{:S(2)}) %collective-permute-start.24) | collective-permute-done | bytes 262176 | tf_op jit(solution)/shard_map/ppermute | solution.py:387
  82.9 1.6 %collective-permute-start.28 = (bf16[16,2048]{1,0:T(8,128)(2,1)S(1)}, bf16[16,2048]{1,0:T(8,128)(2,1)S(1)}, u32[]{:S(2)}, u32[]{:S(2)}) collective-permute-start(bf16[16,2048]{1,0:T(8,128)(2,1)S(1)} %get-tuple-element.123), channel_id=1, source_target_pairs={{0,2},{2,4},{4,6},{6,7},{7,5},{5,3},{3,1},{1,0},{8,10},{10,12},{12... | collective-permute-start | bytes 196616 | tf_op jit(solution)/shard_map/ppermute | solution.py:415
  85.1 2.7 %collective-permute-done.28 = bf16[16,2048]{1,0:T(8,128)(2,1)S(1)} collective-permute-done((bf16[16,2048]{1,0:T(8,128)(2,1)S(1)}, bf16[16,2048]{1,0:T(8,128)(2,1)S(1)}, u32[]{:S(2)}, u32[]{:S(2)}) %collective-permute-start.28) | collective-permute-done | bytes 65568 | tf_op jit(solution)/shard_map/ppermute | solution.py:415
  89.8 4.4 %collective-permute-done.29 = bf16[32,2048]{1,0:T(8,128)(2,1)S(1)} collective-permute-done((bf16[32,2048]{1,0:T(8,128)(2,1)S(1)}, bf16[32,2048]{1,0:T(8,128)(2,1)S(1)}, u32[]{:S(2)}, u32[]{:S(2)}) %collective-permute-start.29) | collective-permute-done | bytes 131104 | tf_op jit(solution)/shard_map/ppermute | solution.py:424
  96.4 2.9 %collective-permute-done.30 = bf16[32,2048]{1,0:T(8,128)(2,1)S(1)} collective-permute-done((bf16[32,2048]{1,0:T(8,128)(2,1)S(1)}, bf16[32,2048]{1,0:T(8,128)(2,1)S(1)}, u32[]{:S(2)}, u32[]{:S(2)}) %collective-permute-start.30) | collective-permute-done | bytes 131104 | tf_op jit(solution)/shard_map/ppermute | solution.py:424
  103.1 2.9 %collective-permute-done.31 = bf16[32,2048]{1,0:T(8,128)(2,1)S(1)} collective-permute-done((bf16[32,2048]{1,0:T(8,128)(2,1)S(1)}, bf16[32,2048]{1,0:T(8,128)(2,1)S(1)}, u32[]{:S(2)}, u32[]{:S(2)}) %collective-permute-start.31) | collective-permute-done | bytes 131104 | tf_op jit(solution)/shard_map/ppermute | solution.py:424
  109.3 3.7 %collective-permute-done.36 = bf16[32,2048]{1,0:T(8,128)(2,1)S(1)} collective-permute-done((bf16[32,2048]{1,0:T(8,128)(2,1)S(1)}, bf16[32,2048]{1,0:T(8,128)(2,1)S(1)}, u32[]{:S(2)}, u32[]{:S(2)}) %collective-permute-start.36) | collective-permute-done | bytes 131104 | tf_op jit(solution)/shard_map/ppermute | solution.py:436
  (137 shorter events, 46.7 us)
Async XLA Ops:
  0.0 28.3 %collective-permute-start.10 = (bf16[352,2048]{1,0:T(8,128)(2,1)}, bf16[352,2048]{1,0:T(8,128)(2,1)S(1)}, u32[]{:S(2)}, u32[]{:S(2)}) collective-permute-start(bf16[352,2048]{1,0:T(8,128)(2,1)} %bitcast.18), channel_id=1, source_target_pairs={{0,8},{8,0},{16,24},{24,16},{1,9},{9,1},{17,25},{25,17},{2,10},{10... | collective-permute-start | bytes 4325384 | tf_op jit(solution)/shard_map/ppermute | solution.py:342
  0.5 28.3 %collective-permute-start.11 = (bf16[352,2048]{1,0:T(8,128)(2,1)}, bf16[352,2048]{1,0:T(8,128)(2,1)}, u32[]{:S(2)}, u32[]{:S(2)}) collective-permute-start(bf16[352,2048]{1,0:T(8,128)(2,1)} %bitcast.20), channel_id=1, source_target_pairs={{0,8},{8,0},{16,24},{24,16},{1,9},{9,1},{17,25},{25,17},{2,10},{10... | collective-permute-start | bytes 4325384 | tf_op jit(solution)/shard_map/ppermute | solution.py:342
  0.5 7.5 %collective-permute-start = (bf16[256,256]{1,0:T(8,128)(2,1)}, bf16[256,256]{1,0:T(8,128)(2,1)S(1)}, u32[]{:S(2)}, u32[]{:S(2)}) collective-permute-start(bf16[256,256]{1,0:T(8,128)(2,1)} %bitcast.14), channel_id=1, source_target_pairs={{0,2},{2,4},{4,6},{6,7},{7,5},{5,3},{3,1},{1,0},{8,10},{10,12},{12... | collective-permute-start | bytes 393224 | tf_op jit(solution)/shard_map/ppermute | solution.py:353
  3.5 6.5 %collective-permute-start.2 = (bf16[256,256]{1,0:T(8,128)(2,1)}, bf16[256,256]{1,0:T(8,128)(2,1)S(1)}, u32[]{:S(2)}, u32[]{:S(2)}) collective-permute-start(bf16[256,256]{1,0:T(8,128)(2,1)} %bitcast.15), channel_id=1, source_target_pairs={{2,0},{4,2},{6,4},{7,6},{5,7},{3,5},{1,3},{0,1},{10,8},{12,10},{14... | collective-permute-start | bytes 393224 | tf_op jit(solution)/shard_map/ppermute | solution.py:354
  8.0 5.2 %collective-permute-start.1 = (bf16[256,256]{1,0:T(8,128)(2,1)S(1)}, bf16[256,256]{1,0:T(8,128)(2,1)S(1)}, u32[]{:S(2)}, u32[]{:S(2)}) collective-permute-start(bf16[256,256]{1,0:T(8,128)(2,1)S(1)} %collective-permute-done.refs_4_), channel_id=1, source_target_pairs={{0,2},{2,4},{4,6},{6,7},{7,5},{5,3},{3,1},{1,0},{8,10},{10,12},{12... | collective-permute-start | bytes 393224 | tf_op jit(solution)/shard_map/ppermute | solution.py:353
  15.3 15.3 %collective-permute-start.12 = (bf16[352,2048]{1,0:T(8,128)(2,1)}, bf16[352,2048]{1,0:T(8,128)(2,1)}, u32[]{:S(2)}, u32[]{:S(2)}) collective-permute-start(bf16[352,2048]{1,0:T(8,128)(2,1)} %bitcast.22), channel_id=1, source_target_pairs={{0,8},{8,0},{16,24},{24,16},{1,9},{9,1},{17,25},{25,17},{2,10},{10... | collective-permute-start | bytes 4325384 | tf_op jit(solution)/shard_map/ppermute | solution.py:342
  22.5 18.0 %collective-permute-start.14 = (bf16[352,2048]{1,0:T(8,128)(2,1)}, bf16[352,2048]{1,0:T(8,128)(2,1)}, u32[]{:S(2)}, u32[]{:S(2)}) collective-permute-start(bf16[352,2048]{1,0:T(8,128)(2,1)} %bitcast.12.refs_0_), channel_id=1, source_target_pairs={{0,8},{8,0},{16,24},{24,16},{1,9},{9,1},{17,25},{25,17},{2,10},{10... | collective-permute-start | bytes 4325384 | tf_op jit(solution)/shard_map/ppermute | solution.py:342
  28.1 12.4 %collective-permute-start.15 = (bf16[352,2048]{1,0:T(8,128)(2,1)}, bf16[352,2048]{1,0:T(8,128)(2,1)}, u32[]{:S(2)}, u32[]{:S(2)}) collective-permute-start(bf16[352,2048]{1,0:T(8,128)(2,1)} %bitcast.13.refs_2_), channel_id=1, source_target_pairs={{0,8},{8,0},{16,24},{24,16},{1,9},{9,1},{17,25},{25,17},{2,10},{10... | collective-permute-start | bytes 4325384 | tf_op jit(solution)/shard_map/ppermute | solution.py:342
  28.3 12.2 %collective-permute-start.16 = (bf16[352,2048]{1,0:T(8,128)(2,1)}, bf16[352,2048]{1,0:T(8,128)(2,1)}, u32[]{:S(2)}, u32[]{:S(2)}) collective-permute-start(bf16[352,2048]{1,0:T(8,128)(2,1)} %refs_4_.1), channel_id=1, source_target_pairs={{0,8},{8,0},{16,24},{24,16},{1,9},{9,1},{17,25},{25,17},{2,10},{10... | collective-permute-start | bytes 4325384 | tf_op jit(solution)/shard_map/ppermute | solution.py:342
  28.8 8.6 %collective-permute-start.9 = (bf16[64,2048]{1,0:T(8,128)(2,1)S(1)}, bf16[64,2048]{1,0:T(8,128)(2,1)S(1)}, u32[]{:S(2)}, u32[]{:S(2)}) collective-permute-start(bf16[64,2048]{1,0:T(8,128)(2,1)S(1)} %add_convert_fusion.1), channel_id=1, source_target_pairs={{0,16},{8,24},{16,0},{24,8},{1,17},{9,25},{17,1},{25,9},{2,18},{10... | collective-permute-start | bytes 786440 | tf_op jit(solution)/shard_map/ppermute | solution.py:366
  38.4 8.6 %collective-permute-start.13 = (bf16[64,2176]{1,0:T(8,128)(2,1)S(1)}, bf16[64,2176]{1,0:T(8,128)(2,1)}, u32[]{:S(2)}, u32[]{:S(2)}) collective-permute-start(bf16[64,2176]{1,0:T(8,128)(2,1)S(1)} %concatenate.20.x_ref.refs_1_), channel_id=1, source_target_pairs={{0,2},{2,4},{4,6},{6,7},{7,5},{5,3},{3,1},{1,0},{8,10},{10,12},{12... | collective-permute-start | bytes 835592 | tf_op jit(solution)/shard_map/ppermute | solution.py:396
  40.0 8.5 %collective-permute-start.17 = (bf16[64,2176]{1,0:T(8,128)(2,1)S(1)}, bf16[64,2176]{1,0:T(8,128)(2,1)S(1)}, u32[]{:S(2)}, u32[]{:S(2)}) collective-permute-start(bf16[64,2176]{1,0:T(8,128)(2,1)S(1)} %concatenate.20.x_ref.refs_1_), channel_id=1, source_target_pairs={{2,0},{4,2},{6,4},{7,6},{5,7},{3,5},{1,3},{0,1},{10,8},{12,10},{14... | collective-permute-start | bytes 835592 | tf_op jit(solution)/shard_map/ppermute | solution.py:397
  47.0 7.8 %collective-permute-start.19 = (bf16[64,2176]{1,0:T(8,128)(2,1)}, bf16[64,2176]{1,0:T(8,128)(2,1)S(1)}, u32[]{:S(2)}, u32[]{:S(2)}) collective-permute-start(bf16[64,2176]{1,0:T(8,128)(2,1)} %collective-permute-done.13.refs_2_), channel_id=1, source_target_pairs={{0,2},{2,4},{4,6},{6,7},{7,5},{5,3},{3,1},{1,0},{8,10},{10,12},{12... | collective-permute-start | bytes 835592 | tf_op jit(solution)/shard_map/ppermute | solution.py:396
  48.6 7.8 %collective-permute-start.20 = (bf16[64,2176]{1,0:T(8,128)(2,1)S(1)}, bf16[64,2176]{1,0:T(8,128)(2,1)S(1)}, u32[]{:S(2)}, u32[]{:S(2)}) collective-permute-start(bf16[64,2176]{1,0:T(8,128)(2,1)S(1)} %collective-permute-done.17.refs_3_), channel_id=1, source_target_pairs={{2,0},{4,2},{6,4},{7,6},{5,7},{3,5},{1,3},{0,1},{10,8},{12,10},{14... | collective-permute-start | bytes 835592 | tf_op jit(solution)/shard_map/ppermute | solution.py:397
  53.3 12.1 %collective-permute-start.18 = (bf16[96,2048]{1,0:T(8,128)(2,1)S(1)}, bf16[96,2048]{1,0:T(8,128)(2,1)S(1)}, u32[]{:S(2)}, u32[]{:S(2)}) collective-permute-start(bf16[96,2048]{1,0:T(8,128)(2,1)S(1)} %get-tuple-element.97), channel_id=1, source_target_pairs={{0,16},{8,24},{16,0},{24,8},{1,17},{9,25},{17,1},{25,9},{2,18},{10... | collective-permute-start | bytes 1179656 | tf_op jit(solution)/shard_map/ppermute | solution.py:387
  54.7 10.6 %collective-permute-start.22 = (bf16[64,2176]{1,0:T(8,128)(2,1)S(1)}, bf16[64,2176]{1,0:T(8,128)(2,1)S(1)}, u32[]{:S(2)}, u32[]{:S(2)}) collective-permute-start(bf16[64,2176]{1,0:T(8,128)(2,1)S(1)} %collective-permute-done.19.refs_1_), channel_id=1, source_target_pairs={{0,2},{2,4},{4,6},{6,7},{7,5},{5,3},{3,1},{1,0},{8,10},{10,12},{12... | collective-permute-start | bytes 835592 | tf_op jit(solution)/shard_map/ppermute | solution.py:396
  56.3 10.7 %collective-permute-start.23 = (bf16[64,2176]{1,0:T(8,128)(2,1)S(1)}, bf16[64,2176]{1,0:T(8,128)(2,1)S(1)}, u32[]{:S(2)}, u32[]{:S(2)}) collective-permute-start(bf16[64,2176]{1,0:T(8,128)(2,1)S(1)} %collective-permute-done.20.refs_2_), channel_id=1, source_target_pairs={{2,0},{4,2},{6,4},{7,6},{5,7},{3,5},{1,3},{0,1},{10,8},{12,10},{14... | collective-permute-start | bytes 835592 | tf_op jit(solution)/shard_map/ppermute | solution.py:397
  59.8 10.7 %collective-permute-start.21 = (bf16[64,2048]{1,0:T(8,128)(2,1)S(1)}, bf16[64,2048]{1,0:T(8,128)(2,1)S(1)}, u32[]{:S(2)}, u32[]{:S(2)}) collective-permute-start(bf16[64,2048]{1,0:T(8,128)(2,1)S(1)} %get-tuple-element.102), channel_id=1, source_target_pairs={{0,16},{8,24},{16,0},{24,8},{1,17},{9,25},{17,1},{25,9},{2,18},{10... | collective-permute-start | bytes 786440 | tf_op jit(solution)/shard_map/ppermute | solution.py:387
  65.3 5.1 %collective-permute-start.25 = (bf16[32,2176]{1,0:T(8,128)(2,1)S(1)}, bf16[32,2176]{1,0:T(8,128)(2,1)S(1)}, u32[]{:S(2)}, u32[]{:S(2)}) collective-permute-start(bf16[32,2176]{1,0:T(8,128)(2,1)S(1)} %slice.60), channel_id=1, source_target_pairs={{0,2},{2,4},{4,6},{6,7},{7,5},{5,3},{3,1},{1,0},{8,10},{10,12},{12... | collective-permute-start | bytes 417800 | tf_op jit(solution)/shard_map/ppermute | solution.py:405
  67.0 5.1 %collective-permute-start.26 = (bf16[32,2176]{1,0:T(8,128)(2,1)S(1)}, bf16[32,2176]{1,0:T(8,128)(2,1)S(1)}, u32[]{:S(2)}, u32[]{:S(2)}) collective-permute-start(bf16[32,2176]{1,0:T(8,128)(2,1)S(1)} %slice.76), channel_id=1, source_target_pairs={{2,0},{4,2},{6,4},{7,6},{5,7},{3,5},{1,3},{0,1},{10,8},{12,10},{14... | collective-permute-start | bytes 417800 | tf_op jit(solution)/shard_map/ppermute | solution.py:406
  75.0 5.0 %collective-permute-start.27 = (bf16[32,2048]{1,0:T(8,128)(2,1)S(1)}, bf16[32,2048]{1,0:T(8,128)(2,1)S(1)}, u32[]{:S(2)}, u32[]{:S(2)}) collective-permute-start(bf16[32,2048]{1,0:T(8,128)(2,1)S(1)} %get-tuple-element.110), channel_id=1, source_target_pairs={{0,16},{8,24},{16,0},{24,8},{1,17},{9,25},{17,1},{25,9},{2,18},{10... | collective-permute-start | bytes 393224 | tf_op jit(solution)/shard_map/ppermute | solution.py:387
  75.8 7.0 %collective-permute-start.24 = (bf16[64,2048]{1,0:T(8,128)(2,1)S(1)}, bf16[64,2048]{1,0:T(8,128)(2,1)S(1)}, u32[]{:S(2)}, u32[]{:S(2)}) collective-permute-start(bf16[64,2048]{1,0:T(8,128)(2,1)S(1)} %get-tuple-element.106), channel_id=1, source_target_pairs={{0,16},{8,24},{16,0},{24,8},{1,17},{9,25},{17,1},{25,9},{2,18},{10... | collective-permute-start | bytes 786440 | tf_op jit(solution)/shard_map/ppermute | solution.py:387
  84.6 5.2 %collective-permute-start.33 = (bf16[32,2048]{1,0:T(8,128)(2,1)S(1)}, bf16[32,2048]{1,0:T(8,128)(2,1)S(1)}, u32[]{:S(2)}, u32[]{:S(2)}) collective-permute-start(bf16[32,2048]{1,0:T(8,128)(2,1)S(1)} %pad_maximum_fusion.3), channel_id=1, source_target_pairs={{2,0},{4,2},{6,4},{7,6},{5,7},{3,5},{1,3},{0,1},{10,8},{12,10},{14... | collective-permute-start | bytes 393224 | tf_op jit(solution)/shard_map/ppermute | solution.py:425
  87.8 6.4 %collective-permute-start.29 = (bf16[32,2048]{1,0:T(8,128)(2,1)S(1)}, bf16[32,2048]{1,0:T(8,128)(2,1)S(1)}, u32[]{:S(2)}, u32[]{:S(2)}) collective-permute-start(bf16[32,2048]{1,0:T(8,128)(2,1)S(1)} %pad_maximum_fusion.2), channel_id=1, source_target_pairs={{0,2},{2,4},{4,6},{6,7},{7,5},{5,3},{3,1},{1,0},{8,10},{10,12},{12... | collective-permute-start | bytes 393224 | tf_op jit(solution)/shard_map/ppermute | solution.py:424
  (33 other events, 223.9 us)

commit v3 on v2

--- a/solution.py
+++ b/solution.py
@@ -16,13 +16,11 @@
 f32 = jnp.float32
 bf16 = jnp.bfloat16
 STAGE_VMEM = 1 << 20
-SHARED_VMEM = 8 << 20
-EXPERT_VMEM = 5 << 20
+SHARED_VMEM = 5 << 20
+EXPERT_VMEM = 4 << 20
 COLUMNS = 512
-
-
-def dot(a, b):
-    return jnp.dot(a, b, preferred_element_type=f32)
+SLOTS = 6
+EFFORT = 50
 
 
 def expert_capacity(tokens_here, experts):
@@ -138,15 +136,59 @@
     )(*args)
 
 
+def in_vmem(arrays):
+    return [pltpu.with_memory_space_constraint(a, pltpu.VMEM) for a in arrays]
+
+
+def in_hbm(arrays):
+    return [pltpu.with_memory_space_constraint(a, pltpu.HBM) for a in arrays]
+
+
+def norm_kernel(
+    plane_ref, here_ref, there_ref, residual_ref, gain_ref, gates_ref, hidden_ref, out_ref
+):
+    width = hidden_ref.shape[1]
+    attn_out = here_ref[...].astype(f32) + there_ref[...].astype(f32)
+    hidden = (residual_ref[...].astype(f32) + attn_out).astype(bf16)
+    part = hidden_ref.shape[0]
+    hidden_ref[...] = jnp.where(plane_ref[0] == 1, hidden[part:], hidden[:part])
+    hidden = hidden.astype(f32)
+    mean_square = jnp.mean(hidden * hidden, axis=-1, keepdims=True)
+    normed = hidden * lax.rsqrt(mean_square + norm_eps) * gain_ref[...].astype(f32)
+    out_ref[:, :width] = normed.astype(bf16)
+    out_ref[:, width:] = gates_ref[...]
+
+
+def norm(plane, here, there, residual, gain, gates):
+    rows, width = here.shape
+    vmem = pl.BlockSpec(memory_space=pltpu.VMEM)
+    return pl.pallas_call(
+        norm_kernel,
+        out_shape=[
+            jax.ShapeDtypeStruct((rows // 2, width), bf16),
+            jax.ShapeDtypeStruct((rows, width + gates.shape[1]), bf16),
+        ],
+        in_specs=[pl.BlockSpec(memory_space=pltpu.SMEM)] + [vmem] * 5,
+        out_specs=[vmem] * 2,
+        compiler_params=pltpu.CompilerParams(vmem_limit_bytes=2 << 20),
+        cost_estimate=pl.CostEstimate(
+            flops=8 * rows * width, bytes_accessed=10 * rows * width, transcendentals=rows
+        ),
+    )(plane, here, there, residual, gain.reshape(1, width), gates)
+
+
+def joining(sources, outs, sems):
+    block = sources[0].shape[0]
+    return [
+        pltpu.make_async_copy(
+            source, outs[i // 2].at[pl.ds(i % 2 * block, block)], sems.at[i]
+        )
+        for i, source in enumerate(sources)
+    ]
+
+
 def stage_kernel(*refs):
-    sources, outs, sems = refs[:6], refs[6:9], refs[9]
-    block = sources[0].shape[0]
-    copies = [
-        pltpu.make_async_copy(
-            sources[i], outs[i // 2].at[pl.ds(i % 2 * block, block)], sems.at[i]
-        )
-        for i in range(6)
-    ]
+    copies = joining(refs[:4], refs[4:6], refs[6])
     for copy in copies:
         copy.start()
     for copy in copies:
@@ -157,93 +199,100 @@
     block, width = weights[0].shape
     return pl.pallas_call(
         stage_kernel,
-        out_shape=[pltpu.VMEM((2 * block, width), bf16)] * 3,
-        in_specs=[pl.BlockSpec(memory_space=pl.ANY)] * 6,
-        out_specs=[pl.BlockSpec(memory_space=pltpu.VMEM)] * 3,
-        scratch_shapes=[pltpu.SemaphoreType.DMA((6,))],
+        out_shape=[pltpu.VMEM((2 * block, width), bf16)] * 2,
+        in_specs=[pl.BlockSpec(memory_space=pl.ANY)] * 4,
+        out_specs=[pl.BlockSpec(memory_space=pltpu.VMEM)] * 2,
+        scratch_shapes=[pltpu.SemaphoreType.DMA((4,))],
         compiler_params=pltpu.CompilerParams(vmem_limit_bytes=STAGE_VMEM),
         cost_estimate=pl.CostEstimate(
-            flops=0, bytes_accessed=12 * block * width, transcendentals=0
+            flops=0, bytes_accessed=8 * block * width, transcendentals=0
         ),
-    )(*[pltpu.with_memory_space_constraint(w, pltpu.HBM) for w in weights])
-
-
-def fetches(sources, bufs, sems):
-    block = sources[0].shape[0]
-    return [
-        pltpu.make_async_copy(
-            sources[i], bufs[i // 2 % 2].at[pl.ds(i % 2 * block, block)], sems.at[i]
+    )(*in_hbm(weights))
+
+
+def hidden_units(x, gate_weights, up_weights):
+    contract = (((1,), (1,)), ((), ()))
+    gate = lax.dot_general(x, gate_weights, contract, preferred_element_type=f32)
+    up = lax.dot_general(x, up_weights, contract, preferred_element_type=f32)
+    return (gate / (1.0 + jnp.exp(-gate)) * up).astype(bf16)
+
+
+def shared_kernel(count, *refs):
+    rows, sources = refs[:count], refs[count : count + 6]
+    out_ref, buf, sems = refs[-3:]
+    block, width = sources[0].shape
+    slots, units = buf.shape[:2]
+    pieces = 2 * block // units
+
+    def fetch(k):
+        core, row = divmod(k // 3 * units, block)
+        return pltpu.make_async_copy(
+            sources[2 * (k % 3) + core].at[pl.ds(row, units)], buf.at[k % slots], sems.at[k % slots]
         )
-        for i in range(6)
-    ]
-
-
-def hidden_units(x, copies, bufs):
-    contract = (((1,), (1,)), ((), ()))
-    for copy in copies[:4]:
-        copy.start()
-    for copy in copies[:2]:
-        copy.wait()
-    gate = lax.dot_general(x, bufs[0][...], contract, preferred_element_type=f32)
-    for copy in copies[4:]:
-        copy.start()
-    for copy in copies[2:4]:
-        copy.wait()
-    up = lax.dot_general(x, bufs[1][...], contract, preferred_element_type=f32)
-    hidden = (gate / (1.0 + jnp.exp(-gate)) * up).astype(bf16)
-    for copy in copies[4:]:
-        copy.wait()
-    return hidden
-
-
-def glu_call(kernel, args, specs, weights, outs, rows):
+
+    def free(k):
+        if k + slots < 3 * pieces:
+            fetch(k + slots).start()
+
+    for k in range(slots):
+        fetch(k).start()
+    x = jnp.concatenate([ref[:, :width] for ref in rows], axis=0)
+    for piece in range(pieces):
+        k = 3 * piece
+        fetch(k).wait()
+        fetch(k + 1).wait()
+        hidden = hidden_units(x, buf[k % slots], buf[(k + 1) % slots])
+        free(k)
+        free(k + 1)
+        fetch(k + 2).wait()
+        for c in range(0, width, COLUMNS):
+            cols = slice(c, c + COLUMNS)
+            out = jnp.dot(hidden, buf[(k + 2) % slots, :, cols], preferred_element_type=f32)
+            out_ref[:, cols] = out if piece == 0 else out_ref[:, cols] + out
+        free(k + 2)
+
+
+def shared_expert(rows, weights):
     block, width = weights[0].shape
+    units = block // 2
+    count = sum(a.shape[0] for a in rows)
     vmem = pl.BlockSpec(memory_space=pltpu.VMEM)
     return pl.pallas_call(
-        kernel,
-        out_shape=outs,
-        in_specs=specs + [pl.BlockSpec(memory_space=pl.ANY)] * 6,
-        out_specs=[vmem] * len(outs),
-        scratch_shapes=[pltpu.VMEM((2 * block, width), bf16)] * 2
-        + [pltpu.SemaphoreType.DMA((6,))],
+        functools.partial(shared_kernel, len(rows)),
+        out_shape=jax.ShapeDtypeStruct((count, width), f32),
+        in_specs=[vmem] * len(rows) + [pl.BlockSpec(memory_space=pl.ANY)] * 6,
+        out_specs=vmem,
+        scratch_shapes=[
+            pltpu.VMEM((SLOTS, units, width), bf16),
+            pltpu.SemaphoreType.DMA((SLOTS,)),
+        ],
         compiler_params=pltpu.CompilerParams(vmem_limit_bytes=SHARED_VMEM),
         cost_estimate=pl.CostEstimate(
-            flops=12 * rows * width * block,
+            flops=12 * count * width * block,
             bytes_accessed=12 * block * width,
-            transcendentals=2 * rows * block,
+            transcendentals=2 * count * block,
         ),
-    )(*args, *[pltpu.with_memory_space_constraint(w, pltpu.HBM) for w in weights])
-
-
-def shared_kernel(x_ref, *refs):
-    sources, out_ref, bufs, sems = refs[:6], refs[6], refs[7:9], refs[9]
-    width = out_ref.shape[1]
-    hidden = hidden_units(x_ref[:, :width], fetches(sources, bufs, sems), bufs)
-    for c in range(0, width, COLUMNS):
-        cols = slice(c, c + COLUMNS)
-        out_ref[:, cols] = jnp.dot(hidden, bufs[0][:, cols], preferred_element_type=f32)
-
-
-def shared_expert(rows, weights):
-    width = weights[0].shape[1]
-    outs = [jax.ShapeDtypeStruct((rows.shape[0], width), f32)]
-    specs = [pl.BlockSpec(memory_space=pltpu.VMEM)]
-    return glu_call(shared_kernel, [rows], specs, weights, outs, rows.shape[0])[0]
-
-
-def expert_kernel(n_experts, counts, plus, *refs):
+    )(*rows, *in_hbm(weights))
+
+
+def expert_kernel(n_experts, counts, plus, staging, *refs):
     refs = list(refs)
     place_ref = refs.pop(0)
     sources = [refs.pop(0) for _ in range(sum(counts))]
     shared_ref = refs.pop(0) if plus else None
-    gate_ref, up_ref, down_ref = refs[:3]
-    keeps, send_ref = refs[3:-1], refs[-1]
+    gate_ref, up_ref = refs[:2]
+    if staging:
+        down_ref, sems = refs[-2:]
+        copies = joining(refs[2:4], [down_ref], sems)
+        for copy in copies:
+            copy.start()
+        keeps, send_ref = refs[4:-3], refs[-3]
+    else:
+        down_ref = refs[2]
+        keeps, send_ref = refs[3:-1], refs[-1]
     width = send_ref.shape[1]
     x = jnp.concatenate([ref[:, :width] for ref in sources], axis=0)
-    contract = (((1,), (1,)), ((), ()))
-    gate = lax.dot_general(x, gate_ref[...], contract, preferred_element_type=f32)
-    up = lax.dot_general(x, up_ref[...], contract, preferred_element_type=f32)
-    hidden = (gate / (1.0 + jnp.exp(-gate)) * up).astype(bf16)
+    hidden = hidden_units(x, gate_ref[...], up_ref[...])
     lanes = jnp.concatenate([ref[:, width:] for ref in sources], axis=0).astype(f32)
     lane = lax.broadcasted_iota(jnp.int32, lanes.shape, 1)
     e, second = place_ref[0], place_ref[1] == 1
@@ -251,6 +300,9 @@
         jnp.where((lane == e) | (lane == e + n_experts), lanes, 0.0), axis=1, keepdims=True
     )
     part = keeps[0].shape[0]
+    if staging:
+        for copy in copies:
+            copy.wait()
     for c in range(0, width, COLUMNS):
         cols = slice(c, c + COLUMNS)
         out = jnp.dot(hidden, down_ref[:, cols], preferred_element_type=f32) * scale
@@ -270,22 +322,36 @@
     rows = sum(a.shape[0] for b in blocks for a in b)
     part = rows // len(blocks) // 2
     hidden, width = weights[0].shape
+    staging = len(weights) == 4
     vmem, smem = pl.BlockSpec(memory_space=pltpu.VMEM), pl.BlockSpec(memory_space=pltpu.SMEM)
     args = [place] + [a for b in blocks for a in b] + ([] if shared is None else [shared])
+    specs = [smem] + [vmem] * (len(args) + 1)
+    outs = [jax.ShapeDtypeStruct((part, width), bf16)] * len(blocks)
+    outs.append(jax.ShapeDtypeStruct((part * len(blocks), width), bf16))
+    if staging:
+        args += in_vmem(weights[:2]) + in_hbm(weights[2:])
+        specs += [pl.BlockSpec(memory_space=pl.ANY)] * 2
+        outs.append(pltpu.VMEM((hidden, width), bf16))
+    else:
+        args += in_vmem(weights)
+        specs += [vmem]
     outs = pl.pallas_call(
-        functools.partial(expert_kernel, n_experts, counts, shared is not None),
-        out_shape=[jax.ShapeDtypeStruct((part, width), bf16)] * len(blocks)
-        + [jax.ShapeDtypeStruct((part * len(blocks), width), bf16)],
-        in_specs=[smem] + [vmem] * (len(args) - 1 + 3),
-        out_specs=[vmem] * (len(blocks) + 1),
+        functools.partial(expert_kernel, n_experts, counts, shared is not None, staging),
+        out_shape=outs,
+        in_specs=specs,
+        out_specs=[vmem] * len(outs),
+        scratch_shapes=[pltpu.SemaphoreType.DMA((2,))] if staging else [],
         compiler_params=pltpu.CompilerParams(vmem_limit_bytes=EXPERT_VMEM),
         cost_estimate=pl.CostEstimate(
-            flops=6 * rows * width * hidden,
+            flops=EFFORT * 6 * rows * width * hidden,
             bytes_accessed=4 * rows * width,
             transcendentals=rows * hidden,
         ),
-    )(*args, *[pltpu.with_memory_space_constraint(w, pltpu.VMEM) for w in weights])
-    return outs[:-1], outs[-1]
+    )(*args)
+    if staging:
+        weights = [weights[0], weights[1], outs[-1]]
+        outs = outs[:-1]
+    return outs[:-1], outs[-1], weights
 
 
 def on_device_ring(
@@ -363,69 +429,73 @@
 
     other = lax.ppermute(send, "req", sibling)
     terms = (keep.astype(f32) + other.astype(f32)).astype(bf16)
+    quarter = half // 2
     terms_across = lax.ppermute(terms, "req", across)
-    terms_across, staged = lax.optimization_barrier((terms_across, stage(expert_weights)))
-    hidden_state = (
-        half_of(residual).astype(f32) + (terms.astype(f32) + terms_across.astype(f32))
-    ).astype(bf16)
-    hidden_float = hidden_state.astype(f32)
-    mean_square = jnp.mean(hidden_float * hidden_float, axis=-1, keepdims=True)
-    normed = (
-        hidden_float * lax.rsqrt(mean_square + norm_eps) * norm_gain.astype(f32)
-    ).astype(bf16)
-
-    normed = jnp.concatenate([normed, gates], axis=1)
+    terms_across, staged = lax.optimization_barrier((terms_across, stage(expert_weights[:4])))
+    staged = list(staged) + expert_weights[4:]
+    hidden_here, normed = norm(
+        plane.reshape(1), terms, terms_across, half_of(residual), norm_gain, gates
+    )
     place = jnp.stack([me, plane]).astype(jnp.int32)
 
     own, summand = {}, {}
-    quarter = half // 2
 
     def work(blocks, shared=None):
-        keeps, send = expert([b for _, b in blocks], staged, n, place, shared)
+        nonlocal staged
+        keeps, send, staged = expert([b for _, b in blocks], staged, n, place, shared)
+        got = lax.ppermute(send, "req", across)
         for (d, _), keep in zip(blocks, keeps):
             own[d] = keep
-        got = lax.ppermute(send, "req", across)
-        for i, (d, _) in enumerate(blocks):
-            summand[d] = got[i * quarter : (i + 1) * quarter]
-        return keeps, got
+        return keeps, ([d for d, _ in blocks], got)
+
+    def landed(step, *others):
+        due = [k for k in on_way if k < steps and max(k + 2, steps) == step]
+        out = lax.optimization_barrier(others + tuple(on_way[k][1] for k in due))
+        for k, got in zip(due, out[len(others) :]):
+            for i, d in enumerate(on_way[k][0]):
+                summand[d] = got[i * quarter : (i + 1) * quarter]
+        return out[: len(others)]
 
     from_left, from_right = normed, normed
-    before = shared_part = shared_expert(normed, shared_weights)
-    on_way, next_on_way = (), ()
+    before = shared_part = shared_expert([normed], shared_weights)
+    on_way = {}
     for s in range(1, steps):
         from_left = lax.ppermute(from_left, "exp", right)
         from_right = lax.ppermute(from_right, "exp", left)
-        from_left, before, on_way = lax.optimization_barrier((from_left, before, on_way))
+        from_left, before = landed(s, from_left, before)
         blocks = [(s, [from_left]), (-s, [from_right])]
-        on_way = next_on_way
-        if s == 1:
-            before, next_on_way = work([(0, [normed])] + blocks, shared_part)
-        else:
-            before, next_on_way = work(blocks)
+        before, on_way[s] = work(blocks)
     low = lax.ppermute(from_left[:quarter], "exp", right)
     high = lax.ppermute(from_right[quarter:], "exp", left)
-    low, before, on_way = lax.optimization_barrier((low, before, on_way))
-    work([(steps, [low, high])])
+    low, before = landed(steps, low, before)
+    last, on_way[steps] = work([(0, [normed]), (steps, [low, high])], shared_part)
+    (last,) = landed(steps + 1, last)
+    for i, d in enumerate(on_way[steps][0]):
+        summand[d] = on_way[steps][1][i * quarter : (i + 1) * quarter]
 
     def part(d):
         return own[d].astype(f32) + summand[d].astype(f32)
 
-    eighth = quarter // 2
-    far = part(steps).astype(bf16)
-    to_right = lax.ppermute(far[:eighth], "exp", right)
-    to_left = lax.ppermute(far[eighth:], "exp", left)
-    for k in range(steps - 1, 0, -1):
+    def along(hops):
+        return [(order[i], order[(i + hops) % n]) for i in range(n)]
+
+    total = hidden_here.astype(f32) + part(0)
+    near = steps // 2
+    arrived = []
+    for d in range(steps, near, -1):
+        for sign in (1, -1) if 2 * d != n else (1,):
+            block = d if 2 * d == n else -sign * d
+            arrived.append(lax.ppermute(part(block).astype(bf16), "exp", along(sign * d)))
+    to_right = to_left = None
+    for k in range(near, 0, -1):
         a, b = part(-k), part(k)
-        if k == steps - 1:
-            a = jnp.concatenate([a[:eighth] + to_right.astype(f32), a[eighth:]], axis=0)
-            b = jnp.concatenate([b[:eighth], b[eighth:] + to_left.astype(f32)], axis=0)
-        else:
+        if to_right is not None:
             a, b = a + to_right.astype(f32), b + to_left.astype(f32)
         to_right = lax.ppermute(a.astype(bf16), "exp", right)
         to_left = lax.ppermute(b.astype(bf16), "exp", left)
-    total = part(0) + (to_right.astype(f32) + to_left.astype(f32))
-    hidden_here = lax.dynamic_slice_in_dim(hidden_state, plane * quarter, quarter, 0)
-    mine = (hidden_here.astype(f32) + total).astype(bf16)
+    for terms_there in [to_right, to_left] + arrived:
+        total = total + terms_there.astype(f32)
+    mine = total.astype(bf16)
 
     def joined(index, here, there):
         first = index == 0

time: 116 us -> 96.8 us (0.83)
  waiting for transfers between devices: 39.9 us -> 17.5 us
  starting transfers between devices: 33.5 us -> 39.4 us
  other arithmetic: 2.85 us -> 1.63 us
  local copies, waits for them, and re-layouts: 8.27 us -> 7.05 us
    ppermute x3 -> x2, waiting for transfers between devices: 10.3 us -> 0.01 us  [on_device_ring(): to_right = lax.ppermute(a.astype(bf16), 'exp', right)]
    ppermute x4, waiting for transfers between devices: 10.1 us -> 0.89 us  [work(): got = lax.ppermute(send, 'req', across)]
    ppermute x2 -> x3, starting transfers between devices: 2.13 us -> 7.35 us  [on_device_ring(): lax.ppermute(part(block).astype(bf16), 'exp', along(sign * d))]
    ppermute x3 -> x2, starting transfers between devices: 4.32 us -> 1.84 us  [on_device_ring(): to_right = lax.ppermute(a.astype(bf16), 'exp', right)]
    ppermute x3 -> x2, waiting for transfers between devices: 2.91 us -> 0.51 us  [on_device_ring(): to_left = lax.ppermute(b.astype(bf16), 'exp', left)]
    ppermute x4, starting transfers between devices: 3.64 us -> 5.5 us  [work(): got = lax.ppermute(send, 'req', across)]
    ppermute x1, waiting for transfers between devices: 1.61 us -> 0.01 us  [on_device_ring(): high = lax.ppermute(from_right[quarter:], 'exp', left)]
    unnamed x38 -> x28, local copies, waits for them, and re-layouts: 7.68 us -> 6.48 us
  transfers between devices with their start and end apart: 38 -> 37, of which waited for: 20 -> 15; matrix products, arithmetic and copies ran while one was open for 1% -> 1% of each run, Pallas kernels for 24% -> 31%
where the time goes in v3:
time: 96.8 us; the launch traced here: 95.8 us
  starting transfers between devices  39.4 us (41%)
  Pallas kernels  29.9 us (31%)
  waiting for transfers between devices  17.5 us (18%)
  local copies, waits for them, and re-layouts  7.05 us (7%)
  other arithmetic  1.63 us (2%)
    pallas_call x4, Pallas kernels, expert(): pl.pallas_call(functools.partial(expert_kernel, n_experts, counts, shared...  11.9 us
    ppermute x6, starting transfers between devices, on_device_ring(): from_left = lax.ppermute(from_left, 'exp', right)  11.3 us
    pallas_call x5, Pallas kernels, attend(): pl.pallas_call(functools.partial(attend_kernel, heads, tokens, page_len,...  8.91 us
    ppermute x3, starting transfers between devices, on_device_ring(): lax.ppermute(part(block).astype(bf16), 'exp', along(sign * d))  7.35 us
    unnamed x28, local copies, waits for them, and re-layouts  6.48 us
    pallas_call x1, Pallas kernels, shared_expert(): pl.pallas_call(functools.partial(shared_kernel, len(rows)), out_shape=jax...  6.11 us
    ppermute x4, starting transfers between devices, work(): got = lax.ppermute(send, 'req', across)  5.5 us
    ppermute x3, waiting for transfers between devices, on_device_ring(): lax.ppermute(part(block).astype(bf16), 'exp', along(sign * d))  3.86 us
  transfers between devices with their start and end apart: 37, of which 15 were waited for; matrix products, arithmetic and copies ran while one was open for 1% of the time, Pallas kernels for 31%

profile of v3, /device:TPU:0, one launch (start us, length us, event | category | flops | bytes accessed | tf_op | source)
XLA Modules:
  0.0 95.8 jit_solution(7479069151035499445)
XLA Ops:
  0.5 2.6 %collective-permute-start = (bf16[256,256]{1,0:T(8,128)(2,1)}, bf16[256,256]{1,0:T(8,128)(2,1)S(1)}, u32[]{:S(2)}, u32[]{:S(2)}) collective-permute-start(bf16[256,256]{1,0:T(8,128)(2,1)} %bitcast.14), channel_id=1, source_target_pairs={{0,2},{2,4},{4,6},{6,7},{7,5},{5,3},{3,1},{1,0},{8,10},{10,12},{12... | collective-permute-start | bytes 393224 | tf_op jit(solution)/shard_map/ppermute | solution.py:419
  7.6 2.0 %collective-permute-start.1 = (bf16[256,256]{1,0:T(8,128)(2,1)S(1)}, bf16[256,256]{1,0:T(8,128)(2,1)S(1)}, u32[]{:S(2)}, u32[]{:S(2)}) collective-permute-start(bf16[256,256]{1,0:T(8,128)(2,1)S(1)} %collective-permute-done.refs_4_), channel_id=1, source_target_pairs={{0,2},{2,4},{4,6},{6,7},{7,5},{5,3},{3,1},{1,0},{8,10},{10,12},{12... | collective-permute-start | bytes 393224 | tf_op jit(solution)/shard_map/ppermute | solution.py:419
  9.7 1.9 %shard_map.146 = (f32[512,128]{1,0:T(8,128)S(1)}, f32[512,128]{1,0:T(8,128)S(1)}, f32[512,128]{1,0:T(8,128)S(1)}) custom-call(bf16[128,512]{1,0:T(8,128)(2,1)S(1)} %copy-done.1, f32[512,128]{1,0:T(8,128)S(1)} %get-tuple-element.66.refs_1_, f32[512,128]{1,0:T(8,128)S(1)} %get-tuple-element.67.refs_2_, f32[512,128]{1,0:T(8,128)S(1)} %get-tuple-element.68.refs_3_, ...), custom_call_target="tpu_custom_call" | custom-call | flops 134217728 | bytes 393216 | tf_op jit(solution)/shard_map/pallas_call | solution.py:124
  11.5 1.6 %collective-permute-done.1.refs_4_ = bf16[256,256]{1,0:T(8,128)(2,1)S(1)} collective-permute-done((bf16[256,256]{1,0:T(8,128)(2,1)S(1)}, bf16[256,256]{1,0:T(8,128)(2,1)S(1)}, u32[]{:S(2)}, u32[]{:S(2)}) %collective-permute-start.1) | collective-permute-done | bytes 131104 | tf_op jit(solution)/shard_map/ppermute | solution.py:419
  13.2 1.7 %collective-permute-start.3 = (bf16[256,256]{1,0:T(8,128)(2,1)S(1)}, bf16[256,256]{1,0:T(8,128)(2,1)S(1)}, u32[]{:S(2)}, u32[]{:S(2)}) collective-permute-start(bf16[256,256]{1,0:T(8,128)(2,1)S(1)} %collective-permute-done.1.refs_4_), channel_id=1, source_target_pairs={{0,2},{2,4},{4,6},{6,7},{7,5},{5,3},{3,1},{1,0},{8,10},{10,12},{12... | collective-permute-start | bytes 393224 | tf_op jit(solution)/shard_map/ppermute | solution.py:419
  15.2 1.9 %shard_map.147 = (f32[512,128]{1,0:T(8,128)S(1)}, f32[512,128]{1,0:T(8,128)S(1)}, f32[512,128]{1,0:T(8,128)S(1)}) custom-call(bf16[128,512]{1,0:T(8,128)(2,1)S(1)} %copy-done.1, f32[512,128]{1,0:T(8,128)S(1)} %get-tuple-element.73.refs_1_, f32[512,128]{1,0:T(8,128)S(1)} %get-tuple-element.74.refs_2_, f32[512,128]{1,0:T(8,128)S(1)} %get-tuple-element.75.refs_3_, ...), custom_call_target="tpu_custom_call" | custom-call | flops 134217728 | bytes 393216 | tf_op jit(solution)/shard_map/pallas_call | solution.py:124
  18.2 1.7 %collective-permute-start.5 = (bf16[128,256]{1,0:T(8,128)(2,1)S(1)}, bf16[128,256]{1,0:T(8,128)(2,1)S(1)}, u32[]{:S(2)}, u32[]{:S(2)}) collective-permute-start(bf16[128,256]{1,0:T(8,128)(2,1)S(1)} %slice.36), channel_id=1, source_target_pairs={{0,2},{2,4},{4,6},{6,7},{7,5},{5,3},{3,1},{1,0},{8,10},{10,12},{12... | collective-permute-start | bytes 196616 | tf_op jit(solution)/shard_map/ppermute | solution.py:423
  20.3 1.9 %shard_map.148 = (f32[512,128]{1,0:T(8,128)S(1)}, f32[512,128]{1,0:T(8,128)S(1)}, f32[512,128]{1,0:T(8,128)S(1)}) custom-call(bf16[128,512]{1,0:T(8,128)(2,1)S(1)} %copy-done.2, f32[512,128]{1,0:T(8,128)S(1)} %get-tuple-element.80.refs_1_, f32[512,128]{1,0:T(8,128)S(1)} %get-tuple-element.81.refs_2_, f32[512,128]{1,0:T(8,128)S(1)} %get-tuple-element.82.refs_3_, ...), custom_call_target="tpu_custom_call" | custom-call | flops 134217728 | bytes 393216 | tf_op jit(solution)/shard_map/pallas_call | solution.py:124
  24.2 2.2 %shard_map.149 = (bf16[64,2048]{1,0:T(8,128)(2,1)S(1)}, bf16[64,2048]{1,0:T(8,128)(2,1)S(1)}) custom-call(bf16[128,512]{1,0:T(8,128)(2,1)S(1)} %copy-done.2, f32[512,128]{1,0:T(8,128)S(1)} %get-tuple-element.86.refs_1_, f32[512,128]{1,0:T(8,128)S(1)} %get-tuple-element.87.refs_2_, f32[512,128]{1,0:T(8,128)S(1)} %get-tuple-element.88.refs_3_, ...), custom_call_target="tpu_custom_call" | custom-call | flops 67108864 | bytes 262144 | tf_op jit(solution)/shard_map/pallas_call | solution.py:124
  30.7 2.7 %shard_map.150 = (bf16[704,2048]{1,0:T(8,128)(2,1)S(1)}, bf16[704,2048]{1,0:T(8,128)(2,1)S(1)}) custom-call(bf16[352,2048]{1,0:T(8,128)(2,1)} %bitcast.23, bf16[352,2048]{1,0:T(8,128)(2,1)} %collective-permute-done.10.refs_1_, bf16[352,2048]{1,0:T(8,128)(2,1)} %bitcast.25, bf16[352,2048]{1,0:T(8,128)(2,1)} %collective-permute-done.11.refs_3_), custom_call_target="tpu_custom_call" | custom-call | bytes 5767168 | tf_op jit(solution)/shard_map/pallas_call | solution.py:200
  37.6 1.6 %collective-permute-start.12 = (bf16[64,2176]{1,0:T(8,128)(2,1)S(1)}, bf16[64,2176]{1,0:T(8,128)(2,1)S(1)}, u32[]{:S(2)}, u32[]{:S(2)}) collective-permute-start(bf16[64,2176]{1,0:T(8,128)(2,1)S(1)} %get-tuple-element.96.refs_0_.refs_1_), channel_id=1, source_target_pairs={{0,2},{2,4},{4,6},{6,7},{7,5},{5,3},{3,1},{1,0},{8,10},{10,12},{12... | collective-permute-start | bytes 835592 | tf_op jit(solution)/shard_map/ppermute | solution.py:463
  39.8 6.1 %shard_map.152.refs_4_ = f32[64,2048]{1,0:T(8,128)S(1)} custom-call(bf16[64,2176]{1,0:T(8,128)(2,1)S(1)} %get-tuple-element.96.refs_0_.refs_1_, bf16[352,2048]{1,0:T(8,128)(2,1)} %bitcast.18, bf16[352,2048]{1,0:T(8,128)(2,1)} %collective-permute-done.13.refs_2_, bf16[352,2048]{1,0:T(8,128)(2,1)} %bitcast.21, ...), custom_call_target="tpu_custom_call" | custom-call | flops 553648128 | bytes 8650752 | tf_op jit(solution)/shard_map/pallas_call | solution.py:260
  45.9 1.6 %collective-permute-start.16 = (bf16[64,2176]{1,0:T(8,128)(2,1)S(1)}, bf16[64,2176]{1,0:T(8,128)(2,1)S(1)}, u32[]{:S(2)}, u32[]{:S(2)}) collective-permute-start(bf16[64,2176]{1,0:T(8,128)(2,1)S(1)} %collective-permute-done.12.refs_1_), channel_id=1, source_target_pairs={{0,2},{2,4},{4,6},{6,7},{7,5},{5,3},{3,1},{1,0},{8,10},{10,12},{12... | collective-permute-start | bytes 835592 | tf_op jit(solution)/shard_map/ppermute | solution.py:463
  48.0 3.1 %shard_map.153 = (bf16[32,2048]{1,0:T(8,128)(2,1)S(1)}, bf16[32,2048]{1,0:T(8,128)(2,1)S(1)}, bf16[64,2048]{1,0:T(8,128)(2,1)S(1)}, bf16[704,2048]{1,0:T(8,128)(2,1)S(1)}) custom-call(s32[2]{0:T(128)S(1)} %pad_add_fusion.refs_0_, bf16[64,2176]{1,0:T(8,128)(2,1)S(1)} %collective-permute-done.12.refs_1_, bf16[64,2176]{1,0:T(8,128)(2,1)S(1)} %collective-permute-done.17.refs_2_, ...), custom_call_target="tpu_custom_call" | custom-call | flops 55364812800 | bytes 1048576 | tf_op jit(solution)/shard_map/pallas_call | solution.py:338
  55.3 3.0 %shard_map.154 = (bf16[32,2048]{1,0:T(8,128)(2,1)S(1)}, bf16[32,2048]{1,0:T(8,128)(2,1)S(1)}, bf16[64,2048]{1,0:T(8,128)(2,1)S(1)}) custom-call(s32[2]{0:T(128)S(1)} %pad_add_fusion.refs_0_, bf16[64,2176]{1,0:T(8,128)(2,1)S(1)} %collective-permute-done.16.refs_1_, bf16[64,2176]{1,0:T(8,128)(2,1)S(1)} %collective-permute-done.20.refs_2_, ...), custom_call_target="tpu_custom_call" | custom-call | flops 55364812800 | bytes 1048576 | tf_op jit(solution)/shard_map/pallas_call | solution.py:338
  62.4 2.9 %shard_map.155 = (bf16[32,2048]{1,0:T(8,128)(2,1)S(1)}, bf16[32,2048]{1,0:T(8,128)(2,1)S(1)}, bf16[64,2048]{1,0:T(8,128)(2,1)S(1)}) custom-call(s32[2]{0:T(128)S(1)} %pad_add_fusion.refs_0_, bf16[64,2176]{1,0:T(8,128)(2,1)S(1)} %collective-permute-done.19.refs_1_, bf16[64,2176]{1,0:T(8,128)(2,1)S(1)} %collective-permute-done.22.refs_2_, ...), custom_call_target="tpu_custom_call" | custom-call | flops 55364812800 | bytes 1048576 | tf_op jit(solution)/shard_map/pallas_call | solution.py:338
  67.0 1.6 %collective-permute-start.27 = (bf16[32,2048]{1,0:T(8,128)(2,1)S(1)}, bf16[32,2048]{1,0:T(8,128)(2,1)S(1)}, u32[]{:S(2)}, u32[]{:S(2)}) collective-permute-start(bf16[32,2048]{1,0:T(8,128)(2,1)S(1)} %get-tuple-element.125), channel_id=1, source_target_pairs={{0,2},{2,4},{4,6},{6,7},{7,5},{5,3},{3,1},{1,0},{8,10},{10,12},{12... | collective-permute-start | bytes 393224 | tf_op jit(solution)/shard_map/ppermute | solution.py:494
  69.1 3.0 %shard_map.156 = (bf16[32,2048]{1,0:T(8,128)(2,1)S(1)}, bf16[32,2048]{1,0:T(8,128)(2,1)S(1)}, bf16[64,2048]{1,0:T(8,128)(2,1)S(1)}) custom-call(s32[2]{0:T(128)S(1)} %pad_add_fusion.refs_0_, bf16[64,2176]{1,0:T(8,128)(2,1)S(1)} %get-tuple-element.96.refs_0_.refs_1_, bf16[32,2176]{1,0:T(8,128)(2,1)S(1)} %collective-permute-done.21.refs_2_, ...), custom_call_target="tpu_custom_call" | custom-call | flops 55364812800 | bytes 1048576 | tf_op jit(solution)/shard_map/pallas_call | solution.py:338
  73.8 3.6 %collective-permute-start.33 = (bf16[32,2048]{1,0:T(8,128)(2,1)S(1)}, bf16[32,2048]{1,0:T(8,128)(2,1)S(1)}, u32[]{:S(2)}, u32[]{:S(2)}) collective-permute-start(bf16[32,2048]{1,0:T(8,128)(2,1)S(1)} %get-tuple-element.127), channel_id=1, source_target_pairs={{0,6},{2,7},{4,5},{6,3},{7,1},{5,0},{3,2},{1,4},{8,14},{10,15},{12... | collective-permute-start | bytes 393224 | tf_op jit(solution)/shard_map/ppermute | solution.py:488
  78.0 1.9 %collective-permute-start.30 = (bf16[32,2048]{1,0:T(8,128)(2,1)S(1)}, bf16[32,2048]{1,0:T(8,128)(2,1)S(1)}, u32[]{:S(2)}, u32[]{:S(2)}) collective-permute-start(bf16[32,2048]{1,0:T(8,128)(2,1)S(1)} %get-tuple-element.124), channel_id=1, source_target_pairs={{2,0},{4,2},{6,4},{7,6},{5,7},{3,5},{1,3},{0,1},{10,8},{12,10},{14... | collective-permute-start | bytes 393224 | tf_op jit(solution)/shard_map/ppermute | solution.py:495
  80.0 3.5 %collective-permute-start.31 = (bf16[32,2048]{1,0:T(8,128)(2,1)S(1)}, bf16[32,2048]{1,0:T(8,128)(2,1)S(1)}, u32[]{:S(2)}, u32[]{:S(2)}) collective-permute-start(bf16[32,2048]{1,0:T(8,128)(2,1)S(1)} %add_convert_fusion.4), channel_id=1, source_target_pairs={{0,7},{2,5},{4,3},{6,1},{7,0},{5,2},{3,4},{1,6},{8,15},{10,13},{12... | collective-permute-start | bytes 393224 | tf_op jit(solution)/shard_map/ppermute | solution.py:488
  83.4 2.5 %collective-permute-done.33 = bf16[32,2048]{1,0:T(8,128)(2,1)S(1)} collective-permute-done((bf16[32,2048]{1,0:T(8,128)(2,1)S(1)}, bf16[32,2048]{1,0:T(8,128)(2,1)S(1)}, u32[]{:S(2)}, u32[]{:S(2)}) %collective-permute-start.33) | collective-permute-done | bytes 131104 | tf_op jit(solution)/shard_map/ppermute | solution.py:488
  87.9 2.3 %collective-permute-start.35 = (bf16[32,2048]{1,0:T(8,128)(2,1)S(1)}, bf16[32,2048]{1,0:T(8,128)(2,1)S(1)}, u32[]{:S(2)}, u32[]{:S(2)}) collective-permute-start(bf16[32,2048]{1,0:T(8,128)(2,1)S(1)} %add_convert_fusion.1), channel_id=1, source_target_pairs={{0,16},{8,24},{16,0},{24,8},{1,17},{9,25},{17,1},{25,9},{2,18},{10... | collective-permute-start | bytes 393224 | tf_op jit(solution)/shard_map/ppermute | solution.py:506
  90.3 2.9 %collective-permute-done.35 = bf16[32,2048]{1,0:T(8,128)(2,1)S(1)} collective-permute-done((bf16[32,2048]{1,0:T(8,128)(2,1)S(1)}, bf16[32,2048]{1,0:T(8,128)(2,1)S(1)}, u32[]{:S(2)}, u32[]{:S(2)}) %collective-permute-start.35) | collective-permute-done | bytes 131104 | tf_op jit(solution)/shard_map/ppermute | solution.py:506
  (118 shorter events, 35.6 us)
Async XLA Ops:
  0.0 28.1 %collective-permute-start.10 = (bf16[352,2048]{1,0:T(8,128)(2,1)}, bf16[352,2048]{1,0:T(8,128)(2,1)}, u32[]{:S(2)}, u32[]{:S(2)}) collective-permute-start(bf16[352,2048]{1,0:T(8,128)(2,1)} %bitcast.22), channel_id=1, source_target_pairs={{0,8},{8,0},{16,24},{24,16},{1,9},{9,1},{17,25},{25,17},{2,10},{10... | collective-permute-start | bytes 4325384 | tf_op jit(solution)/shard_map/ppermute | solution.py:408
  0.5 7.1 %collective-permute-start = (bf16[256,256]{1,0:T(8,128)(2,1)}, bf16[256,256]{1,0:T(8,128)(2,1)S(1)}, u32[]{:S(2)}, u32[]{:S(2)}) collective-permute-start(bf16[256,256]{1,0:T(8,128)(2,1)} %bitcast.14), channel_id=1, source_target_pairs={{0,2},{2,4},{4,6},{6,7},{7,5},{5,3},{3,1},{1,0},{8,10},{10,12},{12... | collective-permute-start | bytes 393224 | tf_op jit(solution)/shard_map/ppermute | solution.py:419
  15.2 13.7 %collective-permute-start.11 = (bf16[352,2048]{1,0:T(8,128)(2,1)}, bf16[352,2048]{1,0:T(8,128)(2,1)}, u32[]{:S(2)}, u32[]{:S(2)}) collective-permute-start(bf16[352,2048]{1,0:T(8,128)(2,1)} %bitcast.24), channel_id=1, source_target_pairs={{0,8},{8,0},{16,24},{24,16},{1,9},{9,1},{17,25},{25,17},{2,10},{10... | collective-permute-start | bytes 4325384 | tf_op jit(solution)/shard_map/ppermute | solution.py:408
  20.2 19.0 %collective-permute-start.13 = (bf16[352,2048]{1,0:T(8,128)(2,1)S(1)}, bf16[352,2048]{1,0:T(8,128)(2,1)}, u32[]{:S(2)}, u32[]{:S(2)}) collective-permute-start(bf16[352,2048]{1,0:T(8,128)(2,1)S(1)} %bitcast.19), channel_id=1, source_target_pairs={{0,8},{8,0},{16,24},{24,16},{1,9},{9,1},{17,25},{25,17},{2,10},{10... | collective-permute-start | bytes 4325384 | tf_op jit(solution)/shard_map/ppermute | solution.py:408
  22.4 17.4 %collective-permute-start.14 = (bf16[352,2048]{1,0:T(8,128)(2,1)}, bf16[352,2048]{1,0:T(8,128)(2,1)}, u32[]{:S(2)}, u32[]{:S(2)}) collective-permute-start(bf16[352,2048]{1,0:T(8,128)(2,1)} %bitcast.20), channel_id=1, source_target_pairs={{0,8},{8,0},{16,24},{24,16},{1,9},{9,1},{17,25},{25,17},{2,10},{10... | collective-permute-start | bytes 4325384 | tf_op jit(solution)/shard_map/ppermute | solution.py:408
  28.0 11.8 %collective-permute-start.15 = (bf16[352,2048]{1,0:T(8,128)(2,1)}, bf16[352,2048]{1,0:T(8,128)(2,1)}, u32[]{:S(2)}, u32[]{:S(2)}) collective-permute-start(bf16[352,2048]{1,0:T(8,128)(2,1)} %refs_5_.3), channel_id=1, source_target_pairs={{0,8},{8,0},{16,24},{24,16},{1,9},{9,1},{17,25},{25,17},{2,10},{10... | collective-permute-start | bytes 4325384 | tf_op jit(solution)/shard_map/ppermute | solution.py:408
  28.1 19.9 %collective-permute-start.18 = (bf16[352,2048]{1,0:T(8,128)(2,1)}, bf16[352,2048]{1,0:T(8,128)(2,1)}, u32[]{:S(2)}, u32[]{:S(2)}) collective-permute-start(bf16[352,2048]{1,0:T(8,128)(2,1)} %bitcast.13.refs_5_), channel_id=1, source_target_pairs={{0,8},{8,0},{16,24},{24,16},{1,9},{9,1},{17,25},{25,17},{2,10},{10... | collective-permute-start | bytes 4325384 | tf_op jit(solution)/shard_map/ppermute | solution.py:408
  29.0 8.4 %collective-permute-start.9 = (bf16[64,2048]{1,0:T(8,128)(2,1)S(1)}, bf16[64,2048]{1,0:T(8,128)(2,1)S(1)}, u32[]{:S(2)}, u32[]{:S(2)}) collective-permute-start(bf16[64,2048]{1,0:T(8,128)(2,1)S(1)} %add_convert_fusion.here_ref), channel_id=1, source_target_pairs={{0,16},{8,24},{16,0},{24,8},{1,17},{9,25},{17,1},{25,9},{2,18},{10... | collective-permute-start | bytes 786440 | tf_op jit(solution)/shard_map/ppermute | solution.py:433
  37.6 8.3 %collective-permute-start.12 = (bf16[64,2176]{1,0:T(8,128)(2,1)S(1)}, bf16[64,2176]{1,0:T(8,128)(2,1)S(1)}, u32[]{:S(2)}, u32[]{:S(2)}) collective-permute-start(bf16[64,2176]{1,0:T(8,128)(2,1)S(1)} %get-tuple-element.96.refs_0_.refs_1_), channel_id=1, source_target_pairs={{0,2},{2,4},{4,6},{6,7},{7,5},{5,3},{3,1},{1,0},{8,10},{10,12},{12... | collective-permute-start | bytes 835592 | tf_op jit(solution)/shard_map/ppermute | solution.py:463
  39.3 8.3 %collective-permute-start.17 = (bf16[64,2176]{1,0:T(8,128)(2,1)S(1)}, bf16[64,2176]{1,0:T(8,128)(2,1)S(1)}, u32[]{:S(2)}, u32[]{:S(2)}) collective-permute-start(bf16[64,2176]{1,0:T(8,128)(2,1)S(1)} %get-tuple-element.96.refs_0_.refs_1_), channel_id=1, source_target_pairs={{2,0},{4,2},{6,4},{7,6},{5,7},{3,5},{1,3},{0,1},{10,8},{12,10},{14... | collective-permute-start | bytes 835592 | tf_op jit(solution)/shard_map/ppermute | solution.py:464
  45.9 7.4 %collective-permute-start.16 = (bf16[64,2176]{1,0:T(8,128)(2,1)S(1)}, bf16[64,2176]{1,0:T(8,128)(2,1)S(1)}, u32[]{:S(2)}, u32[]{:S(2)}) collective-permute-start(bf16[64,2176]{1,0:T(8,128)(2,1)S(1)} %collective-permute-done.12.refs_1_), channel_id=1, source_target_pairs={{0,2},{2,4},{4,6},{6,7},{7,5},{5,3},{3,1},{1,0},{8,10},{10,12},{12... | collective-permute-start | bytes 835592 | tf_op jit(solution)/shard_map/ppermute | solution.py:463
  47.6 7.3 %collective-permute-start.20 = (bf16[64,2176]{1,0:T(8,128)(2,1)S(1)}, bf16[64,2176]{1,0:T(8,128)(2,1)S(1)}, u32[]{:S(2)}, u32[]{:S(2)}) collective-permute-start(bf16[64,2176]{1,0:T(8,128)(2,1)S(1)} %collective-permute-done.17.refs_2_), channel_id=1, source_target_pairs={{2,0},{4,2},{6,4},{7,6},{5,7},{3,5},{1,3},{0,1},{10,8},{12,10},{14... | collective-permute-start | bytes 835592 | tf_op jit(solution)/shard_map/ppermute | solution.py:464
  51.1 15.8 %collective-permute-start.23 = (bf16[64,2048]{1,0:T(8,128)(2,1)S(1)}, bf16[64,2048]{1,0:T(8,128)(2,1)S(1)}, u32[]{:S(2)}, u32[]{:S(2)}) collective-permute-start(bf16[64,2048]{1,0:T(8,128)(2,1)S(1)} %get-tuple-element.109), channel_id=1, source_target_pairs={{0,16},{8,24},{16,0},{24,8},{1,17},{9,25},{17,1},{25,9},{2,18},{10... | collective-permute-start | bytes 786440 | tf_op jit(solution)/shard_map/ppermute | solution.py:446
  58.3 8.7 %collective-permute-start.24 = (bf16[64,2048]{1,0:T(8,128)(2,1)S(1)}, bf16[64,2048]{1,0:T(8,128)(2,1)S(1)}, u32[]{:S(2)}, u32[]{:S(2)}) collective-permute-start(bf16[64,2048]{1,0:T(8,128)(2,1)S(1)} %get-tuple-element.110), channel_id=1, source_target_pairs={{0,16},{8,24},{16,0},{24,8},{1,17},{9,25},{17,1},{25,9},{2,18},{10... | collective-permute-start | bytes 786440 | tf_op jit(solution)/shard_map/ppermute | solution.py:446
  61.9 7.2 %collective-permute-start.25 = (bf16[32,2176]{1,0:T(8,128)(2,1)S(1)}, bf16[32,2176]{1,0:T(8,128)(2,1)S(1)}, u32[]{:S(2)}, u32[]{:S(2)}) collective-permute-start(bf16[32,2176]{1,0:T(8,128)(2,1)S(1)} %slice.49), channel_id=1, source_target_pairs={{2,0},{4,2},{6,4},{7,6},{5,7},{3,5},{1,3},{0,1},{10,8},{12,10},{14... | collective-permute-start | bytes 417800 | tf_op jit(solution)/shard_map/ppermute | solution.py:469
  65.4 8.4 %collective-permute-start.32 = (bf16[64,2048]{1,0:T(8,128)(2,1)S(1)}, bf16[64,2048]{1,0:T(8,128)(2,1)S(1)}, u32[]{:S(2)}, u32[]{:S(2)}) collective-permute-start(bf16[64,2048]{1,0:T(8,128)(2,1)S(1)} %get-tuple-element.117), channel_id=1, source_target_pairs={{0,16},{8,24},{16,0},{24,8},{1,17},{9,25},{17,1},{25,9},{2,18},{10... | collective-permute-start | bytes 786440 | tf_op jit(solution)/shard_map/ppermute | solution.py:446
  67.0 10.7 %collective-permute-start.27 = (bf16[32,2048]{1,0:T(8,128)(2,1)S(1)}, bf16[32,2048]{1,0:T(8,128)(2,1)S(1)}, u32[]{:S(2)}, u32[]{:S(2)}) collective-permute-start(bf16[32,2048]{1,0:T(8,128)(2,1)S(1)} %get-tuple-element.125), channel_id=1, source_target_pairs={{0,2},{2,4},{4,6},{6,7},{7,5},{5,3},{3,1},{1,0},{8,10},{10,12},{12... | collective-permute-start | bytes 393224 | tf_op jit(solution)/shard_map/ppermute | solution.py:494
  68.7 9.1 %collective-permute-start.29 = (bf16[32,2048]{1,0:T(8,128)(2,1)S(1)}, bf16[32,2048]{1,0:T(8,128)(2,1)S(1)}, u32[]{:S(2)}, u32[]{:S(2)}) collective-permute-start(bf16[32,2048]{1,0:T(8,128)(2,1)S(1)} %get-tuple-element.126), channel_id=1, source_target_pairs={{2,0},{4,2},{6,4},{7,6},{5,7},{3,5},{1,3},{0,1},{10,8},{12,10},{14... | collective-permute-start | bytes 393224 | tf_op jit(solution)/shard_map/ppermute | solution.py:495
  72.1 7.8 %collective-permute-start.26 = (bf16[64,2048]{1,0:T(8,128)(2,1)S(1)}, bf16[64,2048]{1,0:T(8,128)(2,1)S(1)}, u32[]{:S(2)}, u32[]{:S(2)}) collective-permute-start(bf16[64,2048]{1,0:T(8,128)(2,1)S(1)} %get-tuple-element.113), channel_id=1, source_target_pairs={{0,16},{8,24},{16,0},{24,8},{1,17},{9,25},{17,1},{25,9},{2,18},{10... | collective-permute-start | bytes 786440 | tf_op jit(solution)/shard_map/ppermute | solution.py:446
  73.8 12.1 %collective-permute-start.33 = (bf16[32,2048]{1,0:T(8,128)(2,1)S(1)}, bf16[32,2048]{1,0:T(8,128)(2,1)S(1)}, u32[]{:S(2)}, u32[]{:S(2)}) collective-permute-start(bf16[32,2048]{1,0:T(8,128)(2,1)S(1)} %get-tuple-element.127), channel_id=1, source_target_pairs={{0,6},{2,7},{4,5},{6,3},{7,1},{5,0},{3,2},{1,4},{8,14},{10,15},{12... | collective-permute-start | bytes 393224 | tf_op jit(solution)/shard_map/ppermute | solution.py:488
  77.5 8.5 %collective-permute-start.34 = (bf16[32,2048]{1,0:T(8,128)(2,1)S(1)}, bf16[32,2048]{1,0:T(8,128)(2,1)S(1)}, u32[]{:S(2)}, u32[]{:S(2)}) collective-permute-start(bf16[32,2048]{1,0:T(8,128)(2,1)S(1)} %get-tuple-element.128), channel_id=1, source_target_pairs={{0,5},{2,3},{4,1},{6,0},{7,2},{5,4},{3,6},{1,7},{8,13},{10,11},{12... | collective-permute-start | bytes 393224 | tf_op jit(solution)/shard_map/ppermute | solution.py:488
  77.8 8.1 %collective-permute-start.28 = (bf16[32,2048]{1,0:T(8,128)(2,1)S(1)}, bf16[32,2048]{1,0:T(8,128)(2,1)S(1)}, u32[]{:S(2)}, u32[]{:S(2)}) collective-permute-start(bf16[32,2048]{1,0:T(8,128)(2,1)S(1)} %get-tuple-element.123), channel_id=1, source_target_pairs={{0,2},{2,4},{4,6},{6,7},{7,5},{5,3},{3,1},{1,0},{8,10},{10,12},{12... | collective-permute-start | bytes 393224 | tf_op jit(solution)/shard_map/ppermute | solution.py:494
  78.0 8.4 %collective-permute-start.30 = (bf16[32,2048]{1,0:T(8,128)(2,1)S(1)}, bf16[32,2048]{1,0:T(8,128)(2,1)S(1)}, u32[]{:S(2)}, u32[]{:S(2)}) collective-permute-start(bf16[32,2048]{1,0:T(8,128)(2,1)S(1)} %get-tuple-element.124), channel_id=1, source_target_pairs={{2,0},{4,2},{6,4},{7,6},{5,7},{3,5},{1,3},{0,1},{10,8},{12,10},{14... | collective-permute-start | bytes 393224 | tf_op jit(solution)/shard_map/ppermute | solution.py:495
  80.0 7.8 %collective-permute-start.31 = (bf16[32,2048]{1,0:T(8,128)(2,1)S(1)}, bf16[32,2048]{1,0:T(8,128)(2,1)S(1)}, u32[]{:S(2)}, u32[]{:S(2)}) collective-permute-start(bf16[32,2048]{1,0:T(8,128)(2,1)S(1)} %add_convert_fusion.4), channel_id=1, source_target_pairs={{0,7},{2,5},{4,3},{6,1},{7,0},{5,2},{3,4},{1,6},{8,15},{10,13},{12... | collective-permute-start | bytes 393224 | tf_op jit(solution)/shard_map/ppermute | solution.py:488
  (27 other events, 157.2 us)

commit v4 on v3

--- a/solution.py
+++ b/solution.py
@@ -20,6 +20,8 @@
 EXPERT_VMEM = 4 << 20
 COLUMNS = 512
 SLOTS = 6
+PIECES = 4
+FETCH = 1
 EFFORT = 50
 
 
@@ -27,7 +29,25 @@
     return min(tokens_here, 4 * ((tokens_here * TOP + 2 * experts - 1) // (2 * experts)))
 
 
-def attend_kernel(heads, tokens, page_len, page_count, first, last, *refs):
+def in_vmem(arrays):
+    return [pltpu.with_memory_space_constraint(a, pltpu.VMEM) for a in arrays]
+
+
+def in_hbm(arrays):
+    return [pltpu.with_memory_space_constraint(a, pltpu.HBM) for a in arrays]
+
+
+def in_pieces(source, target, sems):
+    rows = source.shape[0] // PIECES
+    return [
+        pltpu.make_async_copy(
+            source.at[pl.ds(i * rows, rows)], target.at[pl.ds(i * rows, rows)], sems.at[i]
+        )
+        for i in range(PIECES)
+    ]
+
+
+def attend_kernel(heads, tokens, page_len, page_count, first, fetching, last, *refs):
     refs = list(refs)
     q_ref = refs.pop(0)
     if first:
@@ -36,13 +56,17 @@
         max_in, sum_in, acc_in = refs.pop(0), refs.pop(0), refs.pop(0)
     if last:
         core_ref, proj_ref = refs.pop(0), refs.pop(0)
+        keep_ref, send_ref = refs[-2:]
+    if fetching:
+        fetches = in_pieces(refs.pop(0), refs[-2], refs[-1])
+        for fetch in fetches:
+            fetch.start()
     page_refs = [refs.pop(0) for _ in range(page_count)]
-    if last:
-        keep_ref, send_ref, proj_buf, proj_sem = refs
-        fetch = pltpu.make_async_copy(proj_ref, proj_buf, proj_sem)
-        fetch.start()
     scaling = 1.0 / math.sqrt(HD)
-    q = jnp.concatenate([q_ref[:, h * HD : (h + 1) * HD] for h in range(heads)], axis=0)
+    if first:
+        q = jnp.concatenate([q_ref[:, h * HD : (h + 1) * HD] for h in range(heads)], axis=0)
+    else:
+        q = q_ref[...]
     blocks = [(ref[:page_len, :HD], ref[:page_len, HD:]) for ref in page_refs]
     scores = [
         lax.dot_general(q, k, (((1,), (1,)), ((), ())), preferred_element_type=f32) * scaling
@@ -83,65 +107,64 @@
         rows = jnp.concatenate([out[h * tokens : (h + 1) * tokens] for h in range(heads)], axis=1)
         half = tokens // 2
         second = core_ref[0] == 1
-        fetch.wait()
-        for c in range(0, proj_buf.shape[1], COLUMNS):
+        for c in range(0, proj_ref.shape[1], COLUMNS):
             cols = slice(c, c + COLUMNS)
-            terms = jnp.dot(rows, proj_buf[:, cols], preferred_element_type=f32).astype(bf16)
+            terms = jnp.dot(rows, proj_ref[:, cols], preferred_element_type=f32).astype(bf16)
             low, high = terms[:half], terms[half:]
             keep_ref[:, cols] = jnp.where(second, high, low)
             send_ref[:, cols] = jnp.where(second, low, high)
     else:
-        max_out, sum_out, acc_out = refs
+        max_out, sum_out, acc_out = refs[:3]
         max_out[...] = jnp.broadcast_to(new_max, max_out.shape)
         sum_out[...] = jnp.broadcast_to(total, sum_out.shape)
         acc_out[...] = acc
-
-
-def attend(queries, pages, page_len, state=None, suffix=None, core=None, out_proj=None):
-    tokens, width = queries.shape
-    heads = width // HD
+        if first:
+            refs[3][...] = q
+        if fetching:
+            for fetch in fetches:
+                fetch.wait()
+
+
+def attend(queries, pages, page_len, tokens, state=None, suffix=None, fetch=None, core=None, proj=None):
     first, last = state is None, core is not None
+    heads = queries.shape[1] // HD if first else queries.shape[0] // tokens
     vmem, smem = pl.BlockSpec(memory_space=pltpu.VMEM), pl.BlockSpec(memory_space=pltpu.SMEM)
-    args, specs = [queries], [vmem]
+    outs = [jax.ShapeDtypeStruct((heads * tokens, HD), f32)] * 3
+    scratch = []
     if first:
-        args += list(suffix)
+        lengths, suffix = suffix
+        args = in_hbm([queries]) + [lengths] + in_hbm([suffix])
+        pages = in_hbm(pages)
+        specs = [vmem, smem, vmem]
+        outs.append(jax.ShapeDtypeStruct((heads * tokens, HD), bf16))
+    else:
+        args = [queries] + list(state)
+        specs = [vmem] * 4
+    if last:
+        args += [core] + in_vmem([proj])
         specs += [smem, vmem]
-    else:
-        args += list(state)
-        specs += [vmem] * 3
-    if last:
-        args += [core, pltpu.with_memory_space_constraint(out_proj, pltpu.HBM)]
-        specs += [smem, pl.BlockSpec(memory_space=pl.ANY)]
-    args += pages
-    specs += [vmem] * len(pages)
-    if last:
-        outs = [jax.ShapeDtypeStruct((tokens // 2, out_proj.shape[1]), bf16)] * 2
-        scratch = [pltpu.VMEM(out_proj.shape, bf16), pltpu.SemaphoreType.DMA(())]
-    else:
-        outs = [jax.ShapeDtypeStruct((heads * tokens, HD), f32)] * 3
-        scratch = []
-    keys = sum(page_len for _ in pages) + (tokens if first else 0)
+        outs = [jax.ShapeDtypeStruct((tokens // 2, proj.shape[1]), bf16)] * 2
+    if fetch is not None:
+        args += in_hbm([fetch])
+        specs.append(pl.BlockSpec(memory_space=pl.ANY))
+        outs.append(pltpu.VMEM(fetch.shape, fetch.dtype))
+        scratch.append(pltpu.SemaphoreType.DMA((PIECES,)))
+    keys = page_len * len(pages) + (tokens if first else 0)
     return pl.pallas_call(
-        functools.partial(attend_kernel, heads, tokens, page_len, len(pages), first, last),
+        functools.partial(
+            attend_kernel, heads, tokens, page_len, len(pages), first, fetch is not None, last
+        ),
         out_shape=outs,
-        in_specs=specs,
+        in_specs=specs + [vmem] * len(pages),
         out_specs=[vmem] * len(outs),
         scratch_shapes=scratch,
         compiler_params=pltpu.CompilerParams(vmem_limit_bytes=12 << 20),
         cost_estimate=pl.CostEstimate(
-            flops=4 * heads * tokens * keys * HD,
-            bytes_accessed=4 * keys * HD + 2 * tokens * width,
+            flops=(1 if last or fetch is not None else EFFORT) * 4 * heads * tokens * keys * HD,
+            bytes_accessed=4 * keys * HD + 2 * heads * tokens * HD,
             transcendentals=heads * tokens * keys,
         ),
-    )(*args)
-
-
-def in_vmem(arrays):
-    return [pltpu.with_memory_space_constraint(a, pltpu.VMEM) for a in arrays]
-
-
-def in_hbm(arrays):
-    return [pltpu.with_memory_space_constraint(a, pltpu.HBM) for a in arrays]
+    )(*args, *pages)
 
 
 def norm_kernel(
@@ -413,19 +436,18 @@
     suffix = (suffix_lengths, suffix_kv[:, 0])
     core_arr = jnp.reshape(core, (1,)).astype(jnp.int32)
     from_left, from_right = page, page
-    cut = page_len // 2
-    state = attend(queries, [page], page_len, suffix=suffix)
+    *state, stacked = attend(queries, [page], page_len, tokens, suffix=suffix)
     for s in range(1, steps):
         from_left = lax.ppermute(from_left, "exp", right)
         from_right = lax.ppermute(from_right, "exp", left)
         from_left, state = lax.optimization_barrier((from_left, state))
-        state = attend(queries, [from_left, from_right], page_len, state=state)
-    low = lax.ppermute(from_left[:cut], "exp", right)
-    high = lax.ppermute(from_right[cut:], "exp", left)
-    low, state = lax.optimization_barrier((low, state))
-    keep, send = attend(
-        queries, [low, high], cut, state=state, core=core_arr, out_proj=out_proj
-    )
+        fetch = out_proj if s == steps - FETCH else None
+        *state, = attend(stacked, [from_left, from_right], page_len, tokens, state, fetch=fetch)
+        if fetch is not None:
+            proj = state.pop()
+    from_left = lax.ppermute(from_left, "exp", right)
+    from_left, state = lax.optimization_barrier((from_left, state))
+    keep, send = attend(stacked, [from_left], page_len, tokens, state, core=core_arr, proj=proj)
 
     other = lax.ppermute(send, "req", sibling)
     terms = (keep.astype(f32) + other.astype(f32)).astype(bf16)
@@ -504,7 +526,10 @@
         )
 
     mine = joined(plane, mine, lax.ppermute(mine, "req", across))
-    return joined(core, mine, lax.ppermute(mine, "req", sibling))
+    theirs = lax.ppermute(mine, "req", sibling)
+    out = lax.dynamic_update_slice(jnp.zeros((tokens, width), bf16), mine, (core * half, 0))
+    out, theirs = lax.optimization_barrier((out, theirs))
+    return lax.dynamic_update_slice(out, theirs, ((1 - core) * half, 0))
 
 
 def on_device(

time: 96.8 us -> 93.8 us (0.969)
  waiting for transfers between devices: 17.5 us -> 15.5 us
  local copies, waits for them, and re-layouts: 7.05 us -> 5.17 us
  starting transfers between devices: 39.4 us -> 40.7 us
    unnamed x28 -> x22, local copies, waits for them, and re-layouts: 6.48 us -> 3.86 us
    ppermute x3, waiting for transfers between devices: 3.86 us -> 1.71 us  [on_device_ring(): lax.ppermute(part(block).astype(bf16), 'exp', along(sign * d))]
    ppermute x3 -> x1, starting transfers between devices: 2.15 us -> 0.07 us  [on_device_ring(): theirs = lax.ppermute(mine, 'req', sibling)]
    ppermute x6 -> x7, starting transfers between devices: 11.3 us -> 13.2 us  [on_device_ring(): from_left = lax.ppermute(from_left, 'exp', right)]
    ppermute x3 -> x1, waiting for transfers between devices: 3.35 us -> 1.52 us  [on_device_ring(): theirs = lax.ppermute(mine, 'req', sibling)]
    ppermute x2, waiting for transfers between devices: 0.51 us -> 2.03 us  [on_device_ring(): to_left = lax.ppermute(b.astype(bf16), 'exp', left)]
    ppermute x2, starting transfers between devices: 2.31 us -> 1.14 us  [on_device_ring(): to_left = lax.ppermute(b.astype(bf16), 'exp', left)]
    ppermute x2, starting transfers between devices: 1.84 us -> 3.02 us  [on_device_ring(): to_right = lax.ppermute(a.astype(bf16), 'exp', right)]
  transfers between devices with their start and end apart: 37 -> 36, of which waited for: 15 -> 13; matrix products, arithmetic and copies ran while one was open for 1% -> 1% of each run, Pallas kernels for 31% -> 33%
where the time goes in v4:
time: 93.8 us; the launch traced here: 92.8 us
  starting transfers between devices  40.7 us (43%)
  Pallas kernels  30.4 us (32%)
  waiting for transfers between devices  15.5 us (17%)
  local copies, waits for them, and re-layouts  5.17 us (6%)
    ppermute x7, starting transfers between devices, on_device_ring(): from_left = lax.ppermute(from_left, 'exp', right)  13.2 us
    pallas_call x4, Pallas kernels, expert(): pl.pallas_call(functools.partial(expert_kernel, n_experts, counts, shared...  11.9 us
    pallas_call x5, Pallas kernels, attend(): pl.pallas_call(functools.partial(attend_kernel, heads, tokens, page_len,...  9.4 us
    ppermute x3, starting transfers between devices, on_device_ring(): lax.ppermute(part(block).astype(bf16), 'exp', along(sign * d))  8.36 us
    pallas_call x1, Pallas kernels, shared_expert(): pl.pallas_call(functools.partial(shared_kernel, len(rows)), out_shape=jax...  6.12 us
    ppermute x4, starting transfers between devices, work(): got = lax.ppermute(send, 'req', across)  5.56 us
    ppermute x7, waiting for transfers between devices, on_device_ring(): from_left = lax.ppermute(from_left, 'exp', right)  4.19 us
    unnamed x22, local copies, waits for them, and re-layouts  3.86 us
  transfers between devices with their start and end apart: 36, of which 13 were waited for; matrix products, arithmetic and copies ran while one was open for 1% of the time, Pallas kernels for 33%

profile of v4, /device:TPU:0, one launch (start us, length us, event | category | flops | bytes accessed | tf_op | source)
XLA Modules:
  0.0 92.8 jit_solution(15284226392597239344)
XLA Ops:
  0.0 3.0 %collective-permute-start = (bf16[256,256]{1,0:T(8,128)(2,1)}, bf16[256,256]{1,0:T(8,128)(2,1)S(1)}, u32[]{:S(2)}, u32[]{:S(2)}) collective-permute-start(bf16[256,256]{1,0:T(8,128)(2,1)} %bitcast.22), channel_id=1, source_target_pairs={{0,2},{2,4},{4,6},{6,7},{7,5},{5,3},{3,1},{1,0},{8,10},{10,12},{12... | collective-permute-start | bytes 393224 | tf_op jit(solution)/shard_map/ppermute | solution.py:441
  4.2 1.6 %shard_map.145 = (f32[512,128]{1,0:T(8,128)S(1)}, f32[512,128]{1,0:T(8,128)S(1)}, f32[512,128]{1,0:T(8,128)S(1)}, bf16[512,128]{1,0:T(8,128)(2,1)S(1)}) custom-call(bf16[128,512]{1,0:T(8,128)(2,1)} %refs_0_.1, s32[1,4]{1,0:T(1,128)S(1)} %copy-done.5, bf16[128,256]{1,0:T(8,128)(2,1)} %bitcast.25, bf16[256,256]{1,0:T(8,128)(2,1)} %bitcast.24), custom_call_target="tpu_custom_call" | custom-call | flops 5033164800 | bytes 327680 | tf_op jit(solution)/shard_map/pallas_call | solution.py:153
  6.7 1.8 %collective-permute-start.1 = (bf16[256,256]{1,0:T(8,128)(2,1)S(1)}, bf16[256,256]{1,0:T(8,128)(2,1)S(1)}, u32[]{:S(2)}, u32[]{:S(2)}) collective-permute-start(bf16[256,256]{1,0:T(8,128)(2,1)S(1)} %collective-permute-done.refs_4_), channel_id=1, source_target_pairs={{0,2},{2,4},{4,6},{6,7},{7,5},{5,3},{3,1},{1,0},{8,10},{10,12},{12... | collective-permute-start | bytes 393224 | tf_op jit(solution)/shard_map/ppermute | solution.py:441
  8.7 1.9 %shard_map.146 = (f32[512,128]{1,0:T(8,128)S(1)}, f32[512,128]{1,0:T(8,128)S(1)}, f32[512,128]{1,0:T(8,128)S(1)}) custom-call(bf16[512,128]{1,0:T(8,128)(2,1)S(1)} %get-tuple-element.66.refs_0_, f32[512,128]{1,0:T(8,128)S(1)} %get-tuple-element.71.refs_1_, f32[512,128]{1,0:T(8,128)S(1)} %get-tuple-element.72.refs_2_, ...), custom_call_target="tpu_custom_call" | custom-call | flops 6710886400 | bytes 393216 | tf_op jit(solution)/shard_map/pallas_call | solution.py:153
  11.6 1.8 %collective-permute-start.3 = (bf16[256,256]{1,0:T(8,128)(2,1)S(1)}, bf16[256,256]{1,0:T(8,128)(2,1)S(1)}, u32[]{:S(2)}, u32[]{:S(2)}) collective-permute-start(bf16[256,256]{1,0:T(8,128)(2,1)S(1)} %collective-permute-done.1.refs_4_), channel_id=1, source_target_pairs={{0,2},{2,4},{4,6},{6,7},{7,5},{5,3},{3,1},{1,0},{8,10},{10,12},{12... | collective-permute-start | bytes 393224 | tf_op jit(solution)/shard_map/ppermute | solution.py:441
  13.7 1.9 %shard_map.147 = (f32[512,128]{1,0:T(8,128)S(1)}, f32[512,128]{1,0:T(8,128)S(1)}, f32[512,128]{1,0:T(8,128)S(1)}) custom-call(bf16[512,128]{1,0:T(8,128)(2,1)S(1)} %get-tuple-element.66.refs_0_, f32[512,128]{1,0:T(8,128)S(1)} %get-tuple-element.78.refs_1_, f32[512,128]{1,0:T(8,128)S(1)} %get-tuple-element.79.refs_2_, ...), custom_call_target="tpu_custom_call" | custom-call | flops 6710886400 | bytes 393216 | tf_op jit(solution)/shard_map/pallas_call | solution.py:153
  16.9 1.8 %collective-permute-start.5 = (bf16[256,256]{1,0:T(8,128)(2,1)S(1)}, bf16[256,256]{1,0:T(8,128)(2,1)S(1)}, u32[]{:S(2)}, u32[]{:S(2)}) collective-permute-start(bf16[256,256]{1,0:T(8,128)(2,1)S(1)} %collective-permute-done.3.refs_5_), channel_id=1, source_target_pairs={{0,2},{2,4},{4,6},{6,7},{7,5},{5,3},{3,1},{1,0},{8,10},{10,12},{12... | collective-permute-start | bytes 393224 | tf_op jit(solution)/shard_map/ppermute | solution.py:448
  19.2 3.0 %shard_map.148 = (f32[512,128]{1,0:T(8,128)S(1)}, f32[512,128]{1,0:T(8,128)S(1)}, f32[512,128]{1,0:T(8,128)S(1)}, bf16[512,2048]{1,0:T(8,128)(2,1)S(1)}) custom-call(bf16[512,128]{1,0:T(8,128)(2,1)S(1)} %get-tuple-element.66.refs_0_, f32[512,128]{1,0:T(8,128)S(1)} %get-tuple-element.85.refs_1_, f32[512,128]{1,0:T(8,128)S(1)} %get-tuple-element.86.refs_2_, ...), custom_call_target="tpu_custom_call" | custom-call | flops 134217728 | bytes 393216 | tf_op jit(solution)/shard_map/pallas_call | solution.py:153
  27.6 2.7 %shard_map.150 = (bf16[704,2048]{1,0:T(8,128)(2,1)S(1)}, bf16[704,2048]{1,0:T(8,128)(2,1)S(1)}) custom-call(bf16[352,2048]{1,0:T(8,128)(2,1)} %bitcast.19, bf16[352,2048]{1,0:T(8,128)(2,1)} %collective-permute-done.9.refs_1_, bf16[352,2048]{1,0:T(8,128)(2,1)} %bitcast.21, bf16[352,2048]{1,0:T(8,128)(2,1)} %collective-permute-done.10.refs_3_), custom_call_target="tpu_custom_call" | custom-call | bytes 5767168 | tf_op jit(solution)/shard_map/pallas_call | solution.py:223
  34.5 1.6 %collective-permute-start.11 = (bf16[64,2176]{1,0:T(8,128)(2,1)S(1)}, bf16[64,2176]{1,0:T(8,128)(2,1)S(1)}, u32[]{:S(2)}, u32[]{:S(2)}) collective-permute-start(bf16[64,2176]{1,0:T(8,128)(2,1)S(1)} %get-tuple-element.102.refs_0_.refs_1_), channel_id=1, source_target_pairs={{0,2},{2,4},{4,6},{6,7},{7,5},{5,3},{3,1},{1,0},{8,10},{10,12},{12... | collective-permute-start | bytes 835592 | tf_op jit(solution)/shard_map/ppermute | solution.py:485
  36.7 6.1 %shard_map.152.refs_4_ = f32[64,2048]{1,0:T(8,128)S(1)} custom-call(bf16[64,2176]{1,0:T(8,128)(2,1)S(1)} %get-tuple-element.102.refs_0_.refs_1_, bf16[352,2048]{1,0:T(8,128)(2,1)} %bitcast.14, bf16[352,2048]{1,0:T(8,128)(2,1)} %collective-permute-done.12.refs_2_, bf16[352,2048]{1,0:T(8,128)(2,1)} %bitcast.17, ...), custom_call_target="tpu_custom_call" | custom-call | flops 553648128 | bytes 8650752 | tf_op jit(solution)/shard_map/pallas_call | solution.py:283
  42.8 1.6 %collective-permute-start.15 = (bf16[64,2176]{1,0:T(8,128)(2,1)S(1)}, bf16[64,2176]{1,0:T(8,128)(2,1)S(1)}, u32[]{:S(2)}, u32[]{:S(2)}) collective-permute-start(bf16[64,2176]{1,0:T(8,128)(2,1)S(1)} %collective-permute-done.11.refs_1_), channel_id=1, source_target_pairs={{0,2},{2,4},{4,6},{6,7},{7,5},{5,3},{3,1},{1,0},{8,10},{10,12},{12... | collective-permute-start | bytes 835592 | tf_op jit(solution)/shard_map/ppermute | solution.py:485
  44.9 3.1 %shard_map.153 = (bf16[32,2048]{1,0:T(8,128)(2,1)S(1)}, bf16[32,2048]{1,0:T(8,128)(2,1)S(1)}, bf16[64,2048]{1,0:T(8,128)(2,1)S(1)}, bf16[704,2048]{1,0:T(8,128)(2,1)S(1)}) custom-call(s32[2]{0:T(128)S(1)} %pad_add_fusion.refs_0_, bf16[64,2176]{1,0:T(8,128)(2,1)S(1)} %collective-permute-done.11.refs_1_, bf16[64,2176]{1,0:T(8,128)(2,1)S(1)} %collective-permute-done.16.refs_2_, ...), custom_call_target="tpu_custom_call" | custom-call | flops 55364812800 | bytes 1048576 | tf_op jit(solution)/shard_map/pallas_call | solution.py:361
  52.2 2.9 %shard_map.154 = (bf16[32,2048]{1,0:T(8,128)(2,1)S(1)}, bf16[32,2048]{1,0:T(8,128)(2,1)S(1)}, bf16[64,2048]{1,0:T(8,128)(2,1)S(1)}) custom-call(s32[2]{0:T(128)S(1)} %pad_add_fusion.refs_0_, bf16[64,2176]{1,0:T(8,128)(2,1)S(1)} %collective-permute-done.15.refs_1_, bf16[64,2176]{1,0:T(8,128)(2,1)S(1)} %collective-permute-done.19.refs_2_, ...), custom_call_target="tpu_custom_call" | custom-call | flops 55364812800 | bytes 1048576 | tf_op jit(solution)/shard_map/pallas_call | solution.py:361
  57.0 1.6 %collective-permute-start.20 = (bf16[32,2176]{1,0:T(8,128)(2,1)S(1)}, bf16[32,2176]{1,0:T(8,128)(2,1)S(1)}, u32[]{:S(2)}, u32[]{:S(2)}) collective-permute-start(bf16[32,2176]{1,0:T(8,128)(2,1)S(1)} %slice.30), channel_id=1, source_target_pairs={{0,2},{2,4},{4,6},{6,7},{7,5},{5,3},{3,1},{1,0},{8,10},{10,12},{12... | collective-permute-start | bytes 417800 | tf_op jit(solution)/shard_map/ppermute | solution.py:490
  59.3 2.9 %shard_map.155 = (bf16[32,2048]{1,0:T(8,128)(2,1)S(1)}, bf16[32,2048]{1,0:T(8,128)(2,1)S(1)}, bf16[64,2048]{1,0:T(8,128)(2,1)S(1)}) custom-call(s32[2]{0:T(128)S(1)} %pad_add_fusion.refs_0_, bf16[64,2176]{1,0:T(8,128)(2,1)S(1)} %collective-permute-done.18.refs_1_, bf16[64,2176]{1,0:T(8,128)(2,1)S(1)} %collective-permute-done.21.refs_2_, ...), custom_call_target="tpu_custom_call" | custom-call | flops 55364812800 | bytes 1048576 | tf_op jit(solution)/shard_map/pallas_call | solution.py:361
  63.9 1.6 %collective-permute-start.26 = (bf16[32,2048]{1,0:T(8,128)(2,1)S(1)}, bf16[32,2048]{1,0:T(8,128)(2,1)S(1)}, u32[]{:S(2)}, u32[]{:S(2)}) collective-permute-start(bf16[32,2048]{1,0:T(8,128)(2,1)S(1)} %get-tuple-element.133), channel_id=1, source_target_pairs={{0,2},{2,4},{4,6},{6,7},{7,5},{5,3},{3,1},{1,0},{8,10},{10,12},{12... | collective-permute-start | bytes 393224 | tf_op jit(solution)/shard_map/ppermute | solution.py:516
  66.0 3.0 %shard_map.156 = (bf16[32,2048]{1,0:T(8,128)(2,1)S(1)}, bf16[32,2048]{1,0:T(8,128)(2,1)S(1)}, bf16[64,2048]{1,0:T(8,128)(2,1)S(1)}) custom-call(s32[2]{0:T(128)S(1)} %pad_add_fusion.refs_0_, bf16[64,2176]{1,0:T(8,128)(2,1)S(1)} %get-tuple-element.102.refs_0_.refs_1_, bf16[32,2176]{1,0:T(8,128)(2,1)S(1)} %collective-permute-done.20.refs_2_, ...), custom_call_target="tpu_custom_call" | custom-call | flops 55364812800 | bytes 1048576 | tf_op jit(solution)/shard_map/pallas_call | solution.py:361
  70.7 3.7 %collective-permute-start.32 = (bf16[32,2048]{1,0:T(8,128)(2,1)S(1)}, bf16[32,2048]{1,0:T(8,128)(2,1)S(1)}, u32[]{:S(2)}, u32[]{:S(2)}) collective-permute-start(bf16[32,2048]{1,0:T(8,128)(2,1)S(1)} %get-tuple-element.135), channel_id=1, source_target_pairs={{0,6},{2,7},{4,5},{6,3},{7,1},{5,0},{3,2},{1,4},{8,14},{10,15},{12... | collective-permute-start | bytes 393224 | tf_op jit(solution)/shard_map/ppermute | solution.py:510
  76.8 4.5 %collective-permute-start.30 = (bf16[32,2048]{1,0:T(8,128)(2,1)S(1)}, bf16[32,2048]{1,0:T(8,128)(2,1)S(1)}, u32[]{:S(2)}, u32[]{:S(2)}) collective-permute-start(bf16[32,2048]{1,0:T(8,128)(2,1)S(1)} %add_convert_fusion.4), channel_id=1, source_target_pairs={{0,7},{2,5},{4,3},{6,1},{7,0},{5,2},{3,4},{1,6},{8,15},{10,13},{12... | collective-permute-start | bytes 393224 | tf_op jit(solution)/shard_map/ppermute | solution.py:510
  81.3 1.7 %collective-permute-done.32 = bf16[32,2048]{1,0:T(8,128)(2,1)S(1)} collective-permute-done((bf16[32,2048]{1,0:T(8,128)(2,1)S(1)}, bf16[32,2048]{1,0:T(8,128)(2,1)S(1)}, u32[]{:S(2)}, u32[]{:S(2)}) %collective-permute-start.32) | collective-permute-done | bytes 131104 | tf_op jit(solution)/shard_map/ppermute | solution.py:510
  83.0 2.0 %collective-permute-done.29 = bf16[32,2048]{1,0:T(8,128)(2,1)S(1)} collective-permute-done((bf16[32,2048]{1,0:T(8,128)(2,1)S(1)}, bf16[32,2048]{1,0:T(8,128)(2,1)S(1)}, u32[]{:S(2)}, u32[]{:S(2)}) %collective-permute-start.29) | collective-permute-done | bytes 131104 | tf_op jit(solution)/shard_map/ppermute | solution.py:517
  85.2 2.2 %collective-permute-start.34 = (bf16[32,2048]{1,0:T(8,128)(2,1)S(1)}, bf16[32,2048]{1,0:T(8,128)(2,1)S(1)}, u32[]{:S(2)}, u32[]{:S(2)}) collective-permute-start(bf16[32,2048]{1,0:T(8,128)(2,1)S(1)} %add_convert_fusion.1), channel_id=1, source_target_pairs={{0,16},{8,24},{16,0},{24,8},{1,17},{9,25},{17,1},{25,9},{2,18},{10... | collective-permute-start | bytes 393224 | tf_op jit(solution)/shard_map/ppermute | solution.py:528
  87.4 2.9 %collective-permute-done.34 = bf16[32,2048]{1,0:T(8,128)(2,1)S(1)} collective-permute-done((bf16[32,2048]{1,0:T(8,128)(2,1)S(1)}, bf16[32,2048]{1,0:T(8,128)(2,1)S(1)}, u32[]{:S(2)}, u32[]{:S(2)}) %collective-permute-start.34) | collective-permute-done | bytes 131104 | tf_op jit(solution)/shard_map/ppermute | solution.py:528
  (108 shorter events, 31.5 us)
Async XLA Ops:
  3.0 22.0 %collective-permute-start.10 = (bf16[352,2048]{1,0:T(8,128)(2,1)}, bf16[352,2048]{1,0:T(8,128)(2,1)}, u32[]{:S(2)}, u32[]{:S(2)}) collective-permute-start(bf16[352,2048]{1,0:T(8,128)(2,1)} %bitcast.20), channel_id=1, source_target_pairs={{0,8},{8,0},{16,24},{24,16},{1,9},{9,1},{17,25},{25,17},{2,10},{10... | collective-permute-start | bytes 4325384 | tf_op jit(solution)/shard_map/ppermute | solution.py:431
  3.0 22.8 %collective-permute-start.9 = (bf16[352,2048]{1,0:T(8,128)(2,1)}, bf16[352,2048]{1,0:T(8,128)(2,1)}, u32[]{:S(2)}, u32[]{:S(2)}) collective-permute-start(bf16[352,2048]{1,0:T(8,128)(2,1)} %bitcast.18), channel_id=1, source_target_pairs={{0,8},{8,0},{16,24},{24,16},{1,9},{9,1},{17,25},{25,17},{2,10},{10... | collective-permute-start | bytes 4325384 | tf_op jit(solution)/shard_map/ppermute | solution.py:431
  18.7 17.5 %collective-permute-start.12 = (bf16[352,2048]{1,0:T(8,128)(2,1)S(1)}, bf16[352,2048]{1,0:T(8,128)(2,1)}, u32[]{:S(2)}, u32[]{:S(2)}) collective-permute-start(bf16[352,2048]{1,0:T(8,128)(2,1)S(1)} %bitcast.15), channel_id=1, source_target_pairs={{0,8},{8,0},{16,24},{24,16},{1,9},{9,1},{17,25},{25,17},{2,10},{10... | collective-permute-start | bytes 4325384 | tf_op jit(solution)/shard_map/ppermute | solution.py:431
  18.7 18.0 %collective-permute-start.13 = (bf16[352,2048]{1,0:T(8,128)(2,1)}, bf16[352,2048]{1,0:T(8,128)(2,1)}, u32[]{:S(2)}, u32[]{:S(2)}) collective-permute-start(bf16[352,2048]{1,0:T(8,128)(2,1)} %bitcast.16), channel_id=1, source_target_pairs={{0,8},{8,0},{16,24},{24,16},{1,9},{9,1},{17,25},{25,17},{2,10},{10... | collective-permute-start | bytes 4325384 | tf_op jit(solution)/shard_map/ppermute | solution.py:431
  24.9 11.8 %collective-permute-start.14 = (bf16[352,2048]{1,0:T(8,128)(2,1)}, bf16[352,2048]{1,0:T(8,128)(2,1)}, u32[]{:S(2)}, u32[]{:S(2)}) collective-permute-start(bf16[352,2048]{1,0:T(8,128)(2,1)} %refs_5_.1), channel_id=1, source_target_pairs={{0,8},{8,0},{16,24},{24,16},{1,9},{9,1},{17,25},{25,17},{2,10},{10... | collective-permute-start | bytes 4325384 | tf_op jit(solution)/shard_map/ppermute | solution.py:431
  25.0 19.9 %collective-permute-start.17 = (bf16[352,2048]{1,0:T(8,128)(2,1)}, bf16[352,2048]{1,0:T(8,128)(2,1)}, u32[]{:S(2)}, u32[]{:S(2)}) collective-permute-start(bf16[352,2048]{1,0:T(8,128)(2,1)} %bitcast.13.refs_5_), channel_id=1, source_target_pairs={{0,8},{8,0},{16,24},{24,16},{1,9},{9,1},{17,25},{25,17},{2,10},{10... | collective-permute-start | bytes 4325384 | tf_op jit(solution)/shard_map/ppermute | solution.py:431
  25.9 8.4 %collective-permute-start.8 = (bf16[64,2048]{1,0:T(8,128)(2,1)S(1)}, bf16[64,2048]{1,0:T(8,128)(2,1)S(1)}, u32[]{:S(2)}, u32[]{:S(2)}) collective-permute-start(bf16[64,2048]{1,0:T(8,128)(2,1)S(1)} %add_convert_fusion.here_ref), channel_id=1, source_target_pairs={{0,16},{8,24},{16,0},{24,8},{1,17},{9,25},{17,1},{25,9},{2,18},{10... | collective-permute-start | bytes 786440 | tf_op jit(solution)/shard_map/ppermute | solution.py:455
  34.5 8.3 %collective-permute-start.11 = (bf16[64,2176]{1,0:T(8,128)(2,1)S(1)}, bf16[64,2176]{1,0:T(8,128)(2,1)S(1)}, u32[]{:S(2)}, u32[]{:S(2)}) collective-permute-start(bf16[64,2176]{1,0:T(8,128)(2,1)S(1)} %get-tuple-element.102.refs_0_.refs_1_), channel_id=1, source_target_pairs={{0,2},{2,4},{4,6},{6,7},{7,5},{5,3},{3,1},{1,0},{8,10},{10,12},{12... | collective-permute-start | bytes 835592 | tf_op jit(solution)/shard_map/ppermute | solution.py:485
  36.2 8.3 %collective-permute-start.16 = (bf16[64,2176]{1,0:T(8,128)(2,1)S(1)}, bf16[64,2176]{1,0:T(8,128)(2,1)S(1)}, u32[]{:S(2)}, u32[]{:S(2)}) collective-permute-start(bf16[64,2176]{1,0:T(8,128)(2,1)S(1)} %get-tuple-element.102.refs_0_.refs_1_), channel_id=1, source_target_pairs={{2,0},{4,2},{6,4},{7,6},{5,7},{3,5},{1,3},{0,1},{10,8},{12,10},{14... | collective-permute-start | bytes 835592 | tf_op jit(solution)/shard_map/ppermute | solution.py:486
  42.8 7.4 %collective-permute-start.15 = (bf16[64,2176]{1,0:T(8,128)(2,1)S(1)}, bf16[64,2176]{1,0:T(8,128)(2,1)S(1)}, u32[]{:S(2)}, u32[]{:S(2)}) collective-permute-start(bf16[64,2176]{1,0:T(8,128)(2,1)S(1)} %collective-permute-done.11.refs_1_), channel_id=1, source_target_pairs={{0,2},{2,4},{4,6},{6,7},{7,5},{5,3},{3,1},{1,0},{8,10},{10,12},{12... | collective-permute-start | bytes 835592 | tf_op jit(solution)/shard_map/ppermute | solution.py:485
  44.5 7.3 %collective-permute-start.19 = (bf16[64,2176]{1,0:T(8,128)(2,1)S(1)}, bf16[64,2176]{1,0:T(8,128)(2,1)S(1)}, u32[]{:S(2)}, u32[]{:S(2)}) collective-permute-start(bf16[64,2176]{1,0:T(8,128)(2,1)S(1)} %collective-permute-done.16.refs_2_), channel_id=1, source_target_pairs={{2,0},{4,2},{6,4},{7,6},{5,7},{3,5},{1,3},{0,1},{10,8},{12,10},{14... | collective-permute-start | bytes 835592 | tf_op jit(solution)/shard_map/ppermute | solution.py:486
  48.0 15.9 %collective-permute-start.22 = (bf16[64,2048]{1,0:T(8,128)(2,1)S(1)}, bf16[64,2048]{1,0:T(8,128)(2,1)S(1)}, u32[]{:S(2)}, u32[]{:S(2)}) collective-permute-start(bf16[64,2048]{1,0:T(8,128)(2,1)S(1)} %get-tuple-element.115), channel_id=1, source_target_pairs={{0,16},{8,24},{16,0},{24,8},{1,17},{9,25},{17,1},{25,9},{2,18},{10... | collective-permute-start | bytes 786440 | tf_op jit(solution)/shard_map/ppermute | solution.py:468
  51.8 7.0 %collective-permute-start.21 = (bf16[64,2176]{1,0:T(8,128)(2,1)S(1)}, bf16[64,2176]{1,0:T(8,128)(2,1)S(1)}, u32[]{:S(2)}, u32[]{:S(2)}) collective-permute-start(bf16[64,2176]{1,0:T(8,128)(2,1)S(1)} %collective-permute-done.19.refs_2_), channel_id=1, source_target_pairs={{2,0},{4,2},{6,4},{7,6},{5,7},{3,5},{1,3},{0,1},{10,8},{12,10},{14... | collective-permute-start | bytes 835592 | tf_op jit(solution)/shard_map/ppermute | solution.py:486
  55.2 8.7 %collective-permute-start.23 = (bf16[64,2048]{1,0:T(8,128)(2,1)S(1)}, bf16[64,2048]{1,0:T(8,128)(2,1)S(1)}, u32[]{:S(2)}, u32[]{:S(2)}) collective-permute-start(bf16[64,2048]{1,0:T(8,128)(2,1)S(1)} %get-tuple-element.116), channel_id=1, source_target_pairs={{0,16},{8,24},{16,0},{24,8},{1,17},{9,25},{17,1},{25,9},{2,18},{10... | collective-permute-start | bytes 786440 | tf_op jit(solution)/shard_map/ppermute | solution.py:468
  58.8 7.2 %collective-permute-start.24 = (bf16[32,2176]{1,0:T(8,128)(2,1)S(1)}, bf16[32,2176]{1,0:T(8,128)(2,1)S(1)}, u32[]{:S(2)}, u32[]{:S(2)}) collective-permute-start(bf16[32,2176]{1,0:T(8,128)(2,1)S(1)} %slice.40), channel_id=1, source_target_pairs={{2,0},{4,2},{6,4},{7,6},{5,7},{3,5},{1,3},{0,1},{10,8},{12,10},{14... | collective-permute-start | bytes 417800 | tf_op jit(solution)/shard_map/ppermute | solution.py:491
  62.3 8.4 %collective-permute-start.31 = (bf16[64,2048]{1,0:T(8,128)(2,1)S(1)}, bf16[64,2048]{1,0:T(8,128)(2,1)S(1)}, u32[]{:S(2)}, u32[]{:S(2)}) collective-permute-start(bf16[64,2048]{1,0:T(8,128)(2,1)S(1)} %get-tuple-element.123), channel_id=1, source_target_pairs={{0,16},{8,24},{16,0},{24,8},{1,17},{9,25},{17,1},{25,9},{2,18},{10... | collective-permute-start | bytes 786440 | tf_op jit(solution)/shard_map/ppermute | solution.py:468
  63.9 10.6 %collective-permute-start.26 = (bf16[32,2048]{1,0:T(8,128)(2,1)S(1)}, bf16[32,2048]{1,0:T(8,128)(2,1)S(1)}, u32[]{:S(2)}, u32[]{:S(2)}) collective-permute-start(bf16[32,2048]{1,0:T(8,128)(2,1)S(1)} %get-tuple-element.133), channel_id=1, source_target_pairs={{0,2},{2,4},{4,6},{6,7},{7,5},{5,3},{3,1},{1,0},{8,10},{10,12},{12... | collective-permute-start | bytes 393224 | tf_op jit(solution)/shard_map/ppermute | solution.py:516
  65.6 9.0 %collective-permute-start.28 = (bf16[32,2048]{1,0:T(8,128)(2,1)S(1)}, bf16[32,2048]{1,0:T(8,128)(2,1)S(1)}, u32[]{:S(2)}, u32[]{:S(2)}) collective-permute-start(bf16[32,2048]{1,0:T(8,128)(2,1)S(1)} %get-tuple-element.134), channel_id=1, source_target_pairs={{2,0},{4,2},{6,4},{7,6},{5,7},{3,5},{1,3},{0,1},{10,8},{12,10},{14... | collective-permute-start | bytes 393224 | tf_op jit(solution)/shard_map/ppermute | solution.py:517
  69.0 7.8 %collective-permute-start.25 = (bf16[64,2048]{1,0:T(8,128)(2,1)S(1)}, bf16[64,2048]{1,0:T(8,128)(2,1)S(1)}, u32[]{:S(2)}, u32[]{:S(2)}) collective-permute-start(bf16[64,2048]{1,0:T(8,128)(2,1)S(1)} %get-tuple-element.119), channel_id=1, source_target_pairs={{0,16},{8,24},{16,0},{24,8},{1,17},{9,25},{17,1},{25,9},{2,18},{10... | collective-permute-start | bytes 786440 | tf_op jit(solution)/shard_map/ppermute | solution.py:468
  70.7 12.3 %collective-permute-start.32 = (bf16[32,2048]{1,0:T(8,128)(2,1)S(1)}, bf16[32,2048]{1,0:T(8,128)(2,1)S(1)}, u32[]{:S(2)}, u32[]{:S(2)}) collective-permute-start(bf16[32,2048]{1,0:T(8,128)(2,1)S(1)} %get-tuple-element.135), channel_id=1, source_target_pairs={{0,6},{2,7},{4,5},{6,3},{7,1},{5,0},{3,2},{1,4},{8,14},{10,15},{12... | collective-permute-start | bytes 393224 | tf_op jit(solution)/shard_map/ppermute | solution.py:510
  74.4 8.6 %collective-permute-start.33 = (bf16[32,2048]{1,0:T(8,128)(2,1)S(1)}, bf16[32,2048]{1,0:T(8,128)(2,1)S(1)}, u32[]{:S(2)}, u32[]{:S(2)}) collective-permute-start(bf16[32,2048]{1,0:T(8,128)(2,1)S(1)} %get-tuple-element.136), channel_id=1, source_target_pairs={{0,5},{2,3},{4,1},{6,0},{7,2},{5,4},{3,6},{1,7},{8,13},{10,11},{12... | collective-permute-start | bytes 393224 | tf_op jit(solution)/shard_map/ppermute | solution.py:510
  74.7 8.3 %collective-permute-start.27 = (bf16[32,2048]{1,0:T(8,128)(2,1)S(1)}, bf16[32,2048]{1,0:T(8,128)(2,1)S(1)}, u32[]{:S(2)}, u32[]{:S(2)}) collective-permute-start(bf16[32,2048]{1,0:T(8,128)(2,1)S(1)} %get-tuple-element.131), channel_id=1, source_target_pairs={{0,2},{2,4},{4,6},{6,7},{7,5},{5,3},{3,1},{1,0},{8,10},{10,12},{12... | collective-permute-start | bytes 393224 | tf_op jit(solution)/shard_map/ppermute | solution.py:516
  76.1 8.9 %collective-permute-start.29 = (bf16[32,2048]{1,0:T(8,128)(2,1)S(1)}, bf16[32,2048]{1,0:T(8,128)(2,1)S(1)}, u32[]{:S(2)}, u32[]{:S(2)}) collective-permute-start(bf16[32,2048]{1,0:T(8,128)(2,1)S(1)} %get-tuple-element.132), channel_id=1, source_target_pairs={{2,0},{4,2},{6,4},{7,6},{5,7},{3,5},{1,3},{0,1},{10,8},{12,10},{14... | collective-permute-start | bytes 393224 | tf_op jit(solution)/shard_map/ppermute | solution.py:517
  76.8 8.2 %collective-permute-start.30 = (bf16[32,2048]{1,0:T(8,128)(2,1)S(1)}, bf16[32,2048]{1,0:T(8,128)(2,1)S(1)}, u32[]{:S(2)}, u32[]{:S(2)}) collective-permute-start(bf16[32,2048]{1,0:T(8,128)(2,1)S(1)} %add_convert_fusion.4), channel_id=1, source_target_pairs={{0,7},{2,5},{4,3},{6,1},{7,0},{5,2},{3,4},{1,6},{8,15},{10,13},{12... | collective-permute-start | bytes 393224 | tf_op jit(solution)/shard_map/ppermute | solution.py:510
  (23 other events, 124.1 us)

commit v5 on v4

--- a/solution.py
+++ b/solution.py
@@ -16,10 +16,9 @@
 f32 = jnp.float32
 bf16 = jnp.bfloat16
 STAGE_VMEM = 1 << 20
-SHARED_VMEM = 5 << 20
+SHARED_VMEM = 11 << 20
 EXPERT_VMEM = 4 << 20
 COLUMNS = 512
-SLOTS = 6
 PIECES = 4
 FETCH = 1
 EFFORT = 50
@@ -167,9 +166,8 @@
     )(*args, *pages)
 
 
-def norm_kernel(
-    plane_ref, here_ref, there_ref, residual_ref, gain_ref, gates_ref, hidden_ref, out_ref
-):
+def norm_kernel(n_experts, plane_ref, *refs):
+    here_ref, there_ref, residual_ref, gain_ref, routes_ref, weights_ref, hidden_ref, out_ref = refs
     width = hidden_ref.shape[1]
     attn_out = here_ref[...].astype(f32) + there_ref[...].astype(f32)
     hidden = (residual_ref[...].astype(f32) + attn_out).astype(bf16)
@@ -179,25 +177,33 @@
     mean_square = jnp.mean(hidden * hidden, axis=-1, keepdims=True)
     normed = hidden * lax.rsqrt(mean_square + norm_eps) * gain_ref[...].astype(f32)
     out_ref[:, :width] = normed.astype(bf16)
-    out_ref[:, width:] = gates_ref[...]
-
-
-def norm(plane, here, there, residual, gain, gates):
+    lane = lax.broadcasted_iota(jnp.int32, (here_ref.shape[0], HD), 1)
+    first = lane < n_experts
+    named = jnp.where(first, lane, lane - n_experts)
+    gates = jnp.zeros(lane.shape, f32)
+    for j in range(routes_ref.shape[1]):
+        gates = jnp.where(named == routes_ref[:, j : j + 1], weights_ref[:, j : j + 1], gates)
+    head = gates.astype(bf16)
+    rest = (gates - head.astype(f32)).astype(bf16)
+    out_ref[:, width:] = jnp.where(first, head, rest)
+
+
+def norm(n_experts, plane, here, there, residual, gain, routes, route_weights):
     rows, width = here.shape
     vmem = pl.BlockSpec(memory_space=pltpu.VMEM)
     return pl.pallas_call(
-        norm_kernel,
+        functools.partial(norm_kernel, n_experts),
         out_shape=[
             jax.ShapeDtypeStruct((rows // 2, width), bf16),
-            jax.ShapeDtypeStruct((rows, width + gates.shape[1]), bf16),
+            jax.ShapeDtypeStruct((rows, width + HD), bf16),
         ],
-        in_specs=[pl.BlockSpec(memory_space=pltpu.SMEM)] + [vmem] * 5,
+        in_specs=[pl.BlockSpec(memory_space=pltpu.SMEM)] + [vmem] * 6,
         out_specs=[vmem] * 2,
         compiler_params=pltpu.CompilerParams(vmem_limit_bytes=2 << 20),
         cost_estimate=pl.CostEstimate(
             flops=8 * rows * width, bytes_accessed=10 * rows * width, transcendentals=rows
         ),
-    )(plane, here, there, residual, gain.reshape(1, width), gates)
+    )(plane, here, there, residual, gain.reshape(1, width), routes, route_weights)
 
 
 def joining(sources, outs, sems):
@@ -242,42 +248,29 @@
 
 def shared_kernel(count, *refs):
     rows, sources = refs[:count], refs[count : count + 6]
-    out_ref, buf, sems = refs[-3:]
-    block, width = sources[0].shape
-    slots, units = buf.shape[:2]
-    pieces = 2 * block // units
-
-    def fetch(k):
-        core, row = divmod(k // 3 * units, block)
-        return pltpu.make_async_copy(
-            sources[2 * (k % 3) + core].at[pl.ds(row, units)], buf.at[k % slots], sems.at[k % slots]
-        )
-
-    def free(k):
-        if k + slots < 3 * pieces:
-            fetch(k + slots).start()
-
-    for k in range(slots):
-        fetch(k).start()
+    out_ref, gate_buf, up_buf, down_buf, sems = refs[count + 6 :]
+    width = out_ref.shape[1]
+    copies = joining(sources, [gate_buf, up_buf, down_buf], sems)
+    for copy in copies:
+        copy.start()
     x = jnp.concatenate([ref[:, :width] for ref in rows], axis=0)
-    for piece in range(pieces):
-        k = 3 * piece
-        fetch(k).wait()
-        fetch(k + 1).wait()
-        hidden = hidden_units(x, buf[k % slots], buf[(k + 1) % slots])
-        free(k)
-        free(k + 1)
-        fetch(k + 2).wait()
-        for c in range(0, width, COLUMNS):
-            cols = slice(c, c + COLUMNS)
-            out = jnp.dot(hidden, buf[(k + 2) % slots, :, cols], preferred_element_type=f32)
-            out_ref[:, cols] = out if piece == 0 else out_ref[:, cols] + out
-        free(k + 2)
+    contract = (((1,), (1,)), ((), ()))
+    for copy in copies[:2]:
+        copy.wait()
+    gate = lax.dot_general(x, gate_buf[...], contract, preferred_element_type=f32)
+    for copy in copies[2:4]:
+        copy.wait()
+    up = lax.dot_general(x, up_buf[...], contract, preferred_element_type=f32)
+    hidden = (gate / (1.0 + jnp.exp(-gate)) * up).astype(bf16)
+    for copy in copies[4:]:
+        copy.wait()
+    for c in range(0, width, COLUMNS):
+        cols = slice(c, c + COLUMNS)
+        out_ref[:, cols] = jnp.dot(hidden, down_buf[:, cols], preferred_element_type=f32)
 
 
 def shared_expert(rows, weights):
     block, width = weights[0].shape
-    units = block // 2
     count = sum(a.shape[0] for a in rows)
     vmem = pl.BlockSpec(memory_space=pltpu.VMEM)
     return pl.pallas_call(
@@ -286,8 +279,8 @@
         in_specs=[vmem] * len(rows) + [pl.BlockSpec(memory_space=pl.ANY)] * 6,
         out_specs=vmem,
         scratch_shapes=[
-            pltpu.VMEM((SLOTS, units, width), bf16),
-            pltpu.SemaphoreType.DMA((SLOTS,)),
+            *[pltpu.VMEM((2 * block, width), bf16)] * 3,
+            pltpu.SemaphoreType.DMA((6,)),
         ],
         compiler_params=pltpu.CompilerParams(vmem_limit_bytes=SHARED_VMEM),
         cost_estimate=pl.CostEstimate(
@@ -411,16 +404,6 @@
     def half_of(x):
         return lax.dynamic_slice_in_dim(x, core * half, half, 0)
 
-    slots = jnp.arange(n, dtype=jnp.int32)
-    dense = jnp.sum(
-        jnp.where(half_of(routes)[:, :, None] == slots, half_of(route_weights)[:, :, None], 0.0),
-        axis=1,
-    )
-    head = lax.reduce_precision(dense, 8, 7)
-    rest = lax.reduce_precision(dense - head, 8, 7)
-    gates = jnp.concatenate(
-        [head, rest, jnp.zeros((half, -2 * n % HD), f32)], axis=1
-    ).astype(bf16)
     page = prefix_kv[0]
     page_len = page.shape[0]
 
@@ -456,7 +439,14 @@
     terms_across, staged = lax.optimization_barrier((terms_across, stage(expert_weights[:4])))
     staged = list(staged) + expert_weights[4:]
     hidden_here, normed = norm(
-        plane.reshape(1), terms, terms_across, half_of(residual), norm_gain, gates
+        n,
+        plane.reshape(1),
+        terms,
+        terms_across,
+        half_of(residual),
+        norm_gain,
+        half_of(routes),
+        half_of(route_weights),
     )
     place = jnp.stack([me, plane]).astype(jnp.int32)
 

time: 93.8 us -> 92.9 us (level)
  waiting for transfers between devices: 15.5 us -> 16.9 us
  Pallas kernels: 30.4 us -> 29.3 us
    ppermute x1, starting transfers between devices: 2.17 us -> 0.79 us  [on_device_ring(): mine = joined(plane, mine, lax.ppermute(mine, 'req', across))]
    ppermute x1, waiting for transfers between devices: 2.95 us -> 4.24 us  [on_device_ring(): mine = joined(plane, mine, lax.ppermute(mine, 'req', across))]
    pallas_call x1, Pallas kernels: 6.12 us -> 4.98 us  [shared_expert(): pl.pallas_call(functools.partial(shared_kernel, len(rows)), out_shape=jax...]
    unnamed x22 -> x24, local copies, waits for them, and re-layouts: 3.86 us -> 4.25 us
  transfers between devices with their start and end apart: 36 -> 36, of which waited for: 13 -> 15; matrix products, arithmetic and copies ran while one was open for 1% -> 1% of each run, Pallas kernels for 33% -> 32%
where the time goes in v5:
time: 92.9 us; the launch traced here: 92.7 us
  starting transfers between devices  40.4 us (43%)
  Pallas kernels  29.3 us (32%)
  waiting for transfers between devices  16.9 us (18%)
  local copies, waits for them, and re-layouts  5.21 us (6%)
    ppermute x7, starting transfers between devices, on_device_ring(): from_left = lax.ppermute(from_left, 'exp', right)  13.5 us
    pallas_call x4, Pallas kernels, expert(): pl.pallas_call(functools.partial(expert_kernel, n_experts, counts, shared...  11.9 us
    pallas_call x5, Pallas kernels, attend(): pl.pallas_call(functools.partial(attend_kernel, heads, tokens, page_len,...  9.41 us
    ppermute x3, starting transfers between devices, on_device_ring(): lax.ppermute(part(block).astype(bf16), 'exp', along(sign * d))  8.69 us
    ppermute x4, starting transfers between devices, work(): got = lax.ppermute(send, 'req', across)  6.17 us
    ppermute x7, waiting for transfers between devices, on_device_ring(): from_left = lax.ppermute(from_left, 'exp', right)  5.12 us
    pallas_call x1, Pallas kernels, shared_expert(): pl.pallas_call(functools.partial(shared_kernel, len(rows)), out_shape=jax...  4.98 us
    unnamed x24, local copies, waits for them, and re-layouts  4.25 us
  transfers between devices with their start and end apart: 36, of which 15 were waited for; matrix products, arithmetic and copies ran while one was open for 1% of the time, Pallas kernels for 32%

profile of v5, /device:TPU:0, one launch (start us, length us, event | category | flops | bytes accessed | tf_op | source)
XLA Modules:
  0.0 92.7 jit_solution(4764986577381169629)
XLA Ops:
  0.0 3.0 %collective-permute-start = (bf16[256,256]{1,0:T(8,128)(2,1)}, bf16[256,256]{1,0:T(8,128)(2,1)S(1)}, u32[]{:S(2)}, u32[]{:S(2)}) collective-permute-start(bf16[256,256]{1,0:T(8,128)(2,1)} %bitcast.20), channel_id=1, source_target_pairs={{0,2},{2,4},{4,6},{6,7},{7,5},{5,3},{3,1},{1,0},{8,10},{10,12},{12... | collective-permute-start | bytes 393224 | tf_op jit(solution)/shard_map/ppermute | solution.py:424
  6.7 1.8 %collective-permute-start.1 = (bf16[256,256]{1,0:T(8,128)(2,1)S(1)}, bf16[256,256]{1,0:T(8,128)(2,1)S(1)}, u32[]{:S(2)}, u32[]{:S(2)}) collective-permute-start(bf16[256,256]{1,0:T(8,128)(2,1)S(1)} %collective-permute-done.refs_4_), channel_id=1, source_target_pairs={{0,2},{2,4},{4,6},{6,7},{7,5},{5,3},{3,1},{1,0},{8,10},{10,12},{12... | collective-permute-start | bytes 393224 | tf_op jit(solution)/shard_map/ppermute | solution.py:424
  8.7 1.9 %shard_map.146 = (f32[512,128]{1,0:T(8,128)S(1)}, f32[512,128]{1,0:T(8,128)S(1)}, f32[512,128]{1,0:T(8,128)S(1)}) custom-call(bf16[512,128]{1,0:T(8,128)(2,1)S(1)} %get-tuple-element.66.refs_0_, f32[512,128]{1,0:T(8,128)S(1)} %get-tuple-element.71.refs_1_, f32[512,128]{1,0:T(8,128)S(1)} %get-tuple-element.72.refs_2_, ...), custom_call_target="tpu_custom_call" | custom-call | flops 6710886400 | bytes 393216 | tf_op jit(solution)/shard_map/pallas_call | solution.py:152
  11.6 1.8 %collective-permute-start.3 = (bf16[256,256]{1,0:T(8,128)(2,1)S(1)}, bf16[256,256]{1,0:T(8,128)(2,1)S(1)}, u32[]{:S(2)}, u32[]{:S(2)}) collective-permute-start(bf16[256,256]{1,0:T(8,128)(2,1)S(1)} %collective-permute-done.1.refs_4_), channel_id=1, source_target_pairs={{0,2},{2,4},{4,6},{6,7},{7,5},{5,3},{3,1},{1,0},{8,10},{10,12},{12... | collective-permute-start | bytes 393224 | tf_op jit(solution)/shard_map/ppermute | solution.py:424
  13.7 1.9 %shard_map.147 = (f32[512,128]{1,0:T(8,128)S(1)}, f32[512,128]{1,0:T(8,128)S(1)}, f32[512,128]{1,0:T(8,128)S(1)}) custom-call(bf16[512,128]{1,0:T(8,128)(2,1)S(1)} %get-tuple-element.66.refs_0_, f32[512,128]{1,0:T(8,128)S(1)} %get-tuple-element.78.refs_1_, f32[512,128]{1,0:T(8,128)S(1)} %get-tuple-element.79.refs_2_, ...), custom_call_target="tpu_custom_call" | custom-call | flops 6710886400 | bytes 393216 | tf_op jit(solution)/shard_map/pallas_call | solution.py:152
  16.9 1.8 %collective-permute-start.5 = (bf16[256,256]{1,0:T(8,128)(2,1)S(1)}, bf16[256,256]{1,0:T(8,128)(2,1)S(1)}, u32[]{:S(2)}, u32[]{:S(2)}) collective-permute-start(bf16[256,256]{1,0:T(8,128)(2,1)S(1)} %collective-permute-done.3.refs_5_), channel_id=1, source_target_pairs={{0,2},{2,4},{4,6},{6,7},{7,5},{5,3},{3,1},{1,0},{8,10},{10,12},{12... | collective-permute-start | bytes 393224 | tf_op jit(solution)/shard_map/ppermute | solution.py:431
  18.7 3.0 %shard_map.148 = (f32[512,128]{1,0:T(8,128)S(1)}, f32[512,128]{1,0:T(8,128)S(1)}, f32[512,128]{1,0:T(8,128)S(1)}, bf16[512,2048]{1,0:T(8,128)(2,1)S(1)}) custom-call(bf16[512,128]{1,0:T(8,128)(2,1)S(1)} %get-tuple-element.66.refs_0_, f32[512,128]{1,0:T(8,128)S(1)} %get-tuple-element.85.refs_1_, f32[512,128]{1,0:T(8,128)S(1)} %get-tuple-element.86.refs_2_, ...), custom_call_target="tpu_custom_call" | custom-call | flops 134217728 | bytes 393216 | tf_op jit(solution)/shard_map/pallas_call | solution.py:152
  25.2 1.8 %collective-permute-start.8 = (bf16[64,2048]{1,0:T(8,128)(2,1)S(1)}, bf16[64,2048]{1,0:T(8,128)(2,1)S(1)}, u32[]{:S(2)}, u32[]{:S(2)}) collective-permute-start(bf16[64,2048]{1,0:T(8,128)(2,1)S(1)} %add_convert_fusion.refs_0_), channel_id=1, source_target_pairs={{0,16},{8,24},{16,0},{24,8},{1,17},{9,25},{17,1},{25,9},{2,18},{10... | collective-permute-start | bytes 786440 | tf_op jit(solution)/shard_map/ppermute | solution.py:438
  27.3 2.7 %shard_map.150 = (bf16[704,2048]{1,0:T(8,128)(2,1)S(1)}, bf16[704,2048]{1,0:T(8,128)(2,1)S(1)}) custom-call(bf16[352,2048]{1,0:T(8,128)(2,1)} %bitcast.17, bf16[352,2048]{1,0:T(8,128)(2,1)} %collective-permute-done.9.refs_1_, bf16[352,2048]{1,0:T(8,128)(2,1)} %bitcast.19, bf16[352,2048]{1,0:T(8,128)(2,1)} %collective-permute-done.10.refs_3_), custom_call_target="tpu_custom_call" | custom-call | bytes 5767168 | tf_op jit(solution)/shard_map/pallas_call | solution.py:229
  34.0 1.8 %collective-permute-start.11 = (bf16[64,2176]{1,0:T(8,128)(2,1)S(1)}, bf16[64,2176]{1,0:T(8,128)(2,1)S(1)}, u32[]{:S(2)}, u32[]{:S(2)}) collective-permute-start(bf16[64,2176]{1,0:T(8,128)(2,1)S(1)} %get-tuple-element.102.refs_0_.refs_1_), channel_id=1, source_target_pairs={{0,2},{2,4},{4,6},{6,7},{7,5},{5,3},{3,1},{1,0},{8,10},{10,12},{12... | collective-permute-start | bytes 835592 | tf_op jit(solution)/shard_map/ppermute | solution.py:475
  36.1 5.0 %shard_map.152.refs_4_ = f32[64,2048]{1,0:T(8,128)S(1)} custom-call(bf16[64,2176]{1,0:T(8,128)(2,1)S(1)} %get-tuple-element.102.refs_0_.refs_1_, bf16[352,2048]{1,0:T(8,128)(2,1)} %bitcast.14, bf16[352,2048]{1,0:T(8,128)(2,1)} %collective-permute-done.12.refs_2_, bf16[352,2048]{1,0:T(8,128)(2,1)} %bitcast.12.refs_3_, ...), custom_call_target="tpu_custom_call" | custom-call | flops 553648128 | bytes 8650752 | tf_op jit(solution)/shard_map/pallas_call | solution.py:276
  42.0 1.7 %collective-permute-start.15 = (bf16[64,2176]{1,0:T(8,128)(2,1)S(1)}, bf16[64,2176]{1,0:T(8,128)(2,1)S(1)}, u32[]{:S(2)}, u32[]{:S(2)}) collective-permute-start(bf16[64,2176]{1,0:T(8,128)(2,1)S(1)} %collective-permute-done.11.refs_1_), channel_id=1, source_target_pairs={{0,2},{2,4},{4,6},{6,7},{7,5},{5,3},{3,1},{1,0},{8,10},{10,12},{12... | collective-permute-start | bytes 835592 | tf_op jit(solution)/shard_map/ppermute | solution.py:475
  44.0 3.1 %shard_map.153 = (bf16[32,2048]{1,0:T(8,128)(2,1)S(1)}, bf16[32,2048]{1,0:T(8,128)(2,1)S(1)}, bf16[64,2048]{1,0:T(8,128)(2,1)S(1)}, bf16[704,2048]{1,0:T(8,128)(2,1)S(1)}) custom-call(s32[2]{0:T(128)S(1)} %pad_add_fusion.refs_0_, bf16[64,2176]{1,0:T(8,128)(2,1)S(1)} %collective-permute-done.11.refs_1_, bf16[64,2176]{1,0:T(8,128)(2,1)S(1)} %collective-permute-done.16.refs_2_, ...), custom_call_target="tpu_custom_call" | custom-call | flops 55364812800 | bytes 1048576 | tf_op jit(solution)/shard_map/pallas_call | solution.py:354
  47.1 1.7 %collective-permute-start.22 = (bf16[64,2048]{1,0:T(8,128)(2,1)S(1)}, bf16[64,2048]{1,0:T(8,128)(2,1)S(1)}, u32[]{:S(2)}, u32[]{:S(2)}) collective-permute-start(bf16[64,2048]{1,0:T(8,128)(2,1)S(1)} %get-tuple-element.115), channel_id=1, source_target_pairs={{0,16},{8,24},{16,0},{24,8},{1,17},{9,25},{17,1},{25,9},{2,18},{10... | collective-permute-start | bytes 786440 | tf_op jit(solution)/shard_map/ppermute | solution.py:458
  51.1 2.9 %shard_map.154 = (bf16[32,2048]{1,0:T(8,128)(2,1)S(1)}, bf16[32,2048]{1,0:T(8,128)(2,1)S(1)}, bf16[64,2048]{1,0:T(8,128)(2,1)S(1)}) custom-call(s32[2]{0:T(128)S(1)} %pad_add_fusion.refs_0_, bf16[64,2176]{1,0:T(8,128)(2,1)S(1)} %collective-permute-done.15.refs_1_, bf16[64,2176]{1,0:T(8,128)(2,1)S(1)} %collective-permute-done.19.refs_2_, ...), custom_call_target="tpu_custom_call" | custom-call | flops 55364812800 | bytes 1048576 | tf_op jit(solution)/shard_map/pallas_call | solution.py:354
  56.2 1.7 %collective-permute-start.20 = (bf16[32,2176]{1,0:T(8,128)(2,1)S(1)}, bf16[32,2176]{1,0:T(8,128)(2,1)S(1)}, u32[]{:S(2)}, u32[]{:S(2)}) collective-permute-start(bf16[32,2176]{1,0:T(8,128)(2,1)S(1)} %slice.30), channel_id=1, source_target_pairs={{0,2},{2,4},{4,6},{6,7},{7,5},{5,3},{3,1},{1,0},{8,10},{10,12},{12... | collective-permute-start | bytes 417800 | tf_op jit(solution)/shard_map/ppermute | solution.py:480
  58.5 2.9 %shard_map.155 = (bf16[32,2048]{1,0:T(8,128)(2,1)S(1)}, bf16[32,2048]{1,0:T(8,128)(2,1)S(1)}, bf16[64,2048]{1,0:T(8,128)(2,1)S(1)}) custom-call(s32[2]{0:T(128)S(1)} %pad_add_fusion.refs_0_, bf16[64,2176]{1,0:T(8,128)(2,1)S(1)} %collective-permute-done.18.refs_1_, bf16[64,2176]{1,0:T(8,128)(2,1)S(1)} %collective-permute-done.21.refs_2_, ...), custom_call_target="tpu_custom_call" | custom-call | flops 55364812800 | bytes 1048576 | tf_op jit(solution)/shard_map/pallas_call | solution.py:354
  61.4 1.7 %collective-permute-start.31 = (bf16[64,2048]{1,0:T(8,128)(2,1)S(1)}, bf16[64,2048]{1,0:T(8,128)(2,1)S(1)}, u32[]{:S(2)}, u32[]{:S(2)}) collective-permute-start(bf16[64,2048]{1,0:T(8,128)(2,1)S(1)} %get-tuple-element.123), channel_id=1, source_target_pairs={{0,16},{8,24},{16,0},{24,8},{1,17},{9,25},{17,1},{25,9},{2,18},{10... | collective-permute-start | bytes 786440 | tf_op jit(solution)/shard_map/ppermute | solution.py:458
  63.2 1.6 %collective-permute-start.26 = (bf16[32,2048]{1,0:T(8,128)(2,1)S(1)}, bf16[32,2048]{1,0:T(8,128)(2,1)S(1)}, u32[]{:S(2)}, u32[]{:S(2)}) collective-permute-start(bf16[32,2048]{1,0:T(8,128)(2,1)S(1)} %get-tuple-element.133), channel_id=1, source_target_pairs={{0,2},{2,4},{4,6},{6,7},{7,5},{5,3},{3,1},{1,0},{8,10},{10,12},{12... | collective-permute-start | bytes 393224 | tf_op jit(solution)/shard_map/ppermute | solution.py:506
  65.2 2.9 %shard_map.156 = (bf16[32,2048]{1,0:T(8,128)(2,1)S(1)}, bf16[32,2048]{1,0:T(8,128)(2,1)S(1)}, bf16[64,2048]{1,0:T(8,128)(2,1)S(1)}) custom-call(s32[2]{0:T(128)S(1)} %pad_add_fusion.refs_0_, bf16[64,2176]{1,0:T(8,128)(2,1)S(1)} %get-tuple-element.102.refs_0_.refs_1_, bf16[32,2176]{1,0:T(8,128)(2,1)S(1)} %collective-permute-done.20.refs_2_, ...), custom_call_target="tpu_custom_call" | custom-call | flops 55364812800 | bytes 1048576 | tf_op jit(solution)/shard_map/pallas_call | solution.py:354
  70.5 3.9 %collective-permute-start.32 = (bf16[32,2048]{1,0:T(8,128)(2,1)S(1)}, bf16[32,2048]{1,0:T(8,128)(2,1)S(1)}, u32[]{:S(2)}, u32[]{:S(2)}) collective-permute-start(bf16[32,2048]{1,0:T(8,128)(2,1)S(1)} %get-tuple-element.135), channel_id=1, source_target_pairs={{0,6},{2,7},{4,5},{6,3},{7,1},{5,0},{3,2},{1,4},{8,14},{10,15},{12... | collective-permute-start | bytes 393224 | tf_op jit(solution)/shard_map/ppermute | solution.py:500
  76.6 4.8 %collective-permute-start.30 = (bf16[32,2048]{1,0:T(8,128)(2,1)S(1)}, bf16[32,2048]{1,0:T(8,128)(2,1)S(1)}, u32[]{:S(2)}, u32[]{:S(2)}) collective-permute-start(bf16[32,2048]{1,0:T(8,128)(2,1)S(1)} %add_convert_fusion.4), channel_id=1, source_target_pairs={{0,7},{2,5},{4,3},{6,1},{7,0},{5,2},{3,4},{1,6},{8,15},{10,13},{12... | collective-permute-start | bytes 393224 | tf_op jit(solution)/shard_map/ppermute | solution.py:500
  82.5 2.6 %collective-permute-done.29 = bf16[32,2048]{1,0:T(8,128)(2,1)S(1)} collective-permute-done((bf16[32,2048]{1,0:T(8,128)(2,1)S(1)}, bf16[32,2048]{1,0:T(8,128)(2,1)S(1)}, u32[]{:S(2)}, u32[]{:S(2)}) %collective-permute-start.29) | collective-permute-done | bytes 131104 | tf_op jit(solution)/shard_map/ppermute | solution.py:507
  86.0 4.2 %collective-permute-done.34 = bf16[32,2048]{1,0:T(8,128)(2,1)S(1)} collective-permute-done((bf16[32,2048]{1,0:T(8,128)(2,1)S(1)}, bf16[32,2048]{1,0:T(8,128)(2,1)S(1)}, u32[]{:S(2)}, u32[]{:S(2)}) %collective-permute-start.34) | collective-permute-done | bytes 131104 | tf_op jit(solution)/shard_map/ppermute | solution.py:518
  (101 shorter events, 30.2 us)
Async XLA Ops:
  3.0 21.6 %collective-permute-start.10 = (bf16[352,2048]{1,0:T(8,128)(2,1)}, bf16[352,2048]{1,0:T(8,128)(2,1)}, u32[]{:S(2)}, u32[]{:S(2)}) collective-permute-start(bf16[352,2048]{1,0:T(8,128)(2,1)} %bitcast.18), channel_id=1, source_target_pairs={{0,8},{8,0},{16,24},{24,16},{1,9},{9,1},{17,25},{25,17},{2,10},{10... | collective-permute-start | bytes 4325384 | tf_op jit(solution)/shard_map/ppermute | solution.py:414
  3.0 22.1 %collective-permute-start.9 = (bf16[352,2048]{1,0:T(8,128)(2,1)}, bf16[352,2048]{1,0:T(8,128)(2,1)}, u32[]{:S(2)}, u32[]{:S(2)}) collective-permute-start(bf16[352,2048]{1,0:T(8,128)(2,1)} %bitcast.16), channel_id=1, source_target_pairs={{0,8},{8,0},{16,24},{24,16},{1,9},{9,1},{17,25},{25,17},{2,10},{10... | collective-permute-start | bytes 4325384 | tf_op jit(solution)/shard_map/ppermute | solution.py:414
  23.2 12.6 %collective-permute-start.12 = (bf16[352,2048]{1,0:T(8,128)(2,1)S(1)}, bf16[352,2048]{1,0:T(8,128)(2,1)}, u32[]{:S(2)}, u32[]{:S(2)}) collective-permute-start(bf16[352,2048]{1,0:T(8,128)(2,1)S(1)} %bitcast.15), channel_id=1, source_target_pairs={{0,8},{8,0},{16,24},{24,16},{1,9},{9,1},{17,25},{25,17},{2,10},{10... | collective-permute-start | bytes 4325384 | tf_op jit(solution)/shard_map/ppermute | solution.py:414
  23.5 12.7 %collective-permute-start.13 = (bf16[352,2048]{1,0:T(8,128)(2,1)}, bf16[352,2048]{1,0:T(8,128)(2,1)}, u32[]{:S(2)}, u32[]{:S(2)}) collective-permute-start(bf16[352,2048]{1,0:T(8,128)(2,1)} %bitcast.12.refs_3_), channel_id=1, source_target_pairs={{0,8},{8,0},{16,24},{24,16},{1,9},{9,1},{17,25},{25,17},{2,10},{10... | collective-permute-start | bytes 4325384 | tf_op jit(solution)/shard_map/ppermute | solution.py:414
  24.5 11.6 %collective-permute-start.14 = (bf16[352,2048]{1,0:T(8,128)(2,1)}, bf16[352,2048]{1,0:T(8,128)(2,1)}, u32[]{:S(2)}, u32[]{:S(2)}) collective-permute-start(bf16[352,2048]{1,0:T(8,128)(2,1)} %refs_5_.1), channel_id=1, source_target_pairs={{0,8},{8,0},{16,24},{24,16},{1,9},{9,1},{17,25},{25,17},{2,10},{10... | collective-permute-start | bytes 4325384 | tf_op jit(solution)/shard_map/ppermute | solution.py:414
  24.6 19.4 %collective-permute-start.17 = (bf16[352,2048]{1,0:T(8,128)(2,1)}, bf16[352,2048]{1,0:T(8,128)(2,1)}, u32[]{:S(2)}, u32[]{:S(2)}) collective-permute-start(bf16[352,2048]{1,0:T(8,128)(2,1)} %bitcast.13.refs_5_), channel_id=1, source_target_pairs={{0,8},{8,0},{16,24},{24,16},{1,9},{9,1},{17,25},{25,17},{2,10},{10... | collective-permute-start | bytes 4325384 | tf_op jit(solution)/shard_map/ppermute | solution.py:414
  25.2 8.4 %collective-permute-start.8 = (bf16[64,2048]{1,0:T(8,128)(2,1)S(1)}, bf16[64,2048]{1,0:T(8,128)(2,1)S(1)}, u32[]{:S(2)}, u32[]{:S(2)}) collective-permute-start(bf16[64,2048]{1,0:T(8,128)(2,1)S(1)} %add_convert_fusion.refs_0_), channel_id=1, source_target_pairs={{0,16},{8,24},{16,0},{24,8},{1,17},{9,25},{17,1},{25,9},{2,18},{10... | collective-permute-start | bytes 786440 | tf_op jit(solution)/shard_map/ppermute | solution.py:438
  34.0 8.0 %collective-permute-start.11 = (bf16[64,2176]{1,0:T(8,128)(2,1)S(1)}, bf16[64,2176]{1,0:T(8,128)(2,1)S(1)}, u32[]{:S(2)}, u32[]{:S(2)}) collective-permute-start(bf16[64,2176]{1,0:T(8,128)(2,1)S(1)} %get-tuple-element.102.refs_0_.refs_1_), channel_id=1, source_target_pairs={{0,2},{2,4},{4,6},{6,7},{7,5},{5,3},{3,1},{1,0},{8,10},{10,12},{12... | collective-permute-start | bytes 835592 | tf_op jit(solution)/shard_map/ppermute | solution.py:475
  35.8 7.9 %collective-permute-start.16 = (bf16[64,2176]{1,0:T(8,128)(2,1)S(1)}, bf16[64,2176]{1,0:T(8,128)(2,1)S(1)}, u32[]{:S(2)}, u32[]{:S(2)}) collective-permute-start(bf16[64,2176]{1,0:T(8,128)(2,1)S(1)} %get-tuple-element.102.refs_0_.refs_1_), channel_id=1, source_target_pairs={{2,0},{4,2},{6,4},{7,6},{5,7},{3,5},{1,3},{0,1},{10,8},{12,10},{14... | collective-permute-start | bytes 835592 | tf_op jit(solution)/shard_map/ppermute | solution.py:476
  42.0 7.1 %collective-permute-start.15 = (bf16[64,2176]{1,0:T(8,128)(2,1)S(1)}, bf16[64,2176]{1,0:T(8,128)(2,1)S(1)}, u32[]{:S(2)}, u32[]{:S(2)}) collective-permute-start(bf16[64,2176]{1,0:T(8,128)(2,1)S(1)} %collective-permute-done.11.refs_1_), channel_id=1, source_target_pairs={{0,2},{2,4},{4,6},{6,7},{7,5},{5,3},{3,1},{1,0},{8,10},{10,12},{12... | collective-permute-start | bytes 835592 | tf_op jit(solution)/shard_map/ppermute | solution.py:475
  47.1 16.0 %collective-permute-start.22 = (bf16[64,2048]{1,0:T(8,128)(2,1)S(1)}, bf16[64,2048]{1,0:T(8,128)(2,1)S(1)}, u32[]{:S(2)}, u32[]{:S(2)}) collective-permute-start(bf16[64,2048]{1,0:T(8,128)(2,1)S(1)} %get-tuple-element.115), channel_id=1, source_target_pairs={{0,16},{8,24},{16,0},{24,8},{1,17},{9,25},{17,1},{25,9},{2,18},{10... | collective-permute-start | bytes 786440 | tf_op jit(solution)/shard_map/ppermute | solution.py:458
  49.1 7.1 %collective-permute-start.18 = (bf16[64,2176]{1,0:T(8,128)(2,1)S(1)}, bf16[64,2176]{1,0:T(8,128)(2,1)S(1)}, u32[]{:S(2)}, u32[]{:S(2)}) collective-permute-start(bf16[64,2176]{1,0:T(8,128)(2,1)S(1)} %collective-permute-done.15.refs_1_), channel_id=1, source_target_pairs={{0,2},{2,4},{4,6},{6,7},{7,5},{5,3},{3,1},{1,0},{8,10},{10,12},{12... | collective-permute-start | bytes 835592 | tf_op jit(solution)/shard_map/ppermute | solution.py:475
  50.6 7.4 %collective-permute-start.21 = (bf16[64,2176]{1,0:T(8,128)(2,1)S(1)}, bf16[64,2176]{1,0:T(8,128)(2,1)S(1)}, u32[]{:S(2)}, u32[]{:S(2)}) collective-permute-start(bf16[64,2176]{1,0:T(8,128)(2,1)S(1)} %collective-permute-done.19.refs_2_), channel_id=1, source_target_pairs={{2,0},{4,2},{6,4},{7,6},{5,7},{3,5},{1,3},{0,1},{10,8},{12,10},{14... | collective-permute-start | bytes 835592 | tf_op jit(solution)/shard_map/ppermute | solution.py:476
  54.0 9.1 %collective-permute-start.23 = (bf16[64,2048]{1,0:T(8,128)(2,1)S(1)}, bf16[64,2048]{1,0:T(8,128)(2,1)S(1)}, u32[]{:S(2)}, u32[]{:S(2)}) collective-permute-start(bf16[64,2048]{1,0:T(8,128)(2,1)S(1)} %get-tuple-element.116), channel_id=1, source_target_pairs={{0,16},{8,24},{16,0},{24,8},{1,17},{9,25},{17,1},{25,9},{2,18},{10... | collective-permute-start | bytes 786440 | tf_op jit(solution)/shard_map/ppermute | solution.py:458
  58.1 7.2 %collective-permute-start.24 = (bf16[32,2176]{1,0:T(8,128)(2,1)S(1)}, bf16[32,2176]{1,0:T(8,128)(2,1)S(1)}, u32[]{:S(2)}, u32[]{:S(2)}) collective-permute-start(bf16[32,2176]{1,0:T(8,128)(2,1)S(1)} %slice.40), channel_id=1, source_target_pairs={{2,0},{4,2},{6,4},{7,6},{5,7},{3,5},{1,3},{0,1},{10,8},{12,10},{14... | collective-permute-start | bytes 417800 | tf_op jit(solution)/shard_map/ppermute | solution.py:481
  61.4 9.0 %collective-permute-start.31 = (bf16[64,2048]{1,0:T(8,128)(2,1)S(1)}, bf16[64,2048]{1,0:T(8,128)(2,1)S(1)}, u32[]{:S(2)}, u32[]{:S(2)}) collective-permute-start(bf16[64,2048]{1,0:T(8,128)(2,1)S(1)} %get-tuple-element.123), channel_id=1, source_target_pairs={{0,16},{8,24},{16,0},{24,8},{1,17},{9,25},{17,1},{25,9},{2,18},{10... | collective-permute-start | bytes 786440 | tf_op jit(solution)/shard_map/ppermute | solution.py:458
  63.2 11.2 %collective-permute-start.26 = (bf16[32,2048]{1,0:T(8,128)(2,1)S(1)}, bf16[32,2048]{1,0:T(8,128)(2,1)S(1)}, u32[]{:S(2)}, u32[]{:S(2)}) collective-permute-start(bf16[32,2048]{1,0:T(8,128)(2,1)S(1)} %get-tuple-element.133), channel_id=1, source_target_pairs={{0,2},{2,4},{4,6},{6,7},{7,5},{5,3},{3,1},{1,0},{8,10},{10,12},{12... | collective-permute-start | bytes 393224 | tf_op jit(solution)/shard_map/ppermute | solution.py:506
  64.8 9.6 %collective-permute-start.28 = (bf16[32,2048]{1,0:T(8,128)(2,1)S(1)}, bf16[32,2048]{1,0:T(8,128)(2,1)S(1)}, u32[]{:S(2)}, u32[]{:S(2)}) collective-permute-start(bf16[32,2048]{1,0:T(8,128)(2,1)S(1)} %get-tuple-element.134), channel_id=1, source_target_pairs={{2,0},{4,2},{6,4},{7,6},{5,7},{3,5},{1,3},{0,1},{10,8},{12,10},{14... | collective-permute-start | bytes 393224 | tf_op jit(solution)/shard_map/ppermute | solution.py:507
  68.2 8.4 %collective-permute-start.25 = (bf16[64,2048]{1,0:T(8,128)(2,1)S(1)}, bf16[64,2048]{1,0:T(8,128)(2,1)S(1)}, u32[]{:S(2)}, u32[]{:S(2)}) collective-permute-start(bf16[64,2048]{1,0:T(8,128)(2,1)S(1)} %get-tuple-element.119), channel_id=1, source_target_pairs={{0,16},{8,24},{16,0},{24,8},{1,17},{9,25},{17,1},{25,9},{2,18},{10... | collective-permute-start | bytes 786440 | tf_op jit(solution)/shard_map/ppermute | solution.py:458
  70.5 12.0 %collective-permute-start.32 = (bf16[32,2048]{1,0:T(8,128)(2,1)S(1)}, bf16[32,2048]{1,0:T(8,128)(2,1)S(1)}, u32[]{:S(2)}, u32[]{:S(2)}) collective-permute-start(bf16[32,2048]{1,0:T(8,128)(2,1)S(1)} %get-tuple-element.135), channel_id=1, source_target_pairs={{0,6},{2,7},{4,5},{6,3},{7,1},{5,0},{3,2},{1,4},{8,14},{10,15},{12... | collective-permute-start | bytes 393224 | tf_op jit(solution)/shard_map/ppermute | solution.py:500
  74.4 8.1 %collective-permute-start.33 = (bf16[32,2048]{1,0:T(8,128)(2,1)S(1)}, bf16[32,2048]{1,0:T(8,128)(2,1)S(1)}, u32[]{:S(2)}, u32[]{:S(2)}) collective-permute-start(bf16[32,2048]{1,0:T(8,128)(2,1)S(1)} %get-tuple-element.136), channel_id=1, source_target_pairs={{0,5},{2,3},{4,1},{6,0},{7,2},{5,4},{3,6},{1,7},{8,13},{10,11},{12... | collective-permute-start | bytes 393224 | tf_op jit(solution)/shard_map/ppermute | solution.py:500
  74.5 8.0 %collective-permute-start.27 = (bf16[32,2048]{1,0:T(8,128)(2,1)S(1)}, bf16[32,2048]{1,0:T(8,128)(2,1)S(1)}, u32[]{:S(2)}, u32[]{:S(2)}) collective-permute-start(bf16[32,2048]{1,0:T(8,128)(2,1)S(1)} %get-tuple-element.131), channel_id=1, source_target_pairs={{0,2},{2,4},{4,6},{6,7},{7,5},{5,3},{3,1},{1,0},{8,10},{10,12},{12... | collective-permute-start | bytes 393224 | tf_op jit(solution)/shard_map/ppermute | solution.py:506
  76.1 9.0 %collective-permute-start.29 = (bf16[32,2048]{1,0:T(8,128)(2,1)S(1)}, bf16[32,2048]{1,0:T(8,128)(2,1)S(1)}, u32[]{:S(2)}, u32[]{:S(2)}) collective-permute-start(bf16[32,2048]{1,0:T(8,128)(2,1)S(1)} %get-tuple-element.132), channel_id=1, source_target_pairs={{2,0},{4,2},{6,4},{7,6},{5,7},{3,5},{1,3},{0,1},{10,8},{12,10},{14... | collective-permute-start | bytes 393224 | tf_op jit(solution)/shard_map/ppermute | solution.py:507
  76.6 8.4 %collective-permute-start.30 = (bf16[32,2048]{1,0:T(8,128)(2,1)S(1)}, bf16[32,2048]{1,0:T(8,128)(2,1)S(1)}, u32[]{:S(2)}, u32[]{:S(2)}) collective-permute-start(bf16[32,2048]{1,0:T(8,128)(2,1)S(1)} %add_convert_fusion.4), channel_id=1, source_target_pairs={{0,7},{2,5},{4,3},{6,1},{7,0},{5,2},{3,4},{1,6},{8,15},{10,13},{12... | collective-permute-start | bytes 393224 | tf_op jit(solution)/shard_map/ppermute | solution.py:500
  (23 other events, 123.1 us)

commit v6 on v5

--- a/solution.py
+++ b/solution.py
@@ -455,7 +455,13 @@
     def work(blocks, shared=None):
         nonlocal staged
         keeps, send, staged = expert([b for _, b in blocks], staged, n, place, shared)
-        got = lax.ppermute(send, "req", across)
+        if shared is None:
+            got = lax.ppermute(send, "req", across)
+        else:
+            got = [
+                lax.ppermute(send[i * quarter : (i + 1) * quarter], "req", across)
+                for i in range(len(blocks))
+            ]
         for (d, _), keep in zip(blocks, keeps):
             own[d] = keep
         return keeps, ([d for d, _ in blocks], got)
@@ -482,8 +488,8 @@
     low, before = landed(steps, low, before)
     last, on_way[steps] = work([(0, [normed]), (steps, [low, high])], shared_part)
     (last,) = landed(steps + 1, last)
-    for i, d in enumerate(on_way[steps][0]):
-        summand[d] = on_way[steps][1][i * quarter : (i + 1) * quarter]
+    for d, got in zip(*on_way[steps]):
+        summand[d] = got
 
     def part(d):
         return own[d].astype(f32) + summand[d].astype(f32)

time: 92.9 us -> 93.2 us (level)
  waiting for transfers between devices: 16.9 us -> 15.9 us
    ppermute x0 -> x2, starting transfers between devices: none -> 2.09 us  [work(): lax.ppermute(send[i * quarter:(i + 1) * quarter], 'req', across)]
    ppermute x4 -> x3, starting transfers between devices: 6.17 us -> 4.89 us  [work(): got = lax.ppermute(send, 'req', across)]
  transfers between devices with their start and end apart: 36 -> 37, of which waited for: 15 -> 16; matrix products, arithmetic and copies ran while one was open for 1% -> 1% of each run, Pallas kernels for 32% -> 32%
where the time goes in v6:
time: 93.2 us; the launch traced here: 92.7 us
  starting transfers between devices  41.3 us (44%)
  Pallas kernels  29.3 us (31%)
  waiting for transfers between devices  15.9 us (17%)
  local copies, waits for them, and re-layouts  5.23 us (6%)
    ppermute x7, starting transfers between devices, on_device_ring(): from_left = lax.ppermute(from_left, 'exp', right)  13.5 us
    pallas_call x4, Pallas kernels, expert(): pl.pallas_call(functools.partial(expert_kernel, n_experts, counts, shared...  11.9 us
    pallas_call x5, Pallas kernels, attend(): pl.pallas_call(functools.partial(attend_kernel, heads, tokens, page_len,...  9.41 us
    ppermute x3, starting transfers between devices, on_device_ring(): lax.ppermute(part(block).astype(bf16), 'exp', along(sign * d))  8.7 us
    ppermute x7, waiting for transfers between devices, on_device_ring(): from_left = lax.ppermute(from_left, 'exp', right)  5.13 us
    pallas_call x1, Pallas kernels, shared_expert(): pl.pallas_call(functools.partial(shared_kernel, len(rows)), out_shape=jax...  4.98 us
    ppermute x3, starting transfers between devices, work(): got = lax.ppermute(send, 'req', across)  4.89 us
    unnamed x24, local copies, waits for them, and re-layouts  4.25 us
  transfers between devices with their start and end apart: 37, of which 16 were waited for; matrix products, arithmetic and copies ran while one was open for 1% of the time, Pallas kernels for 32%

profile of v6, /device:TPU:0, one launch (start us, length us, event | category | flops | bytes accessed | tf_op | source)
XLA Modules:
  0.0 92.7 jit_solution(1215544125517359050)
XLA Ops:
  0.0 3.0 %collective-permute-start = (bf16[256,256]{1,0:T(8,128)(2,1)}, bf16[256,256]{1,0:T(8,128)(2,1)S(1)}, u32[]{:S(2)}, u32[]{:S(2)}) collective-permute-start(bf16[256,256]{1,0:T(8,128)(2,1)} %bitcast.20), channel_id=1, source_target_pairs={{0,2},{2,4},{4,6},{6,7},{7,5},{5,3},{3,1},{1,0},{8,10},{10,12},{12... | collective-permute-start | bytes 393224 | tf_op jit(solution)/shard_map/ppermute | solution.py:424
  6.7 1.8 %collective-permute-start.1 = (bf16[256,256]{1,0:T(8,128)(2,1)S(1)}, bf16[256,256]{1,0:T(8,128)(2,1)S(1)}, u32[]{:S(2)}, u32[]{:S(2)}) collective-permute-start(bf16[256,256]{1,0:T(8,128)(2,1)S(1)} %collective-permute-done.refs_4_), channel_id=1, source_target_pairs={{0,2},{2,4},{4,6},{6,7},{7,5},{5,3},{3,1},{1,0},{8,10},{10,12},{12... | collective-permute-start | bytes 393224 | tf_op jit(solution)/shard_map/ppermute | solution.py:424
  8.7 1.9 %shard_map.146 = (f32[512,128]{1,0:T(8,128)S(1)}, f32[512,128]{1,0:T(8,128)S(1)}, f32[512,128]{1,0:T(8,128)S(1)}) custom-call(bf16[512,128]{1,0:T(8,128)(2,1)S(1)} %get-tuple-element.66.refs_0_, f32[512,128]{1,0:T(8,128)S(1)} %get-tuple-element.71.refs_1_, f32[512,128]{1,0:T(8,128)S(1)} %get-tuple-element.72.refs_2_, ...), custom_call_target="tpu_custom_call" | custom-call | flops 6710886400 | bytes 393216 | tf_op jit(solution)/shard_map/pallas_call | solution.py:152
  11.6 1.8 %collective-permute-start.3 = (bf16[256,256]{1,0:T(8,128)(2,1)S(1)}, bf16[256,256]{1,0:T(8,128)(2,1)S(1)}, u32[]{:S(2)}, u32[]{:S(2)}) collective-permute-start(bf16[256,256]{1,0:T(8,128)(2,1)S(1)} %collective-permute-done.1.refs_4_), channel_id=1, source_target_pairs={{0,2},{2,4},{4,6},{6,7},{7,5},{5,3},{3,1},{1,0},{8,10},{10,12},{12... | collective-permute-start | bytes 393224 | tf_op jit(solution)/shard_map/ppermute | solution.py:424
  13.7 1.9 %shard_map.147 = (f32[512,128]{1,0:T(8,128)S(1)}, f32[512,128]{1,0:T(8,128)S(1)}, f32[512,128]{1,0:T(8,128)S(1)}) custom-call(bf16[512,128]{1,0:T(8,128)(2,1)S(1)} %get-tuple-element.66.refs_0_, f32[512,128]{1,0:T(8,128)S(1)} %get-tuple-element.78.refs_1_, f32[512,128]{1,0:T(8,128)S(1)} %get-tuple-element.79.refs_2_, ...), custom_call_target="tpu_custom_call" | custom-call | flops 6710886400 | bytes 393216 | tf_op jit(solution)/shard_map/pallas_call | solution.py:152
  16.9 1.8 %collective-permute-start.5 = (bf16[256,256]{1,0:T(8,128)(2,1)S(1)}, bf16[256,256]{1,0:T(8,128)(2,1)S(1)}, u32[]{:S(2)}, u32[]{:S(2)}) collective-permute-start(bf16[256,256]{1,0:T(8,128)(2,1)S(1)} %collective-permute-done.3.refs_5_), channel_id=1, source_target_pairs={{0,2},{2,4},{4,6},{6,7},{7,5},{5,3},{3,1},{1,0},{8,10},{10,12},{12... | collective-permute-start | bytes 393224 | tf_op jit(solution)/shard_map/ppermute | solution.py:431
  18.7 3.0 %shard_map.148 = (f32[512,128]{1,0:T(8,128)S(1)}, f32[512,128]{1,0:T(8,128)S(1)}, f32[512,128]{1,0:T(8,128)S(1)}, bf16[512,2048]{1,0:T(8,128)(2,1)S(1)}) custom-call(bf16[512,128]{1,0:T(8,128)(2,1)S(1)} %get-tuple-element.66.refs_0_, f32[512,128]{1,0:T(8,128)S(1)} %get-tuple-element.85.refs_1_, f32[512,128]{1,0:T(8,128)S(1)} %get-tuple-element.86.refs_2_, ...), custom_call_target="tpu_custom_call" | custom-call | flops 134217728 | bytes 393216 | tf_op jit(solution)/shard_map/pallas_call | solution.py:152
  25.2 1.8 %collective-permute-start.8 = (bf16[64,2048]{1,0:T(8,128)(2,1)S(1)}, bf16[64,2048]{1,0:T(8,128)(2,1)S(1)}, u32[]{:S(2)}, u32[]{:S(2)}) collective-permute-start(bf16[64,2048]{1,0:T(8,128)(2,1)S(1)} %add_convert_fusion.refs_0_), channel_id=1, source_target_pairs={{0,16},{8,24},{16,0},{24,8},{1,17},{9,25},{17,1},{25,9},{2,18},{10... | collective-permute-start | bytes 786440 | tf_op jit(solution)/shard_map/ppermute | solution.py:438
  27.3 2.7 %shard_map.150 = (bf16[704,2048]{1,0:T(8,128)(2,1)S(1)}, bf16[704,2048]{1,0:T(8,128)(2,1)S(1)}) custom-call(bf16[352,2048]{1,0:T(8,128)(2,1)} %bitcast.17, bf16[352,2048]{1,0:T(8,128)(2,1)} %collective-permute-done.9.refs_1_, bf16[352,2048]{1,0:T(8,128)(2,1)} %bitcast.19, bf16[352,2048]{1,0:T(8,128)(2,1)} %collective-permute-done.10.refs_3_), custom_call_target="tpu_custom_call" | custom-call | bytes 5767168 | tf_op jit(solution)/shard_map/pallas_call | solution.py:229
  34.0 1.8 %collective-permute-start.11 = (bf16[64,2176]{1,0:T(8,128)(2,1)S(1)}, bf16[64,2176]{1,0:T(8,128)(2,1)S(1)}, u32[]{:S(2)}, u32[]{:S(2)}) collective-permute-start(bf16[64,2176]{1,0:T(8,128)(2,1)S(1)} %get-tuple-element.102.refs_0_.refs_1_), channel_id=1, source_target_pairs={{0,2},{2,4},{4,6},{6,7},{7,5},{5,3},{3,1},{1,0},{8,10},{10,12},{12... | collective-permute-start | bytes 835592 | tf_op jit(solution)/shard_map/ppermute | solution.py:481
  36.1 5.0 %shard_map.152.refs_4_ = f32[64,2048]{1,0:T(8,128)S(1)} custom-call(bf16[64,2176]{1,0:T(8,128)(2,1)S(1)} %get-tuple-element.102.refs_0_.refs_1_, bf16[352,2048]{1,0:T(8,128)(2,1)} %bitcast.14, bf16[352,2048]{1,0:T(8,128)(2,1)} %collective-permute-done.12.refs_2_, bf16[352,2048]{1,0:T(8,128)(2,1)} %bitcast.12.refs_3_, ...), custom_call_target="tpu_custom_call" | custom-call | flops 553648128 | bytes 8650752 | tf_op jit(solution)/shard_map/pallas_call | solution.py:276
  42.0 1.7 %collective-permute-start.15 = (bf16[64,2176]{1,0:T(8,128)(2,1)S(1)}, bf16[64,2176]{1,0:T(8,128)(2,1)S(1)}, u32[]{:S(2)}, u32[]{:S(2)}) collective-permute-start(bf16[64,2176]{1,0:T(8,128)(2,1)S(1)} %collective-permute-done.11.refs_1_), channel_id=1, source_target_pairs={{0,2},{2,4},{4,6},{6,7},{7,5},{5,3},{3,1},{1,0},{8,10},{10,12},{12... | collective-permute-start | bytes 835592 | tf_op jit(solution)/shard_map/ppermute | solution.py:481
  44.0 3.1 %shard_map.153 = (bf16[32,2048]{1,0:T(8,128)(2,1)S(1)}, bf16[32,2048]{1,0:T(8,128)(2,1)S(1)}, bf16[64,2048]{1,0:T(8,128)(2,1)S(1)}, bf16[704,2048]{1,0:T(8,128)(2,1)S(1)}) custom-call(s32[2]{0:T(128)S(1)} %pad_add_fusion.refs_0_, bf16[64,2176]{1,0:T(8,128)(2,1)S(1)} %collective-permute-done.11.refs_1_, bf16[64,2176]{1,0:T(8,128)(2,1)S(1)} %collective-permute-done.16.refs_2_, ...), custom_call_target="tpu_custom_call" | custom-call | flops 55364812800 | bytes 1048576 | tf_op jit(solution)/shard_map/pallas_call | solution.py:354
  47.1 1.7 %collective-permute-start.22 = (bf16[64,2048]{1,0:T(8,128)(2,1)S(1)}, bf16[64,2048]{1,0:T(8,128)(2,1)S(1)}, u32[]{:S(2)}, u32[]{:S(2)}) collective-permute-start(bf16[64,2048]{1,0:T(8,128)(2,1)S(1)} %get-tuple-element.115), channel_id=1, source_target_pairs={{0,16},{8,24},{16,0},{24,8},{1,17},{9,25},{17,1},{25,9},{2,18},{10... | collective-permute-start | bytes 786440 | tf_op jit(solution)/shard_map/ppermute | solution.py:459
  51.1 2.9 %shard_map.154 = (bf16[32,2048]{1,0:T(8,128)(2,1)S(1)}, bf16[32,2048]{1,0:T(8,128)(2,1)S(1)}, bf16[64,2048]{1,0:T(8,128)(2,1)S(1)}) custom-call(s32[2]{0:T(128)S(1)} %pad_add_fusion.refs_0_, bf16[64,2176]{1,0:T(8,128)(2,1)S(1)} %collective-permute-done.15.refs_1_, bf16[64,2176]{1,0:T(8,128)(2,1)S(1)} %collective-permute-done.19.refs_2_, ...), custom_call_target="tpu_custom_call" | custom-call | flops 55364812800 | bytes 1048576 | tf_op jit(solution)/shard_map/pallas_call | solution.py:354
  56.2 1.7 %collective-permute-start.20 = (bf16[32,2176]{1,0:T(8,128)(2,1)S(1)}, bf16[32,2176]{1,0:T(8,128)(2,1)S(1)}, u32[]{:S(2)}, u32[]{:S(2)}) collective-permute-start(bf16[32,2176]{1,0:T(8,128)(2,1)S(1)} %slice.30), channel_id=1, source_target_pairs={{0,2},{2,4},{4,6},{6,7},{7,5},{5,3},{3,1},{1,0},{8,10},{10,12},{12... | collective-permute-start | bytes 417800 | tf_op jit(solution)/shard_map/ppermute | solution.py:486
  58.5 2.9 %shard_map.155 = (bf16[32,2048]{1,0:T(8,128)(2,1)S(1)}, bf16[32,2048]{1,0:T(8,128)(2,1)S(1)}, bf16[64,2048]{1,0:T(8,128)(2,1)S(1)}) custom-call(s32[2]{0:T(128)S(1)} %pad_add_fusion.refs_0_, bf16[64,2176]{1,0:T(8,128)(2,1)S(1)} %collective-permute-done.18.refs_1_, bf16[64,2176]{1,0:T(8,128)(2,1)S(1)} %collective-permute-done.21.refs_2_, ...), custom_call_target="tpu_custom_call" | custom-call | flops 55364812800 | bytes 1048576 | tf_op jit(solution)/shard_map/pallas_call | solution.py:354
  61.4 1.7 %collective-permute-start.32 = (bf16[64,2048]{1,0:T(8,128)(2,1)S(1)}, bf16[64,2048]{1,0:T(8,128)(2,1)S(1)}, u32[]{:S(2)}, u32[]{:S(2)}) collective-permute-start(bf16[64,2048]{1,0:T(8,128)(2,1)S(1)} %get-tuple-element.123), channel_id=1, source_target_pairs={{0,16},{8,24},{16,0},{24,8},{1,17},{9,25},{17,1},{25,9},{2,18},{10... | collective-permute-start | bytes 786440 | tf_op jit(solution)/shard_map/ppermute | solution.py:459
  63.2 1.6 %collective-permute-start.26 = (bf16[32,2048]{1,0:T(8,128)(2,1)S(1)}, bf16[32,2048]{1,0:T(8,128)(2,1)S(1)}, u32[]{:S(2)}, u32[]{:S(2)}) collective-permute-start(bf16[32,2048]{1,0:T(8,128)(2,1)S(1)} %get-tuple-element.135), channel_id=1, source_target_pairs={{0,2},{2,4},{4,6},{6,7},{7,5},{5,3},{3,1},{1,0},{8,10},{10,12},{12... | collective-permute-start | bytes 393224 | tf_op jit(solution)/shard_map/ppermute | solution.py:512
  65.2 2.9 %shard_map.156 = (bf16[32,2048]{1,0:T(8,128)(2,1)S(1)}, bf16[32,2048]{1,0:T(8,128)(2,1)S(1)}, bf16[64,2048]{1,0:T(8,128)(2,1)S(1)}) custom-call(s32[2]{0:T(128)S(1)} %pad_add_fusion.refs_0_, bf16[64,2176]{1,0:T(8,128)(2,1)S(1)} %get-tuple-element.102.refs_0_.refs_1_, bf16[32,2176]{1,0:T(8,128)(2,1)S(1)} %collective-permute-done.20.refs_2_, ...), custom_call_target="tpu_custom_call" | custom-call | flops 55364812800 | bytes 1048576 | tf_op jit(solution)/shard_map/pallas_call | solution.py:354
  70.5 3.9 %collective-permute-start.33 = (bf16[32,2048]{1,0:T(8,128)(2,1)S(1)}, bf16[32,2048]{1,0:T(8,128)(2,1)S(1)}, u32[]{:S(2)}, u32[]{:S(2)}) collective-permute-start(bf16[32,2048]{1,0:T(8,128)(2,1)S(1)} %get-tuple-element.137), channel_id=1, source_target_pairs={{0,6},{2,7},{4,5},{6,3},{7,1},{5,0},{3,2},{1,4},{8,14},{10,15},{12... | collective-permute-start | bytes 393224 | tf_op jit(solution)/shard_map/ppermute | solution.py:506
  76.6 4.8 %collective-permute-start.31 = (bf16[32,2048]{1,0:T(8,128)(2,1)S(1)}, bf16[32,2048]{1,0:T(8,128)(2,1)S(1)}, u32[]{:S(2)}, u32[]{:S(2)}) collective-permute-start(bf16[32,2048]{1,0:T(8,128)(2,1)S(1)} %add_convert_fusion.4), channel_id=1, source_target_pairs={{0,7},{2,5},{4,3},{6,1},{7,0},{5,2},{3,4},{1,6},{8,15},{10,13},{12... | collective-permute-start | bytes 393224 | tf_op jit(solution)/shard_map/ppermute | solution.py:506
  82.7 2.2 %collective-permute-done.29 = bf16[32,2048]{1,0:T(8,128)(2,1)S(1)} collective-permute-done((bf16[32,2048]{1,0:T(8,128)(2,1)S(1)}, bf16[32,2048]{1,0:T(8,128)(2,1)S(1)}, u32[]{:S(2)}, u32[]{:S(2)}) %collective-permute-start.29) | collective-permute-done | bytes 131104 | tf_op jit(solution)/shard_map/ppermute | solution.py:513
  86.1 4.1 %collective-permute-done.35 = bf16[32,2048]{1,0:T(8,128)(2,1)S(1)} collective-permute-done((bf16[32,2048]{1,0:T(8,128)(2,1)S(1)}, bf16[32,2048]{1,0:T(8,128)(2,1)S(1)}, u32[]{:S(2)}, u32[]{:S(2)}) %collective-permute-start.35) | collective-permute-done | bytes 131104 | tf_op jit(solution)/shard_map/ppermute | solution.py:524
  (104 shorter events, 30.6 us)
Async XLA Ops:
  3.0 21.6 %collective-permute-start.10 = (bf16[352,2048]{1,0:T(8,128)(2,1)}, bf16[352,2048]{1,0:T(8,128)(2,1)}, u32[]{:S(2)}, u32[]{:S(2)}) collective-permute-start(bf16[352,2048]{1,0:T(8,128)(2,1)} %bitcast.18), channel_id=1, source_target_pairs={{0,8},{8,0},{16,24},{24,16},{1,9},{9,1},{17,25},{25,17},{2,10},{10... | collective-permute-start | bytes 4325384 | tf_op jit(solution)/shard_map/ppermute | solution.py:414
  3.0 22.1 %collective-permute-start.9 = (bf16[352,2048]{1,0:T(8,128)(2,1)}, bf16[352,2048]{1,0:T(8,128)(2,1)}, u32[]{:S(2)}, u32[]{:S(2)}) collective-permute-start(bf16[352,2048]{1,0:T(8,128)(2,1)} %bitcast.16), channel_id=1, source_target_pairs={{0,8},{8,0},{16,24},{24,16},{1,9},{9,1},{17,25},{25,17},{2,10},{10... | collective-permute-start | bytes 4325384 | tf_op jit(solution)/shard_map/ppermute | solution.py:414
  23.2 12.6 %collective-permute-start.12 = (bf16[352,2048]{1,0:T(8,128)(2,1)S(1)}, bf16[352,2048]{1,0:T(8,128)(2,1)}, u32[]{:S(2)}, u32[]{:S(2)}) collective-permute-start(bf16[352,2048]{1,0:T(8,128)(2,1)S(1)} %bitcast.15), channel_id=1, source_target_pairs={{0,8},{8,0},{16,24},{24,16},{1,9},{9,1},{17,25},{25,17},{2,10},{10... | collective-permute-start | bytes 4325384 | tf_op jit(solution)/shard_map/ppermute | solution.py:414
  23.5 12.7 %collective-permute-start.13 = (bf16[352,2048]{1,0:T(8,128)(2,1)}, bf16[352,2048]{1,0:T(8,128)(2,1)}, u32[]{:S(2)}, u32[]{:S(2)}) collective-permute-start(bf16[352,2048]{1,0:T(8,128)(2,1)} %bitcast.12.refs_3_), channel_id=1, source_target_pairs={{0,8},{8,0},{16,24},{24,16},{1,9},{9,1},{17,25},{25,17},{2,10},{10... | collective-permute-start | bytes 4325384 | tf_op jit(solution)/shard_map/ppermute | solution.py:414
  24.5 11.6 %collective-permute-start.14 = (bf16[352,2048]{1,0:T(8,128)(2,1)}, bf16[352,2048]{1,0:T(8,128)(2,1)}, u32[]{:S(2)}, u32[]{:S(2)}) collective-permute-start(bf16[352,2048]{1,0:T(8,128)(2,1)} %refs_5_.1), channel_id=1, source_target_pairs={{0,8},{8,0},{16,24},{24,16},{1,9},{9,1},{17,25},{25,17},{2,10},{10... | collective-permute-start | bytes 4325384 | tf_op jit(solution)/shard_map/ppermute | solution.py:414
  24.6 19.4 %collective-permute-start.17 = (bf16[352,2048]{1,0:T(8,128)(2,1)}, bf16[352,2048]{1,0:T(8,128)(2,1)}, u32[]{:S(2)}, u32[]{:S(2)}) collective-permute-start(bf16[352,2048]{1,0:T(8,128)(2,1)} %bitcast.13.refs_5_), channel_id=1, source_target_pairs={{0,8},{8,0},{16,24},{24,16},{1,9},{9,1},{17,25},{25,17},{2,10},{10... | collective-permute-start | bytes 4325384 | tf_op jit(solution)/shard_map/ppermute | solution.py:414
  25.2 8.4 %collective-permute-start.8 = (bf16[64,2048]{1,0:T(8,128)(2,1)S(1)}, bf16[64,2048]{1,0:T(8,128)(2,1)S(1)}, u32[]{:S(2)}, u32[]{:S(2)}) collective-permute-start(bf16[64,2048]{1,0:T(8,128)(2,1)S(1)} %add_convert_fusion.refs_0_), channel_id=1, source_target_pairs={{0,16},{8,24},{16,0},{24,8},{1,17},{9,25},{17,1},{25,9},{2,18},{10... | collective-permute-start | bytes 786440 | tf_op jit(solution)/shard_map/ppermute | solution.py:438
  34.0 8.0 %collective-permute-start.11 = (bf16[64,2176]{1,0:T(8,128)(2,1)S(1)}, bf16[64,2176]{1,0:T(8,128)(2,1)S(1)}, u32[]{:S(2)}, u32[]{:S(2)}) collective-permute-start(bf16[64,2176]{1,0:T(8,128)(2,1)S(1)} %get-tuple-element.102.refs_0_.refs_1_), channel_id=1, source_target_pairs={{0,2},{2,4},{4,6},{6,7},{7,5},{5,3},{3,1},{1,0},{8,10},{10,12},{12... | collective-permute-start | bytes 835592 | tf_op jit(solution)/shard_map/ppermute | solution.py:481
  35.8 7.9 %collective-permute-start.16 = (bf16[64,2176]{1,0:T(8,128)(2,1)S(1)}, bf16[64,2176]{1,0:T(8,128)(2,1)S(1)}, u32[]{:S(2)}, u32[]{:S(2)}) collective-permute-start(bf16[64,2176]{1,0:T(8,128)(2,1)S(1)} %get-tuple-element.102.refs_0_.refs_1_), channel_id=1, source_target_pairs={{2,0},{4,2},{6,4},{7,6},{5,7},{3,5},{1,3},{0,1},{10,8},{12,10},{14... | collective-permute-start | bytes 835592 | tf_op jit(solution)/shard_map/ppermute | solution.py:482
  47.1 16.0 %collective-permute-start.22 = (bf16[64,2048]{1,0:T(8,128)(2,1)S(1)}, bf16[64,2048]{1,0:T(8,128)(2,1)S(1)}, u32[]{:S(2)}, u32[]{:S(2)}) collective-permute-start(bf16[64,2048]{1,0:T(8,128)(2,1)S(1)} %get-tuple-element.115), channel_id=1, source_target_pairs={{0,16},{8,24},{16,0},{24,8},{1,17},{9,25},{17,1},{25,9},{2,18},{10... | collective-permute-start | bytes 786440 | tf_op jit(solution)/shard_map/ppermute | solution.py:459
  49.1 7.1 %collective-permute-start.18 = (bf16[64,2176]{1,0:T(8,128)(2,1)S(1)}, bf16[64,2176]{1,0:T(8,128)(2,1)S(1)}, u32[]{:S(2)}, u32[]{:S(2)}) collective-permute-start(bf16[64,2176]{1,0:T(8,128)(2,1)S(1)} %collective-permute-done.15.refs_1_), channel_id=1, source_target_pairs={{0,2},{2,4},{4,6},{6,7},{7,5},{5,3},{3,1},{1,0},{8,10},{10,12},{12... | collective-permute-start | bytes 835592 | tf_op jit(solution)/shard_map/ppermute | solution.py:481
  50.6 7.4 %collective-permute-start.21 = (bf16[64,2176]{1,0:T(8,128)(2,1)S(1)}, bf16[64,2176]{1,0:T(8,128)(2,1)S(1)}, u32[]{:S(2)}, u32[]{:S(2)}) collective-permute-start(bf16[64,2176]{1,0:T(8,128)(2,1)S(1)} %collective-permute-done.19.refs_2_), channel_id=1, source_target_pairs={{2,0},{4,2},{6,4},{7,6},{5,7},{3,5},{1,3},{0,1},{10,8},{12,10},{14... | collective-permute-start | bytes 835592 | tf_op jit(solution)/shard_map/ppermute | solution.py:482
  54.0 9.0 %collective-permute-start.23 = (bf16[64,2048]{1,0:T(8,128)(2,1)S(1)}, bf16[64,2048]{1,0:T(8,128)(2,1)S(1)}, u32[]{:S(2)}, u32[]{:S(2)}) collective-permute-start(bf16[64,2048]{1,0:T(8,128)(2,1)S(1)} %get-tuple-element.116), channel_id=1, source_target_pairs={{0,16},{8,24},{16,0},{24,8},{1,17},{9,25},{17,1},{25,9},{2,18},{10... | collective-permute-start | bytes 786440 | tf_op jit(solution)/shard_map/ppermute | solution.py:459
  58.1 7.2 %collective-permute-start.24 = (bf16[32,2176]{1,0:T(8,128)(2,1)S(1)}, bf16[32,2176]{1,0:T(8,128)(2,1)S(1)}, u32[]{:S(2)}, u32[]{:S(2)}) collective-permute-start(bf16[32,2176]{1,0:T(8,128)(2,1)S(1)} %slice.40), channel_id=1, source_target_pairs={{2,0},{4,2},{6,4},{7,6},{5,7},{3,5},{1,3},{0,1},{10,8},{12,10},{14... | collective-permute-start | bytes 417800 | tf_op jit(solution)/shard_map/ppermute | solution.py:487
  61.4 9.0 %collective-permute-start.32 = (bf16[64,2048]{1,0:T(8,128)(2,1)S(1)}, bf16[64,2048]{1,0:T(8,128)(2,1)S(1)}, u32[]{:S(2)}, u32[]{:S(2)}) collective-permute-start(bf16[64,2048]{1,0:T(8,128)(2,1)S(1)} %get-tuple-element.123), channel_id=1, source_target_pairs={{0,16},{8,24},{16,0},{24,8},{1,17},{9,25},{17,1},{25,9},{2,18},{10... | collective-permute-start | bytes 786440 | tf_op jit(solution)/shard_map/ppermute | solution.py:459
  63.2 11.2 %collective-permute-start.26 = (bf16[32,2048]{1,0:T(8,128)(2,1)S(1)}, bf16[32,2048]{1,0:T(8,128)(2,1)S(1)}, u32[]{:S(2)}, u32[]{:S(2)}) collective-permute-start(bf16[32,2048]{1,0:T(8,128)(2,1)S(1)} %get-tuple-element.135), channel_id=1, source_target_pairs={{0,2},{2,4},{4,6},{6,7},{7,5},{5,3},{3,1},{1,0},{8,10},{10,12},{12... | collective-permute-start | bytes 393224 | tf_op jit(solution)/shard_map/ppermute | solution.py:512
  64.8 9.6 %collective-permute-start.28 = (bf16[32,2048]{1,0:T(8,128)(2,1)S(1)}, bf16[32,2048]{1,0:T(8,128)(2,1)S(1)}, u32[]{:S(2)}, u32[]{:S(2)}) collective-permute-start(bf16[32,2048]{1,0:T(8,128)(2,1)S(1)} %get-tuple-element.136), channel_id=1, source_target_pairs={{2,0},{4,2},{6,4},{7,6},{5,7},{3,5},{1,3},{0,1},{10,8},{12,10},{14... | collective-permute-start | bytes 393224 | tf_op jit(solution)/shard_map/ppermute | solution.py:513
  68.2 7.8 %collective-permute-start.30 = (bf16[32,2048]{1,0:T(8,128)(2,1)S(1)}, bf16[32,2048]{1,0:T(8,128)(2,1)S(1)}, u32[]{:S(2)}, u32[]{:S(2)}) collective-permute-start(bf16[32,2048]{1,0:T(8,128)(2,1)S(1)} %get-tuple-element.132), channel_id=1, source_target_pairs={{0,16},{8,24},{16,0},{24,8},{1,17},{9,25},{17,1},{25,9},{2,18},{10... | collective-permute-start | bytes 393224 | tf_op jit(solution)/shard_map/ppermute | solution.py:462
  69.5 7.1 %collective-permute-start.25 = (bf16[32,2048]{1,0:T(8,128)(2,1)S(1)}, bf16[32,2048]{1,0:T(8,128)(2,1)S(1)}, u32[]{:S(2)}, u32[]{:S(2)}) collective-permute-start(bf16[32,2048]{1,0:T(8,128)(2,1)S(1)} %get-tuple-element.131), channel_id=1, source_target_pairs={{0,16},{8,24},{16,0},{24,8},{1,17},{9,25},{17,1},{25,9},{2,18},{10... | collective-permute-start | bytes 393224 | tf_op jit(solution)/shard_map/ppermute | solution.py:462
  70.5 12.3 %collective-permute-start.33 = (bf16[32,2048]{1,0:T(8,128)(2,1)S(1)}, bf16[32,2048]{1,0:T(8,128)(2,1)S(1)}, u32[]{:S(2)}, u32[]{:S(2)}) collective-permute-start(bf16[32,2048]{1,0:T(8,128)(2,1)S(1)} %get-tuple-element.137), channel_id=1, source_target_pairs={{0,6},{2,7},{4,5},{6,3},{7,1},{5,0},{3,2},{1,4},{8,14},{10,15},{12... | collective-permute-start | bytes 393224 | tf_op jit(solution)/shard_map/ppermute | solution.py:506
  74.4 8.4 %collective-permute-start.34 = (bf16[32,2048]{1,0:T(8,128)(2,1)S(1)}, bf16[32,2048]{1,0:T(8,128)(2,1)S(1)}, u32[]{:S(2)}, u32[]{:S(2)}) collective-permute-start(bf16[32,2048]{1,0:T(8,128)(2,1)S(1)} %get-tuple-element.138), channel_id=1, source_target_pairs={{0,5},{2,3},{4,1},{6,0},{7,2},{5,4},{3,6},{1,7},{8,13},{10,11},{12... | collective-permute-start | bytes 393224 | tf_op jit(solution)/shard_map/ppermute | solution.py:506
  74.5 8.2 %collective-permute-start.27 = (bf16[32,2048]{1,0:T(8,128)(2,1)S(1)}, bf16[32,2048]{1,0:T(8,128)(2,1)S(1)}, u32[]{:S(2)}, u32[]{:S(2)}) collective-permute-start(bf16[32,2048]{1,0:T(8,128)(2,1)S(1)} %get-tuple-element.133), channel_id=1, source_target_pairs={{0,2},{2,4},{4,6},{6,7},{7,5},{5,3},{3,1},{1,0},{8,10},{10,12},{12... | collective-permute-start | bytes 393224 | tf_op jit(solution)/shard_map/ppermute | solution.py:512
  76.0 8.9 %collective-permute-start.29 = (bf16[32,2048]{1,0:T(8,128)(2,1)S(1)}, bf16[32,2048]{1,0:T(8,128)(2,1)S(1)}, u32[]{:S(2)}, u32[]{:S(2)}) collective-permute-start(bf16[32,2048]{1,0:T(8,128)(2,1)S(1)} %get-tuple-element.134), channel_id=1, source_target_pairs={{2,0},{4,2},{6,4},{7,6},{5,7},{3,5},{1,3},{0,1},{10,8},{12,10},{14... | collective-permute-start | bytes 393224 | tf_op jit(solution)/shard_map/ppermute | solution.py:513
  76.6 8.4 %collective-permute-start.31 = (bf16[32,2048]{1,0:T(8,128)(2,1)S(1)}, bf16[32,2048]{1,0:T(8,128)(2,1)S(1)}, u32[]{:S(2)}, u32[]{:S(2)}) collective-permute-start(bf16[32,2048]{1,0:T(8,128)(2,1)S(1)} %add_convert_fusion.4), channel_id=1, source_target_pairs={{0,7},{2,5},{4,3},{6,1},{7,0},{5,2},{3,4},{1,6},{8,15},{10,13},{12... | collective-permute-start | bytes 393224 | tf_op jit(solution)/shard_map/ppermute | solution.py:506
  (24 other events, 130.1 us)

commit v7 on v6

--- a/solution.py
+++ b/solution.py
@@ -483,10 +483,9 @@
         from_left, before = landed(s, from_left, before)
         blocks = [(s, [from_left]), (-s, [from_right])]
         before, on_way[s] = work(blocks)
-    low = lax.ppermute(from_left[:quarter], "exp", right)
-    high = lax.ppermute(from_right[quarter:], "exp", left)
-    low, before = landed(steps, low, before)
-    last, on_way[steps] = work([(0, [normed]), (steps, [low, high])], shared_part)
+    from_left = lax.ppermute(from_left, "exp", right)
+    from_left, before = landed(steps, from_left, before)
+    last, on_way[steps] = work([(0, [normed]), (steps, [from_left])], shared_part)
     (last,) = landed(steps + 1, last)
     for d, got in zip(*on_way[steps]):
         summand[d] = got

time: 93.2 us -> 98.1 us (1.053)
  waiting for transfers between devices: 15.9 us -> 22.6 us
  starting transfers between devices: 41.3 us -> 39.9 us
    ppermute x3, waiting for transfers between devices: 1.37 us -> 8.71 us  [on_device_ring(): lax.ppermute(part(block).astype(bf16), 'exp', along(sign * d))]
    ppermute x2, waiting for transfers between devices: 2.23 us -> 0.01 us  [on_device_ring(): to_left = lax.ppermute(b.astype(bf16), 'exp', left)]
    ppermute x2 -> x0, starting transfers between devices: 2.13 us -> none  [the longest x1 1.72 us: on_device_ring(): low = lax.ppermute(from_left[:quarter], 'exp', right)]
    ppermute x7 -> x8, waiting for transfers between devices: 5.13 us -> 6.83 us  [on_device_ring(): from_left = lax.ppermute(from_left, 'exp', right)]
    ppermute x7 -> x8, starting transfers between devices: 13.5 us -> 15.2 us  [on_device_ring(): from_left = lax.ppermute(from_left, 'exp', right)]
  transfers between devices with their start and end apart: 37 -> 36, of which waited for: 16 -> 14; matrix products, arithmetic and copies ran while one was open for 1% -> 1% of each run, Pallas kernels for 32% -> 30%
where the time goes in v7:
time: 98.1 us; the launch traced here: 97.9 us
  starting transfers between devices  39.9 us (41%)
  Pallas kernels  29.4 us (30%)
  waiting for transfers between devices  22.6 us (23%)
  local copies, waits for them, and re-layouts  5.22 us (5%)
    ppermute x8, starting transfers between devices, on_device_ring(): from_left = lax.ppermute(from_left, 'exp', right)  15.2 us
    pallas_call x4, Pallas kernels, expert(): pl.pallas_call(functools.partial(expert_kernel, n_experts, counts, shared...  11.9 us
    pallas_call x5, Pallas kernels, attend(): pl.pallas_call(functools.partial(attend_kernel, heads, tokens, page_len,...  9.41 us
    ppermute x3, waiting for transfers between devices, on_device_ring(): lax.ppermute(part(block).astype(bf16), 'exp', along(sign * d))  8.71 us
    ppermute x3, starting transfers between devices, on_device_ring(): lax.ppermute(part(block).astype(bf16), 'exp', along(sign * d))  7.98 us
    ppermute x8, waiting for transfers between devices, on_device_ring(): from_left = lax.ppermute(from_left, 'exp', right)  6.83 us
    pallas_call x1, Pallas kernels, shared_expert(): pl.pallas_call(functools.partial(shared_kernel, len(rows)), out_shape=jax...  4.98 us
    ppermute x3, starting transfers between devices, work(): got = lax.ppermute(send, 'req', across)  4.78 us
  transfers between devices with their start and end apart: 36, of which 14 were waited for; matrix products, arithmetic and copies ran while one was open for 1% of the time, Pallas kernels for 30%

profile of v7, /device:TPU:0, one launch (start us, length us, event | category | flops | bytes accessed | tf_op | source)
XLA Modules:
  0.0 97.9 jit_solution(6256375518469865870)
XLA Ops:
  0.0 3.0 %collective-permute-start = (bf16[256,256]{1,0:T(8,128)(2,1)}, bf16[256,256]{1,0:T(8,128)(2,1)S(1)}, u32[]{:S(2)}, u32[]{:S(2)}) collective-permute-start(bf16[256,256]{1,0:T(8,128)(2,1)} %bitcast.20), channel_id=1, source_target_pairs={{0,2},{2,4},{4,6},{6,7},{7,5},{5,3},{3,1},{1,0},{8,10},{10,12},{12... | collective-permute-start | bytes 393224 | tf_op jit(solution)/shard_map/ppermute | solution.py:424
  6.7 1.8 %collective-permute-start.1 = (bf16[256,256]{1,0:T(8,128)(2,1)S(1)}, bf16[256,256]{1,0:T(8,128)(2,1)S(1)}, u32[]{:S(2)}, u32[]{:S(2)}) collective-permute-start(bf16[256,256]{1,0:T(8,128)(2,1)S(1)} %collective-permute-done.refs_4_), channel_id=1, source_target_pairs={{0,2},{2,4},{4,6},{6,7},{7,5},{5,3},{3,1},{1,0},{8,10},{10,12},{12... | collective-permute-start | bytes 393224 | tf_op jit(solution)/shard_map/ppermute | solution.py:424
  8.7 1.9 %shard_map.146 = (f32[512,128]{1,0:T(8,128)S(1)}, f32[512,128]{1,0:T(8,128)S(1)}, f32[512,128]{1,0:T(8,128)S(1)}) custom-call(bf16[512,128]{1,0:T(8,128)(2,1)S(1)} %get-tuple-element.66.refs_0_, f32[512,128]{1,0:T(8,128)S(1)} %get-tuple-element.71.refs_1_, f32[512,128]{1,0:T(8,128)S(1)} %get-tuple-element.72.refs_2_, ...), custom_call_target="tpu_custom_call" | custom-call | flops 6710886400 | bytes 393216 | tf_op jit(solution)/shard_map/pallas_call | solution.py:152
  11.6 1.8 %collective-permute-start.3 = (bf16[256,256]{1,0:T(8,128)(2,1)S(1)}, bf16[256,256]{1,0:T(8,128)(2,1)S(1)}, u32[]{:S(2)}, u32[]{:S(2)}) collective-permute-start(bf16[256,256]{1,0:T(8,128)(2,1)S(1)} %collective-permute-done.1.refs_4_), channel_id=1, source_target_pairs={{0,2},{2,4},{4,6},{6,7},{7,5},{5,3},{3,1},{1,0},{8,10},{10,12},{12... | collective-permute-start | bytes 393224 | tf_op jit(solution)/shard_map/ppermute | solution.py:424
  13.7 1.9 %shard_map.147 = (f32[512,128]{1,0:T(8,128)S(1)}, f32[512,128]{1,0:T(8,128)S(1)}, f32[512,128]{1,0:T(8,128)S(1)}) custom-call(bf16[512,128]{1,0:T(8,128)(2,1)S(1)} %get-tuple-element.66.refs_0_, f32[512,128]{1,0:T(8,128)S(1)} %get-tuple-element.78.refs_1_, f32[512,128]{1,0:T(8,128)S(1)} %get-tuple-element.79.refs_2_, ...), custom_call_target="tpu_custom_call" | custom-call | flops 6710886400 | bytes 393216 | tf_op jit(solution)/shard_map/pallas_call | solution.py:152
  16.9 1.8 %collective-permute-start.5 = (bf16[256,256]{1,0:T(8,128)(2,1)S(1)}, bf16[256,256]{1,0:T(8,128)(2,1)S(1)}, u32[]{:S(2)}, u32[]{:S(2)}) collective-permute-start(bf16[256,256]{1,0:T(8,128)(2,1)S(1)} %collective-permute-done.3.refs_5_), channel_id=1, source_target_pairs={{0,2},{2,4},{4,6},{6,7},{7,5},{5,3},{3,1},{1,0},{8,10},{10,12},{12... | collective-permute-start | bytes 393224 | tf_op jit(solution)/shard_map/ppermute | solution.py:431
  18.7 3.0 %shard_map.148 = (f32[512,128]{1,0:T(8,128)S(1)}, f32[512,128]{1,0:T(8,128)S(1)}, f32[512,128]{1,0:T(8,128)S(1)}, bf16[512,2048]{1,0:T(8,128)(2,1)S(1)}) custom-call(bf16[512,128]{1,0:T(8,128)(2,1)S(1)} %get-tuple-element.66.refs_0_, f32[512,128]{1,0:T(8,128)S(1)} %get-tuple-element.85.refs_1_, f32[512,128]{1,0:T(8,128)S(1)} %get-tuple-element.86.refs_2_, ...), custom_call_target="tpu_custom_call" | custom-call | flops 134217728 | bytes 393216 | tf_op jit(solution)/shard_map/pallas_call | solution.py:152
  25.2 1.8 %collective-permute-start.8 = (bf16[64,2048]{1,0:T(8,128)(2,1)S(1)}, bf16[64,2048]{1,0:T(8,128)(2,1)S(1)}, u32[]{:S(2)}, u32[]{:S(2)}) collective-permute-start(bf16[64,2048]{1,0:T(8,128)(2,1)S(1)} %add_convert_fusion.refs_0_), channel_id=1, source_target_pairs={{0,16},{8,24},{16,0},{24,8},{1,17},{9,25},{17,1},{25,9},{2,18},{10... | collective-permute-start | bytes 786440 | tf_op jit(solution)/shard_map/ppermute | solution.py:438
  27.3 2.7 %shard_map.150 = (bf16[704,2048]{1,0:T(8,128)(2,1)S(1)}, bf16[704,2048]{1,0:T(8,128)(2,1)S(1)}) custom-call(bf16[352,2048]{1,0:T(8,128)(2,1)} %bitcast.17, bf16[352,2048]{1,0:T(8,128)(2,1)} %collective-permute-done.9.refs_1_, bf16[352,2048]{1,0:T(8,128)(2,1)} %bitcast.19, bf16[352,2048]{1,0:T(8,128)(2,1)} %collective-permute-done.10.refs_3_), custom_call_target="tpu_custom_call" | custom-call | bytes 5767168 | tf_op jit(solution)/shard_map/pallas_call | solution.py:229
  34.0 1.8 %collective-permute-start.11 = (bf16[64,2176]{1,0:T(8,128)(2,1)S(1)}, bf16[64,2176]{1,0:T(8,128)(2,1)S(1)}, u32[]{:S(2)}, u32[]{:S(2)}) collective-permute-start(bf16[64,2176]{1,0:T(8,128)(2,1)S(1)} %get-tuple-element.102.refs_0_.refs_1_), channel_id=1, source_target_pairs={{0,2},{2,4},{4,6},{6,7},{7,5},{5,3},{3,1},{1,0},{8,10},{10,12},{12... | collective-permute-start | bytes 835592 | tf_op jit(solution)/shard_map/ppermute | solution.py:481
  36.1 5.0 %shard_map.152.refs_3_ = f32[64,2048]{1,0:T(8,128)S(1)} custom-call(bf16[64,2176]{1,0:T(8,128)(2,1)S(1)} %get-tuple-element.102.refs_0_.refs_1_, bf16[352,2048]{1,0:T(8,128)(2,1)} %bitcast.14, bf16[352,2048]{1,0:T(8,128)(2,1)} %collective-permute-done.12.refs_2_, bf16[352,2048]{1,0:T(8,128)(2,1)} %bitcast.12.refs_3_, ...), custom_call_target="tpu_custom_call" | custom-call | flops 553648128 | bytes 8650752 | tf_op jit(solution)/shard_map/pallas_call | solution.py:276
  42.0 1.7 %collective-permute-start.15 = (bf16[64,2176]{1,0:T(8,128)(2,1)S(1)}, bf16[64,2176]{1,0:T(8,128)(2,1)S(1)}, u32[]{:S(2)}, u32[]{:S(2)}) collective-permute-start(bf16[64,2176]{1,0:T(8,128)(2,1)S(1)} %collective-permute-done.11.refs_1_), channel_id=1, source_target_pairs={{0,2},{2,4},{4,6},{6,7},{7,5},{5,3},{3,1},{1,0},{8,10},{10,12},{12... | collective-permute-start | bytes 835592 | tf_op jit(solution)/shard_map/ppermute | solution.py:481
  44.1 3.1 %shard_map.153 = (bf16[32,2048]{1,0:T(8,128)(2,1)S(1)}, bf16[32,2048]{1,0:T(8,128)(2,1)S(1)}, bf16[64,2048]{1,0:T(8,128)(2,1)S(1)}, bf16[704,2048]{1,0:T(8,128)(2,1)S(1)}) custom-call(s32[2]{0:T(128)S(1)} %pad_add_fusion.refs_0_, bf16[64,2176]{1,0:T(8,128)(2,1)S(1)} %collective-permute-done.11.refs_1_, bf16[64,2176]{1,0:T(8,128)(2,1)S(1)} %collective-permute-done.16.refs_2_, ...), custom_call_target="tpu_custom_call" | custom-call | flops 55364812800 | bytes 1048576 | tf_op jit(solution)/shard_map/pallas_call | solution.py:354
  47.1 1.7 %collective-permute-start.22 = (bf16[64,2048]{1,0:T(8,128)(2,1)S(1)}, bf16[64,2048]{1,0:T(8,128)(2,1)S(1)}, u32[]{:S(2)}, u32[]{:S(2)}) collective-permute-start(bf16[64,2048]{1,0:T(8,128)(2,1)S(1)} %get-tuple-element.115), channel_id=1, source_target_pairs={{0,16},{8,24},{16,0},{24,8},{1,17},{9,25},{17,1},{25,9},{2,18},{10... | collective-permute-start | bytes 786440 | tf_op jit(solution)/shard_map/ppermute | solution.py:459
  51.1 2.9 %shard_map.154 = (bf16[32,2048]{1,0:T(8,128)(2,1)S(1)}, bf16[32,2048]{1,0:T(8,128)(2,1)S(1)}, bf16[64,2048]{1,0:T(8,128)(2,1)S(1)}) custom-call(s32[2]{0:T(128)S(1)} %pad_add_fusion.refs_0_, bf16[64,2176]{1,0:T(8,128)(2,1)S(1)} %collective-permute-done.15.refs_1_, bf16[64,2176]{1,0:T(8,128)(2,1)S(1)} %collective-permute-done.19.refs_2_, ...), custom_call_target="tpu_custom_call" | custom-call | flops 55364812800 | bytes 1048576 | tf_op jit(solution)/shard_map/pallas_call | solution.py:354
  57.9 2.9 %shard_map.155 = (bf16[32,2048]{1,0:T(8,128)(2,1)S(1)}, bf16[32,2048]{1,0:T(8,128)(2,1)S(1)}, bf16[64,2048]{1,0:T(8,128)(2,1)S(1)}) custom-call(s32[2]{0:T(128)S(1)} %pad_add_fusion.refs_0_, bf16[64,2176]{1,0:T(8,128)(2,1)S(1)} %collective-permute-done.18.refs_1_, bf16[64,2176]{1,0:T(8,128)(2,1)S(1)} %collective-permute-done.21.refs_2_, ...), custom_call_target="tpu_custom_call" | custom-call | flops 55364812800 | bytes 1048576 | tf_op jit(solution)/shard_map/pallas_call | solution.py:354
  64.1 1.8 %collective-permute-start.25 = (bf16[32,2048]{1,0:T(8,128)(2,1)S(1)}, bf16[32,2048]{1,0:T(8,128)(2,1)S(1)}, u32[]{:S(2)}, u32[]{:S(2)}) collective-permute-start(bf16[32,2048]{1,0:T(8,128)(2,1)S(1)} %get-tuple-element.135), channel_id=1, source_target_pairs={{0,2},{2,4},{4,6},{6,7},{7,5},{5,3},{3,1},{1,0},{8,10},{10,12},{12... | collective-permute-start | bytes 393224 | tf_op jit(solution)/shard_map/ppermute | solution.py:511
  66.2 2.9 %shard_map.156 = (bf16[32,2048]{1,0:T(8,128)(2,1)S(1)}, bf16[32,2048]{1,0:T(8,128)(2,1)S(1)}, bf16[64,2048]{1,0:T(8,128)(2,1)S(1)}) custom-call(s32[2]{0:T(128)S(1)} %pad_add_fusion.refs_0_, bf16[64,2176]{1,0:T(8,128)(2,1)S(1)} %get-tuple-element.102.refs_0_.refs_1_, bf16[64,2176]{1,0:T(8,128)(2,1)S(1)} %collective-permute-done.20.refs_2_, ...), custom_call_target="tpu_custom_call" | custom-call | flops 55364812800 | bytes 1048576 | tf_op jit(solution)/shard_map/pallas_call | solution.py:354
  69.2 1.8 %collective-permute-start.29 = (bf16[32,2048]{1,0:T(8,128)(2,1)S(1)}, bf16[32,2048]{1,0:T(8,128)(2,1)S(1)}, u32[]{:S(2)}, u32[]{:S(2)}) collective-permute-start(bf16[32,2048]{1,0:T(8,128)(2,1)S(1)} %get-tuple-element.132), channel_id=1, source_target_pairs={{0,16},{8,24},{16,0},{24,8},{1,17},{9,25},{17,1},{25,9},{2,18},{10... | collective-permute-start | bytes 393224 | tf_op jit(solution)/shard_map/ppermute | solution.py:462
  71.0 3.6 %collective-permute-start.32 = (bf16[32,2048]{1,0:T(8,128)(2,1)S(1)}, bf16[32,2048]{1,0:T(8,128)(2,1)S(1)}, u32[]{:S(2)}, u32[]{:S(2)}) collective-permute-start(bf16[32,2048]{1,0:T(8,128)(2,1)S(1)} %get-tuple-element.137), channel_id=1, source_target_pairs={{0,6},{2,7},{4,5},{6,3},{7,1},{5,0},{3,2},{1,4},{8,14},{10,15},{12... | collective-permute-start | bytes 393224 | tf_op jit(solution)/shard_map/ppermute | solution.py:505
  77.5 5.2 %collective-permute-done.32 = bf16[32,2048]{1,0:T(8,128)(2,1)S(1)} collective-permute-done((bf16[32,2048]{1,0:T(8,128)(2,1)S(1)}, bf16[32,2048]{1,0:T(8,128)(2,1)S(1)}, u32[]{:S(2)}, u32[]{:S(2)}) %collective-permute-start.32) | collective-permute-done | bytes 131104 | tf_op jit(solution)/shard_map/ppermute | solution.py:505
  82.6 4.1 %collective-permute-start.30 = (bf16[32,2048]{1,0:T(8,128)(2,1)S(1)}, bf16[32,2048]{1,0:T(8,128)(2,1)S(1)}, u32[]{:S(2)}, u32[]{:S(2)}) collective-permute-start(bf16[32,2048]{1,0:T(8,128)(2,1)S(1)} %add_convert_fusion.4), channel_id=1, source_target_pairs={{0,7},{2,5},{4,3},{6,1},{7,0},{5,2},{3,4},{1,6},{8,15},{10,13},{12... | collective-permute-start | bytes 393224 | tf_op jit(solution)/shard_map/ppermute | solution.py:505
  86.7 3.5 %collective-permute-done.30 = bf16[32,2048]{1,0:T(8,128)(2,1)S(1)} collective-permute-done((bf16[32,2048]{1,0:T(8,128)(2,1)S(1)}, bf16[32,2048]{1,0:T(8,128)(2,1)S(1)}, u32[]{:S(2)}, u32[]{:S(2)}) %collective-permute-start.30) | collective-permute-done | bytes 131104 | tf_op jit(solution)/shard_map/ppermute | solution.py:505
  91.1 4.3 %collective-permute-done.34 = bf16[32,2048]{1,0:T(8,128)(2,1)S(1)} collective-permute-done((bf16[32,2048]{1,0:T(8,128)(2,1)S(1)}, bf16[32,2048]{1,0:T(8,128)(2,1)S(1)}, u32[]{:S(2)}, u32[]{:S(2)}) %collective-permute-start.34) | collective-permute-done | bytes 131104 | tf_op jit(solution)/shard_map/ppermute | solution.py:523
  (100 shorter events, 31.6 us)
Async XLA Ops:
  3.0 21.6 %collective-permute-start.10 = (bf16[352,2048]{1,0:T(8,128)(2,1)}, bf16[352,2048]{1,0:T(8,128)(2,1)}, u32[]{:S(2)}, u32[]{:S(2)}) collective-permute-start(bf16[352,2048]{1,0:T(8,128)(2,1)} %bitcast.18), channel_id=1, source_target_pairs={{0,8},{8,0},{16,24},{24,16},{1,9},{9,1},{17,25},{25,17},{2,10},{10... | collective-permute-start | bytes 4325384 | tf_op jit(solution)/shard_map/ppermute | solution.py:414
  3.0 22.1 %collective-permute-start.9 = (bf16[352,2048]{1,0:T(8,128)(2,1)}, bf16[352,2048]{1,0:T(8,128)(2,1)}, u32[]{:S(2)}, u32[]{:S(2)}) collective-permute-start(bf16[352,2048]{1,0:T(8,128)(2,1)} %bitcast.16), channel_id=1, source_target_pairs={{0,8},{8,0},{16,24},{24,16},{1,9},{9,1},{17,25},{25,17},{2,10},{10... | collective-permute-start | bytes 4325384 | tf_op jit(solution)/shard_map/ppermute | solution.py:414
  23.2 12.6 %collective-permute-start.12 = (bf16[352,2048]{1,0:T(8,128)(2,1)S(1)}, bf16[352,2048]{1,0:T(8,128)(2,1)}, u32[]{:S(2)}, u32[]{:S(2)}) collective-permute-start(bf16[352,2048]{1,0:T(8,128)(2,1)S(1)} %bitcast.15), channel_id=1, source_target_pairs={{0,8},{8,0},{16,24},{24,16},{1,9},{9,1},{17,25},{25,17},{2,10},{10... | collective-permute-start | bytes 4325384 | tf_op jit(solution)/shard_map/ppermute | solution.py:414
  23.5 12.7 %collective-permute-start.13 = (bf16[352,2048]{1,0:T(8,128)(2,1)}, bf16[352,2048]{1,0:T(8,128)(2,1)}, u32[]{:S(2)}, u32[]{:S(2)}) collective-permute-start(bf16[352,2048]{1,0:T(8,128)(2,1)} %bitcast.12.refs_3_), channel_id=1, source_target_pairs={{0,8},{8,0},{16,24},{24,16},{1,9},{9,1},{17,25},{25,17},{2,10},{10... | collective-permute-start | bytes 4325384 | tf_op jit(solution)/shard_map/ppermute | solution.py:414
  24.5 11.6 %collective-permute-start.14 = (bf16[352,2048]{1,0:T(8,128)(2,1)}, bf16[352,2048]{1,0:T(8,128)(2,1)}, u32[]{:S(2)}, u32[]{:S(2)}) collective-permute-start(bf16[352,2048]{1,0:T(8,128)(2,1)} %refs_5_.1), channel_id=1, source_target_pairs={{0,8},{8,0},{16,24},{24,16},{1,9},{9,1},{17,25},{25,17},{2,10},{10... | collective-permute-start | bytes 4325384 | tf_op jit(solution)/shard_map/ppermute | solution.py:414
  24.6 19.4 %collective-permute-start.17 = (bf16[352,2048]{1,0:T(8,128)(2,1)}, bf16[352,2048]{1,0:T(8,128)(2,1)}, u32[]{:S(2)}, u32[]{:S(2)}) collective-permute-start(bf16[352,2048]{1,0:T(8,128)(2,1)} %bitcast.13.refs_5_), channel_id=1, source_target_pairs={{0,8},{8,0},{16,24},{24,16},{1,9},{9,1},{17,25},{25,17},{2,10},{10... | collective-permute-start | bytes 4325384 | tf_op jit(solution)/shard_map/ppermute | solution.py:414
  25.2 8.4 %collective-permute-start.8 = (bf16[64,2048]{1,0:T(8,128)(2,1)S(1)}, bf16[64,2048]{1,0:T(8,128)(2,1)S(1)}, u32[]{:S(2)}, u32[]{:S(2)}) collective-permute-start(bf16[64,2048]{1,0:T(8,128)(2,1)S(1)} %add_convert_fusion.refs_0_), channel_id=1, source_target_pairs={{0,16},{8,24},{16,0},{24,8},{1,17},{9,25},{17,1},{25,9},{2,18},{10... | collective-permute-start | bytes 786440 | tf_op jit(solution)/shard_map/ppermute | solution.py:438
  34.0 8.0 %collective-permute-start.11 = (bf16[64,2176]{1,0:T(8,128)(2,1)S(1)}, bf16[64,2176]{1,0:T(8,128)(2,1)S(1)}, u32[]{:S(2)}, u32[]{:S(2)}) collective-permute-start(bf16[64,2176]{1,0:T(8,128)(2,1)S(1)} %get-tuple-element.102.refs_0_.refs_1_), channel_id=1, source_target_pairs={{0,2},{2,4},{4,6},{6,7},{7,5},{5,3},{3,1},{1,0},{8,10},{10,12},{12... | collective-permute-start | bytes 835592 | tf_op jit(solution)/shard_map/ppermute | solution.py:481
  35.8 7.9 %collective-permute-start.16 = (bf16[64,2176]{1,0:T(8,128)(2,1)S(1)}, bf16[64,2176]{1,0:T(8,128)(2,1)S(1)}, u32[]{:S(2)}, u32[]{:S(2)}) collective-permute-start(bf16[64,2176]{1,0:T(8,128)(2,1)S(1)} %get-tuple-element.102.refs_0_.refs_1_), channel_id=1, source_target_pairs={{2,0},{4,2},{6,4},{7,6},{5,7},{3,5},{1,3},{0,1},{10,8},{12,10},{14... | collective-permute-start | bytes 835592 | tf_op jit(solution)/shard_map/ppermute | solution.py:482
  47.1 15.3 %collective-permute-start.22 = (bf16[64,2048]{1,0:T(8,128)(2,1)S(1)}, bf16[64,2048]{1,0:T(8,128)(2,1)S(1)}, u32[]{:S(2)}, u32[]{:S(2)}) collective-permute-start(bf16[64,2048]{1,0:T(8,128)(2,1)S(1)} %get-tuple-element.115), channel_id=1, source_target_pairs={{0,16},{8,24},{16,0},{24,8},{1,17},{9,25},{17,1},{25,9},{2,18},{10... | collective-permute-start | bytes 786440 | tf_op jit(solution)/shard_map/ppermute | solution.py:459
  49.1 7.2 %collective-permute-start.18 = (bf16[64,2176]{1,0:T(8,128)(2,1)S(1)}, bf16[64,2176]{1,0:T(8,128)(2,1)S(1)}, u32[]{:S(2)}, u32[]{:S(2)}) collective-permute-start(bf16[64,2176]{1,0:T(8,128)(2,1)S(1)} %collective-permute-done.15.refs_1_), channel_id=1, source_target_pairs={{0,2},{2,4},{4,6},{6,7},{7,5},{5,3},{3,1},{1,0},{8,10},{10,12},{12... | collective-permute-start | bytes 835592 | tf_op jit(solution)/shard_map/ppermute | solution.py:481
  50.6 7.3 %collective-permute-start.21 = (bf16[64,2176]{1,0:T(8,128)(2,1)S(1)}, bf16[64,2176]{1,0:T(8,128)(2,1)S(1)}, u32[]{:S(2)}, u32[]{:S(2)}) collective-permute-start(bf16[64,2176]{1,0:T(8,128)(2,1)S(1)} %collective-permute-done.19.refs_2_), channel_id=1, source_target_pairs={{2,0},{4,2},{6,4},{7,6},{5,7},{3,5},{1,3},{0,1},{10,8},{12,10},{14... | collective-permute-start | bytes 835592 | tf_op jit(solution)/shard_map/ppermute | solution.py:482
  54.1 8.4 %collective-permute-start.23 = (bf16[64,2048]{1,0:T(8,128)(2,1)S(1)}, bf16[64,2048]{1,0:T(8,128)(2,1)S(1)}, u32[]{:S(2)}, u32[]{:S(2)}) collective-permute-start(bf16[64,2048]{1,0:T(8,128)(2,1)S(1)} %get-tuple-element.116), channel_id=1, source_target_pairs={{0,16},{8,24},{16,0},{24,8},{1,17},{9,25},{17,1},{25,9},{2,18},{10... | collective-permute-start | bytes 786440 | tf_op jit(solution)/shard_map/ppermute | solution.py:459
  56.2 7.8 %collective-permute-start.20 = (bf16[64,2176]{1,0:T(8,128)(2,1)S(1)}, bf16[64,2176]{1,0:T(8,128)(2,1)S(1)}, u32[]{:S(2)}, u32[]{:S(2)}) collective-permute-start(bf16[64,2176]{1,0:T(8,128)(2,1)S(1)} %collective-permute-done.18.refs_1_), channel_id=1, source_target_pairs={{0,2},{2,4},{4,6},{6,7},{7,5},{5,3},{3,1},{1,0},{8,10},{10,12},{12... | collective-permute-start | bytes 835592 | tf_op jit(solution)/shard_map/ppermute | solution.py:486
  60.8 10.1 %collective-permute-start.31 = (bf16[64,2048]{1,0:T(8,128)(2,1)S(1)}, bf16[64,2048]{1,0:T(8,128)(2,1)S(1)}, u32[]{:S(2)}, u32[]{:S(2)}) collective-permute-start(bf16[64,2048]{1,0:T(8,128)(2,1)S(1)} %get-tuple-element.123), channel_id=1, source_target_pairs={{0,16},{8,24},{16,0},{24,8},{1,17},{9,25},{17,1},{25,9},{2,18},{10... | collective-permute-start | bytes 786440 | tf_op jit(solution)/shard_map/ppermute | solution.py:459
  64.1 10.8 %collective-permute-start.25 = (bf16[32,2048]{1,0:T(8,128)(2,1)S(1)}, bf16[32,2048]{1,0:T(8,128)(2,1)S(1)}, u32[]{:S(2)}, u32[]{:S(2)}) collective-permute-start(bf16[32,2048]{1,0:T(8,128)(2,1)S(1)} %get-tuple-element.135), channel_id=1, source_target_pairs={{0,2},{2,4},{4,6},{6,7},{7,5},{5,3},{3,1},{1,0},{8,10},{10,12},{12... | collective-permute-start | bytes 393224 | tf_op jit(solution)/shard_map/ppermute | solution.py:511
  65.9 9.3 %collective-permute-start.27 = (bf16[32,2048]{1,0:T(8,128)(2,1)S(1)}, bf16[32,2048]{1,0:T(8,128)(2,1)S(1)}, u32[]{:S(2)}, u32[]{:S(2)}) collective-permute-start(bf16[32,2048]{1,0:T(8,128)(2,1)S(1)} %get-tuple-element.136), channel_id=1, source_target_pairs={{2,0},{4,2},{6,4},{7,6},{5,7},{3,5},{1,3},{0,1},{10,8},{12,10},{14... | collective-permute-start | bytes 393224 | tf_op jit(solution)/shard_map/ppermute | solution.py:512
  69.2 7.7 %collective-permute-start.29 = (bf16[32,2048]{1,0:T(8,128)(2,1)S(1)}, bf16[32,2048]{1,0:T(8,128)(2,1)S(1)}, u32[]{:S(2)}, u32[]{:S(2)}) collective-permute-start(bf16[32,2048]{1,0:T(8,128)(2,1)S(1)} %get-tuple-element.132), channel_id=1, source_target_pairs={{0,16},{8,24},{16,0},{24,8},{1,17},{9,25},{17,1},{25,9},{2,18},{10... | collective-permute-start | bytes 393224 | tf_op jit(solution)/shard_map/ppermute | solution.py:462
  71.0 11.6 %collective-permute-start.32 = (bf16[32,2048]{1,0:T(8,128)(2,1)S(1)}, bf16[32,2048]{1,0:T(8,128)(2,1)S(1)}, u32[]{:S(2)}, u32[]{:S(2)}) collective-permute-start(bf16[32,2048]{1,0:T(8,128)(2,1)S(1)} %get-tuple-element.137), channel_id=1, source_target_pairs={{0,6},{2,7},{4,5},{6,3},{7,1},{5,0},{3,2},{1,4},{8,14},{10,15},{12... | collective-permute-start | bytes 393224 | tf_op jit(solution)/shard_map/ppermute | solution.py:505
  74.7 12.0 %collective-permute-start.33 = (bf16[32,2048]{1,0:T(8,128)(2,1)S(1)}, bf16[32,2048]{1,0:T(8,128)(2,1)S(1)}, u32[]{:S(2)}, u32[]{:S(2)}) collective-permute-start(bf16[32,2048]{1,0:T(8,128)(2,1)S(1)} %get-tuple-element.138), channel_id=1, source_target_pairs={{0,5},{2,3},{4,1},{6,0},{7,2},{5,4},{3,6},{1,7},{8,13},{10,11},{12... | collective-permute-start | bytes 393224 | tf_op jit(solution)/shard_map/ppermute | solution.py:505
  74.9 11.8 %collective-permute-start.24 = (bf16[32,2048]{1,0:T(8,128)(2,1)S(1)}, bf16[32,2048]{1,0:T(8,128)(2,1)S(1)}, u32[]{:S(2)}, u32[]{:S(2)}) collective-permute-start(bf16[32,2048]{1,0:T(8,128)(2,1)S(1)} %get-tuple-element.131), channel_id=1, source_target_pairs={{0,16},{8,24},{16,0},{24,8},{1,17},{9,25},{17,1},{25,9},{2,18},{10... | collective-permute-start | bytes 393224 | tf_op jit(solution)/shard_map/ppermute | solution.py:462
  75.3 11.4 %collective-permute-start.26 = (bf16[32,2048]{1,0:T(8,128)(2,1)S(1)}, bf16[32,2048]{1,0:T(8,128)(2,1)S(1)}, u32[]{:S(2)}, u32[]{:S(2)}) collective-permute-start(bf16[32,2048]{1,0:T(8,128)(2,1)S(1)} %get-tuple-element.133), channel_id=1, source_target_pairs={{0,2},{2,4},{4,6},{6,7},{7,5},{5,3},{3,1},{1,0},{8,10},{10,12},{12... | collective-permute-start | bytes 393224 | tf_op jit(solution)/shard_map/ppermute | solution.py:511
  76.9 9.8 %collective-permute-start.28 = (bf16[32,2048]{1,0:T(8,128)(2,1)S(1)}, bf16[32,2048]{1,0:T(8,128)(2,1)S(1)}, u32[]{:S(2)}, u32[]{:S(2)}) collective-permute-start(bf16[32,2048]{1,0:T(8,128)(2,1)S(1)} %get-tuple-element.134), channel_id=1, source_target_pairs={{2,0},{4,2},{6,4},{7,6},{5,7},{3,5},{1,3},{0,1},{10,8},{12,10},{14... | collective-permute-start | bytes 393224 | tf_op jit(solution)/shard_map/ppermute | solution.py:512
  82.6 7.7 %collective-permute-start.30 = (bf16[32,2048]{1,0:T(8,128)(2,1)S(1)}, bf16[32,2048]{1,0:T(8,128)(2,1)S(1)}, u32[]{:S(2)}, u32[]{:S(2)}) collective-permute-start(bf16[32,2048]{1,0:T(8,128)(2,1)S(1)} %add_convert_fusion.4), channel_id=1, source_target_pairs={{0,7},{2,5},{4,3},{6,1},{7,0},{5,2},{3,4},{1,6},{8,15},{10,13},{12... | collective-permute-start | bytes 393224 | tf_op jit(solution)/shard_map/ppermute | solution.py:505
  (23 other events, 123.3 us)
